TPU v7x, 32 devices: a whole 2x2x4 slice. The times are simulated.
32 devices in a mesh: seq: 8 (over z, y), batch: 4 (over x, core).
Axes of the slice: x: 2, y: 2, z: 4, core: 2. Of those that a mesh axis runs over, the one named last changes fastest.
Arguments:
- inputs: bfloat16 [16, 1024, 768], P('batch', 'seq'), may hold values from -6 to 6
- gain_one: bfloat16 [768], replicated, may hold values from 0.5 to 1.5
- bias_one: bfloat16 [768], replicated, may hold values from -1.25 to 1.25
- project_weight: bfloat16 [768, 2304], replicated, may hold values from -0.21875 to 0.21875
- project_bias: bfloat16 [2304], replicated, may hold values from -0.3125 to 0.3125
- query_map: bfloat16 [12, 64, 64], replicated, may hold values from -0.75 to 0.75
- key_map: bfloat16 [12, 64, 64], replicated, may hold values from -0.75 to 0.75
- output_weight: bfloat16 [768, 768], replicated, may hold values from -0.875 to 0.875
- output_bias: bfloat16 [768], replicated, may hold values from -1.25 to 1.25
- gain_two: bfloat16 [768], replicated, may hold values from 0.5 to 1.5
- bias_two: bfloat16 [768], replicated, may hold values from -1.25 to 1.25
- expand_weight: bfloat16 [768, 3072], replicated, may hold values from -0.21875 to 0.21875
- expand_bias: bfloat16 [3072], replicated, may hold values from -1.25 to 1.25
- contract_weight: bfloat16 [3072, 768], replicated, may hold values from -0.109375 to 0.109375
- contract_bias: bfloat16 [768], replicated, may hold values from -1.25 to 1.25
- bounds: int32 [16, 2], P('batch'), may hold values from 1 to 1023, as said below
- cotangent: bfloat16 [16, 1024, 768], P('batch', 'seq'), may hold values from -6 to 6
Outputs:
- block_output: bfloat16 [16, 1024, 768], P('batch', 'seq')
- input_grad: bfloat16 [16, 1024, 768], P('batch', 'seq')
- gain_one_grad: float32 [768], replicated
- bias_one_grad: float32 [768], replicated
- project_weight_grad: float32 [768, 2304], P('seq')
- project_bias_grad: float32 [2304], replicated
- query_map_grad: float32 [12, 64, 64], replicated
- key_map_grad: float32 [12, 64, 64], replicated
- output_weight_grad: float32 [768, 768], P('seq')
- output_bias_grad: float32 [768], replicated
- gain_two_grad: float32 [768], replicated
- bias_two_grad: float32 [768], replicated
- expand_weight_grad: float32 [768, 3072], P('seq')
- expand_bias_grad: float32 [3072], replicated
- contract_weight_grad: float32 [3072, 768], P('seq')
- contract_bias_grad: float32 [768], replicated
Inputs may be any that keep to these rules, and one draw needn't show every extreme that they name: bounds[i, 0] < bounds[i, 1]; among the 4 sequences of each index of batch, at least at least one, which one drawn from the seed, has bounds[i, 0] < 128 and bounds[i, 1] >= 896.
All inputs are finite; a program needn't handle non-finite values.
Results may differ from a plain program's by a relative error of at most 0.011.
Values sent between devices are 32-bit elements; how exact they have to be, the bound alone decides.
A program may use at most 320 MiB of HBM per device.

v0:
```python
from functools import partial

import jax
import jax.numpy as jnp
from jax import lax
from jax.sharding import PartitionSpec as P

epsilon = 1e-05
precise = lax.Precision.HIGHEST
bfloat = jnp.bfloat16
single = jnp.float32


def entering(part, axis, combine, identity, reverse):
    count = lax.axis_size(axis)
    place = lax.axis_index(axis)
    ahead = count - 1 - place if reverse else place
    gathered = jax.tree.map(lambda a: lax.all_gather(a, axis), part)
    state = jax.tree.map(lambda a, e: jnp.zeros_like(a) + jnp.asarray(e, a.dtype), part, identity)

    def one(lap, state):
        source = count - 1 - lap if reverse else lap
        return combine(
            state, jax.tree.map(lambda a: lax.dynamic_index_in_dim(a, source, 0, False), gathered)
        )

    return lax.fori_loop(0, ahead, one, state)


def norm_forward(values, gain_vector, shift_vector):
    centered = values - jnp.mean(values, axis=-1, keepdims=True)
    inverse = lax.rsqrt(jnp.mean(centered * centered, axis=-1, keepdims=True) + epsilon)
    unit_rows = centered * inverse
    return (unit_rows * gain_vector + shift_vector, unit_rows, inverse)


def norm_backward(gradient, unit_rows, inverse, gain_vector):
    inner = gradient * gain_vector
    result = inverse * (
        inner
        - jnp.mean(inner, axis=-1, keepdims=True)
        - unit_rows * jnp.mean(inner * unit_rows, axis=-1, keepdims=True)
    )
    return (result, jnp.sum(gradient * unit_rows, axis=0), jnp.sum(gradient, axis=0))


def feature_forward(vectors, weights):
    mapped = jnp.einsum("rhd,hde->rhe", vectors, weights, preferred_element_type=single)
    return (jax.nn.softmax(mapped, axis=-1), jax.nn.softmax(-mapped, axis=-1))


def feature_backward(feat_grad, positive, negative, vectors, weights):
    head_width = weights.shape[-1]
    grad_pos = feat_grad[..., :head_width]
    grad_neg = feat_grad[..., head_width:]
    mapped_grad = positive * (
        grad_pos - jnp.sum(positive * grad_pos, axis=-1, keepdims=True)
    ) - negative * (grad_neg - jnp.sum(negative * grad_neg, axis=-1, keepdims=True))
    mapped_low = mapped_grad.astype(bfloat)
    weight_grad = jnp.einsum("rhd,rhe->hde", vectors, mapped_low, preferred_element_type=single)
    vector_grad = jnp.einsum("rhe,hde->rhd", mapped_low, weights, preferred_element_type=single)
    return (vector_grad, weight_grad)


def doc_number(positions, first_bound, second_bound):
    return (positions >= first_bound).astype(jnp.int32) + (positions >= second_bound).astype(
        jnp.int32
    )


def carry_combine(earlier_part, later_part):
    factor = later_part[2]
    return (
        later_part[0] + factor[:, None, None, None] * earlier_part[0],
        later_part[1] + factor[:, None, None] * earlier_part[1],
        earlier_part[2] * later_part[2],
    )


def per_device(
    inputs,
    gain_one,
    bias_one,
    project_weight,
    project_bias,
    query_map,
    key_map,
    output_weight,
    output_bias,
    gain_two,
    bias_two,
    expand_weight,
    expand_bias,
    contract_weight,
    contract_bias,
    bounds,
    cotangent,
):
    micro_count, row_count, model_width = inputs.shape
    head_count, head_width = (query_map.shape[0], query_map.shape[1])
    feat_width = 2 * head_width
    total_rows = micro_count * row_count
    first_row = lax.axis_index("seq") * row_count
    positions = first_row + jnp.arange(row_count, dtype=jnp.int32)
    first_bound = bounds[:, 0:1]
    second_bound = bounds[:, 1:2]
    doc_ids = doc_number(positions[None, :], first_bound, second_bound)
    doc_prev = doc_number(first_row - 1, first_bound, second_bound)
    doc_last = doc_number(first_row + row_count - 1, first_bound, second_bound)
    use_in = (doc_ids == doc_prev).astype(single)
    in_last = (doc_ids == doc_last).astype(single)
    keep_state = (doc_prev == doc_last).astype(single)[:, 0]
    causal = positions[:, None] >= positions[None, :]
    attend_mask = (causal[None] & (doc_ids[:, :, None] == doc_ids[:, None, :])).astype(single)
    flat_input = inputs.reshape(total_rows, model_width).astype(single)
    normed, unit_one, inverse_one = norm_forward(
        flat_input, gain_one.astype(single), bias_one.astype(single)
    )
    normed_low = normed.astype(bfloat)
    projected = (
        jnp.dot(normed_low, project_weight, preferred_element_type=single)
        + project_bias.astype(single)
    ).astype(bfloat)
    queries = projected[:, :model_width].reshape(total_rows, head_count, head_width)
    key_rows = projected[:, model_width : 2 * model_width].reshape(
        total_rows, head_count, head_width
    )
    value_rows = projected[:, 2 * model_width :].reshape(
        micro_count, row_count, head_count, head_width
    )
    query_pos, query_neg = feature_forward(queries, query_map)
    key_pos, key_neg = feature_forward(key_rows, key_map)
    feat_query = (
        jnp.concatenate([query_pos, query_neg], axis=-1)
        .astype(bfloat)
        .reshape(micro_count, row_count, head_count, feat_width)
    )
    feat_key = (
        jnp.concatenate([key_pos, key_neg], axis=-1)
        .astype(bfloat)
        .reshape(micro_count, row_count, head_count, feat_width)
    )
    last_keys = feat_key * in_last[:, :, None, None].astype(bfloat)
    local_state = jnp.einsum(
        "mthf,mthe->mhfe", last_keys, value_rows, preferred_element_type=single
    )
    local_sum = jnp.sum(last_keys.astype(single), axis=1)
    zero_state = jnp.zeros_like(local_state)
    zero_sum = jnp.zeros_like(local_sum)
    one_keep = jnp.ones_like(keep_state)
    state_in, sum_in, chain_keep = entering(
        (local_state, local_sum, keep_state),
        "seq",
        carry_combine,
        (zero_state, zero_sum, one_keep),
        False,
    )
    query_wide = feat_query.astype(single)
    key_wide = feat_key.astype(single)
    value_wide = value_rows.astype(single)
    use_wide = use_in[:, :, None, None]
    scores = (
        jnp.einsum("mthf,mshf->mhts", feat_query, feat_key, preferred_element_type=single)
        * attend_mask[:, None]
    )
    numerator = jnp.einsum(
        "mhts,mshe->mthe", scores, value_wide, precision=precise
    ) + use_wide * jnp.einsum("mthf,mhfe->mthe", query_wide, state_in, precision=precise)
    denominator = jnp.transpose(jnp.sum(scores, axis=-1), (0, 2, 1)) + use_in[
        :, :, None
    ] * jnp.einsum("mthf,mhf->mth", query_wide, sum_in, precision=precise)
    attended = numerator / denominator[..., None]
    attended_low = attended.reshape(total_rows, model_width).astype(bfloat)
    branch = jnp.dot(
        attended_low, output_weight, preferred_element_type=single
    ) + output_bias.astype(single)
    middle = flat_input + branch
    normed_two, unit_two, inverse_two = norm_forward(
        middle, gain_two.astype(single), bias_two.astype(single)
    )
    normed_two_low = normed_two.astype(bfloat)
    expanded = jnp.dot(
        normed_two_low, expand_weight, preferred_element_type=single
    ) + expand_bias.astype(single)
    gelu_value, gelu_pull = jax.vjp(partial(jax.nn.gelu, approximate=True), expanded)
    hidden_low = gelu_value.astype(bfloat)
    result = (
        middle
        + jnp.dot(hidden_low, contract_weight, preferred_element_type=single)
        + contract_bias.astype(single)
    )
    block_output = result.astype(bfloat).reshape(micro_count, row_count, model_width)
    grad_contract = cotangent.reshape(total_rows, model_width)
    grad_wide = grad_contract.astype(single)
    hidden_grad = jnp.einsum(
        "rd,fd->rf", grad_contract, contract_weight, preferred_element_type=single
    )
    expanded_grad = gelu_pull(hidden_grad)[0].astype(bfloat)
    normed_two_grad = jnp.einsum(
        "rf,df->rd", expanded_grad, expand_weight, preferred_element_type=single
    )
    middle_norm_grad, gain_two_grad, bias_two_grad = norm_backward(
        normed_two_grad, unit_two, inverse_two, gain_two.astype(single)
    )
    middle_grad = grad_wide + middle_norm_grad
    branch_low = middle_grad.astype(bfloat)
    attended_grad = jnp.einsum(
        "rd,ed->re", branch_low, output_weight, preferred_element_type=single
    ).reshape(micro_count, row_count, head_count, head_width)
    numer_grad = attended_grad / denominator[..., None]
    denom_grad = -jnp.sum(attended_grad * attended, axis=-1) / denominator
    score_grad = (
        jnp.einsum("mthe,mshe->mhts", numer_grad, value_wide, precision=precise)
        + jnp.transpose(denom_grad, (0, 2, 1))[..., None]
    ) * attend_mask[:, None]
    query_feat_grad = jnp.einsum(
        "mhts,mshf->mthf", score_grad, key_wide, precision=precise
    ) + use_wide * (
        jnp.einsum("mthe,mhfe->mthf", numer_grad, state_in, precision=precise)
        + denom_grad[..., None] * sum_in[:, None]
    )
    key_feat_grad = jnp.einsum("mhts,mthf->mshf", score_grad, query_wide, precision=precise)
    value_grad = jnp.einsum("mhts,mthe->mshe", scores, numer_grad, precision=precise)
    query_used = query_wide * use_wide
    state_local_grad = jnp.einsum("mthf,mthe->mhfe", query_used, numer_grad, precision=precise)
    sum_local_grad = jnp.einsum("mthf,mth->mhf", query_used, denom_grad, precision=precise)
    state_out_grad, sum_out_grad, chain_rest = entering(
        (state_local_grad, sum_local_grad, keep_state),
        "seq",
        carry_combine,
        (zero_state, zero_sum, one_keep),
        True,
    )
    last_wide = in_last[:, :, None, None]
    key_feat_grad = key_feat_grad + last_wide * (
        jnp.einsum("mhfe,mthe->mthf", state_out_grad, value_wide, precision=precise)
        + sum_out_grad[:, None]
    )
    value_grad = value_grad + last_wide * jnp.einsum(
        "mthf,mhfe->mthe", key_wide, state_out_grad, precision=precise
    )
    query_vec_grad, query_map_grad = feature_backward(
        query_feat_grad.reshape(total_rows, head_count, feat_width),
        query_pos,
        query_neg,
        queries,
        query_map,
    )
    key_vec_grad, key_map_grad = feature_backward(
        key_feat_grad.reshape(total_rows, head_count, feat_width),
        key_pos,
        key_neg,
        key_rows,
        key_map,
    )
    projected_grad = jnp.concatenate(
        [
            query_vec_grad.reshape(total_rows, model_width),
            key_vec_grad.reshape(total_rows, model_width),
            value_grad.reshape(total_rows, model_width),
        ],
        axis=1,
    ).astype(bfloat)
    normed_grad = jnp.einsum(
        "rc,dc->rd", projected_grad, project_weight, preferred_element_type=single
    )
    input_norm_grad, gain_one_grad, bias_one_grad = norm_backward(
        normed_grad, unit_one, inverse_one, gain_one.astype(single)
    )
    input_grad = (
        (middle_grad + input_norm_grad).astype(bfloat).reshape(micro_count, row_count, model_width)
    )
    shares = (
        lax.psum_scatter(
            jnp.einsum("rd,rc->dc", normed_low, projected_grad, preferred_element_type=single),
            "seq",
            scatter_dimension=0,
            tiled=True,
        ),
        lax.psum_scatter(
            jnp.einsum("rd,re->de", attended_low, branch_low, preferred_element_type=single),
            "seq",
            scatter_dimension=0,
            tiled=True,
        ),
        lax.psum_scatter(
            jnp.einsum("rd,rf->df", normed_two_low, expanded_grad, preferred_element_type=single),
            "seq",
            scatter_dimension=0,
            tiled=True,
        ),
        lax.psum_scatter(
            jnp.einsum(
                "rf,rd->fd",
                hidden_low[0 : 0 + total_rows],
                grad_contract,
                preferred_element_type=single,
            ),
            "seq",
            scatter_dimension=0,
            tiled=True,
        ),
    )
    totals = lax.psum((shares[0], shares[1], shares[2], shares[3]), "batch")
    project_bias_grad = jnp.sum(projected_grad.astype(single), axis=0)
    output_bias_grad = jnp.sum(branch_low.astype(single), axis=0)
    expand_bias_grad = jnp.sum(expanded_grad.astype(single), axis=0)
    contract_bias_grad = jnp.sum(grad_wide, axis=0)
    small_sums = lax.psum(
        (
            gain_one_grad,
            bias_one_grad,
            project_bias_grad,
            query_map_grad,
            key_map_grad,
            output_bias_grad,
            gain_two_grad,
            bias_two_grad,
            expand_bias_grad,
            contract_bias_grad,
        ),
        ("seq", "batch"),
    )
    return (
        block_output,
        input_grad,
        small_sums[0],
        small_sums[1],
        totals[0],
        small_sums[2],
        small_sums[3],
        small_sums[4],
        totals[1],
        small_sums[5],
        small_sums[6],
        small_sums[7],
        totals[2],
        small_sums[8],
        totals[3],
        small_sums[9],
    )


def solution(mesh):
    placed = (
        P("batch", "seq", None),
        P(),
        P(),
        P(),
        P(),
        P(),
        P(),
        P(),
        P(),
        P(),
        P(),
        P(),
        P(),
        P(),
        P(),
        P("batch", None),
        P("batch", "seq", None),
    )
    return jax.shard_map(
        per_device,
        mesh=mesh,
        in_specs=placed,
        out_specs=(
            P("batch", "seq", None),
            P("batch", "seq", None),
            P(),
            P(),
            P("seq", None),
            P(),
            P(),
            P(),
            P("seq", None),
            P(),
            P(),
            P(),
            P("seq", None),
            P(),
            P("seq", None),
            P(),
        ),
        check_vma=False,
    )
```

profile of v0, /device:TPU:0, one launch (start us, length us, event | category | flops | bytes accessed | tf_op | source)
XLA Modules:
  0.0 1310.7 jit_solution(12416251887906377907)
XLA Ops:
  17.1 3.3 fusion.148
  41.6 3.8 convert_reduce_fusion.2
  48.4 23.8 %all-reduce = f32[32]{0:T(128)S(1)} all-reduce(f32[32]{0:T(128)} %copy-done.68), channel_id=3, replica_groups=mesh['seq'=8,'batch'=4] {'seq'}, use_global_device_ids=true, to_apply=%add | all-reduce | flops 32 | bytes 256
  79.7 3.3 fusion.146
  96.3 33.9 %all-gather.2 = f32[32,12,128]{2,1,0:T(8,128)} all-gather(f32[4,12,128]{2,1,0:T(8,128)} %get-tuple-element.288), channel_id=4, replica_groups=mesh['seq'=8,'batch'=4] {'seq'}, dimensions={0}, use_global_device_ids=true | all-gather | bytes 221184 | tf_op jit(solution)/shard_map/all_gather | solution.py:18
  139.9 90.0 %all-gather.8.cloned.1.call-done = f32[32,12,128,64]{2,3,1,0:T(8,128)} async-done(((f32[4,12,128,64]{2,3,1,0:T(8,128)}), f32[32,12,128,64]{2,3,1,0:T(8,128)}) %all-gather.8.cloned.1.call-update) | async-done | bytes 12582928 | tf_op jit(solution)/shard_map/all_gather | solution.py:18
  232.9 4.1 fusion.121
  237.6 6.6 fusion.150
  250.8 10.6 convert_reduce_fusion
  261.4 3.6 multiply_reduce_fusion.1
  272.0 6.2 fusion.25
  278.3 3.8 fusion.100
  282.6 10.3 fusion.141
  292.9 8.9 fusion.139
  314.2 8.0 fusion.23
  322.2 4.9 copy.111
  327.1 5.1 reshape.636
  332.1 124.7 %all-gather.4 = f32[32,12,128]{2,1,0:T(8,128)} all-gather(f32[4,12,128]{2,1,0:T(8,128)} %bitcast.244), channel_id=6, replica_groups=mesh['seq'=8,'batch'=4] {'seq'}, dimensions={0}, use_global_device_ids=true | all-gather | bytes 221184 | tf_op jit(solution)/shard_map/all_gather | solution.py:18
  460.1 6.0 convolution_convert_fusion.1
  466.1 9.9 fusion.28
  476.0 3.4 fusion.26
  479.4 70.3 %all-gather.10.cloned.1.call-done = f32[32,12,128,64]{2,3,1,0:T(8,128)} async-done(((f32[4,12,128,64]{2,3,1,0:T(8,128)}), f32[32,12,128,64]{2,3,1,0:T(8,128)}) %all-gather.10.cloned.1.call-update) | async-done | bytes 12582928 | tf_op jit(solution)/shard_map/all_gather | solution.py:18
  552.3 96.3 %while.31 = (s32[]{:T(128)}, f32[4,12,128,64]{3,2,1,0:T(8,128)}, f32[4,12,128]{2,1,0:T(8,128)}, s32[]{:T(128)}, f32[8,4,12,128,64]{3,4,2,1,0:T(8,128)}, /*index=...) while((s32[]{:T(128)}, f32[4,12,128,64]{3,2,1,0:T(8,128)}, ...), condition=%wide.region_22.23_spmd, body=%wide.region_21.22_spmd.sunk | while | flops 798726 | bytes 11084015 | solution.py:27
  560.6 5.3 bitcast_add_fusion.13
  574.2 5.4 bitcast_add_fusion.13
  584.5 3.3 copy.178
  587.8 5.3 bitcast_add_fusion.13
  601.4 5.3 bitcast_add_fusion.13
  615.0 5.4 bitcast_add_fusion.13
  628.7 6.1 bitcast_add_fusion.13
  643.1 5.4 bitcast_add_fusion.13
  648.7 6.0 fusion.99
  656.9 4.9 bitcast_add_fusion.4
  661.8 4.9 copy.115
  666.7 5.2 reshape.638
  675.1 5.9 convolution_convert_fusion
  681.0 6.8 fusion.137
  687.9 6.1 fusion.90
  694.1 6.1 fusion.95
  702.4 84.5 %reduce-scatter.11.cloned.1.call-done = f32[384,768]{1,0:T(8,128)} async-done(((f32[3072,768]{1,0:T(8,128)}), f32[384,768]{1,0:T(8,128)}) %reduce-scatter.11.cloned.1.call-update) | async-done | bytes 1179664 | tf_op jit(solution)/shard_map/reduce_scatter | solution.py:292
  786.9 165.9 %reduce-scatter.9.cloned.1.call-done = f32[96,3072]{1,0:T(8,128)} async-done(((f32[768,3072]{1,0:T(8,128)}), f32[96,3072]{1,0:T(8,128)}) %reduce-scatter.9.cloned.1.call-update) | async-done | bytes 1179664 | tf_op jit(solution)/shard_map/reduce_scatter | solution.py:286
  952.8 131.7 %reduce-scatter.5.cloned.1.call-done = f32[96,2304]{1,0:T(8,128)} async-done(((f32[768,2304]{1,0:T(8,128)}), f32[96,2304]{1,0:T(8,128)}) %reduce-scatter.5.cloned.1.call-update) | async-done | bytes 884752 | tf_op jit(solution)/shard_map/reduce_scatter | solution.py:274
  1085.2 9.6 add_convert_fusion.1
  1095.9 4.2 fusion.56
  1100.2 41.3 %all-reduce.1 = (f32[768]{0:T(1024)}, f32[768]{0:T(1024)}, f32[2304]{0:T(1024)}, f32[768]{0:T(1024)}, f32[768]{0:T(1024)}, /*index=5*/f32[768]{0:T(1024)}, f32[3072]{0:T(1024)}, f32[768]{0:T(1024)}) all-reduce(f32[768]{0:T(1024)} %get-tuple-element.236, ...), channel_id=1, replica_groups=mesh['seq'=8,'batch'=4] {'seq','batch'}, use_global_device_ids=true, to_apply=%region_28.29 | all-reduce | flops 9984 | bytes 79872 | tf_op jit(solution)/shard_map/psum | solution.py:309
  1142.8 3.6 fusion.55
  1146.4 73.4 %all-reduce.7.cloned.1.call-done = (f32[12,64,64]{2,1,0:T(8,128)}, f32[12,64,64]{2,1,0:T(8,128)}) async-done(((f32[12,64,64]{2,1,0:T(8,128)}, f32[12,64,64]{2,1,0:T(8,128)}), (f32[12,64,64]{2,1,0:T(8,128)}, f32[12,64,64]{2,1,0:T(8,128)})) %all-reduce.7.cloned.1.call-update) | async-done | bytes 393232 | tf_op jit(solution)/shard_map/psum | solution.py:309
  1219.9 77.0 %all-reduce.9.cloned.1.call-done = (f32[96,2304]{1,0:T(8,128)}, f32[96,768]{1,0:T(8,128)}, f32[96,3072]{1,0:T(8,128)}, f32[384,768]{1,0:T(8,128)}) async-done(((f32[96,2304]{1,0:T(8,128)}, f32[96,768]{1,0:T(8,128)}, f32[96,3072]{1,0:T(8,128)}, f32[384,768]{1,0:T(8,128)}), (f32[96,2304]{1,0:T(8,128)}, f32[96,768]{1,0:T(8,128)}, f32[96,3072]{1,0:T(8,128)}, f32[384,768]{1,0:T(8,128)})) %all-reduce.9.cloned.1.call-update) | async-done | bytes 3538960 | tf_op jit(solution)/shard_map/psum | solution.py:304
  (273 shorter events, 171.3 us)
Async XLA Ops:
  7.2 4.1 copy-start
  7.2 3.1 copy-start.65
  7.2 3.1 copy-start.66
  7.2 3.1 copy-start.58
  7.2 222.6 %all-gather.8.cloned.1.call-start = ((), (), s32[]{:S(2)}) async-start(), calls=%async_computation.8 | async-start | bytes 14155776 | tf_op jit(solution)/shard_map/all_gather | solution.py:18
  7.3 3.6 copy-start.16
  20.4 3.3 copy-start.64
  24.2 16.6 %copy-start.59 = (s32[4]{0:T(128)}, s32[4]{0:T(128)S(1)}, u32[]{:S(2)}) copy-start(s32[4]{0:T(128)S(1)} %get-tuple-element.301) | copy-start | bytes 52
  41.6 5.0 copy-start.19
  48.4 501.3 %all-gather.10.cloned.1.call-start = ((), (), s32[]{:S(2)}) async-start(), calls=%async_computation.9 | async-start | bytes 14155776 | tf_op jit(solution)/shard_map/all_gather | solution.py:18
  130.2 2.9 copy-start.60
  130.2 2.9 copy-start.61
  130.2 3.2 copy-start.8
  133.5 3.5 copy-start.20
  232.9 4.1 copy-start.44
  232.9 4.7 copy-start.4
  237.6 6.6 copy-start.38
  237.6 7.2 copy-start.36
  246.3 18.7 %copy-start.26 = (f32[512,768]{1,0:T(8,128)}, f32[512,768]{1,0:T(8,128)S(1)}, u32[]{:S(2)}) copy-start(f32[512,768]{1,0:T(8,128)S(1)} %get-tuple-element.316) | copy-start | bytes 4718596
  248.0 17.0 %copy-start.57 = (f32[512]{0:T(512)}, f32[512]{0:T(512)S(1)}, u32[]{:S(2)}) copy-start(f32[512]{0:T(512)S(1)} %add_rsqrt_fusion) | copy-start | bytes 6148
  250.8 10.6 copy-start.70
  261.4 3.6 copy-start.71
  278.3 424.2 %reduce-scatter.7.cloned.1.call-start = ((), (), s32[]{:S(2)}) async-start(), calls=%async_computation.5 | async-start | bytes 2654208 | tf_op jit(solution)/shard_map/reduce_scatter | solution.py:280
  282.1 504.8 %reduce-scatter.11.cloned.1.call-start = ((), (), s32[]{:S(2)}) async-start(), calls=%async_computation.7 | async-start | bytes 10616832 | tf_op jit(solution)/shard_map/reduce_scatter | solution.py:292
  292.9 659.9 %reduce-scatter.9.cloned.1.call-start = ((), (), s32[]{:S(2)}) async-start(), calls=%async_computation.6 | async-start | bytes 10616832 | tf_op jit(solution)/shard_map/reduce_scatter | solution.py:286
  301.9 782.6 %reduce-scatter.5.cloned.1.call-start = ((), (), s32[]{:S(2)}) async-start(), calls=%async_computation.4 | async-start | bytes 7962624 | tf_op jit(solution)/shard_map/reduce_scatter | solution.py:274
  304.3 3.7 copy-start.45
  304.3 3.7 copy-start.48
  304.3 3.7 copy-start.11
  304.3 3.7 copy-start.21
  308.0 3.4 copy-start.9
  308.1 3.4 copy-start.24
  466.1 10.0 copy-start.6
  466.1 10.0 copy-start.15
  466.1 10.0 copy-start.25
  466.1 10.0 copy-start.43
  648.6 7.7 copy-start.13
  648.7 7.7 copy-start.22
  648.7 7.7 copy-start.33
  687.9 532.0 %all-reduce.7.cloned.1.call-start = ((), (), s32[]{:S(2)}) async-start(), calls=%async_computation.10 | async-start | bytes 1572864 | tf_op jit(solution)/shard_map/psum | solution.py:309
  694.1 6.5 copy-start.67
  700.2 596.6 %all-reduce.9.cloned.1.call-start = ((), (), s32[]{:S(2)}) async-start(), calls=%async_computation.11 | async-start | bytes 7077888 | tf_op jit(solution)/shard_map/psum | solution.py:304
  1085.2 9.6 copy-start.28
  1085.2 9.6 copy-start.30
  1085.2 9.6 copy-start.31
  1296.9 3.0 copy-start.40
  1296.9 3.8 copy-start.46
  1296.9 4.5 copy-start.35
  (34 other events, 58.0 us)
Sparse Core Ops, SparseCore 0:
  48.5 181.2 all-gather.7
  278.4 271.2 all-gather.9
  553.2 67.8 reduce-scatter.6
  624.5 162.3 reduce-scatter.10
  790.3 162.3 reduce-scatter.8
  956.3 128.1 reduce-scatter.4
  1091.3 128.4 all-reduce.6
  1222.4 74.3 all-reduce.8
where the time goes:
time: 1320 us; the launch traced here: 1310 us
  waiting for transfers between devices  693 us (52%)
  blocking collectives  224 us (17%)
  matrix products  166 us (13%)
  local copies, waits for them, and re-layouts  129 us (10%)
  other arithmetic  81.8 us (6%)
  between operations  16 us (1%)
    reduce_scatter x1, waiting for transfers between devices, per_device(): lax.psum_scatter(jnp.einsum('rd,rf->df', normed_two_low, expanded_grad, p...  166 us
    all_gather x2, waiting for transfers between devices, entering(): gathered = jax.tree.map(lambda a: lax.all_gather(a, axis), part)  160 us
    all_gather x2, blocking collectives, entering(): gathered = jax.tree.map(lambda a: lax.all_gather(a, axis), part)  159 us
    reduce_scatter x1, waiting for transfers between devices, per_device(): lax.psum_scatter(jnp.einsum('rd,rc->dc', normed_low, projected_grad, pref...  132 us
    reduce_scatter x1, waiting for transfers between devices, per_device(): lax.psum_scatter(jnp.einsum('rf,rd->fd', hidden_low[0:0 + total_rows], gr...  84.5 us
    psum x1, waiting for transfers between devices, per_device(): totals = lax.psum((shares[0], shares[1], shares[2], shares[3]), 'batch')  77 us
    psum x1, waiting for transfers between devices, per_device(): lax.psum((gain_one_grad, bias_one_grad, project_bias_grad, query_map_grad...  73.4 us
    dynamic_slice x14, local copies, waits for them, and re-layouts, one(): lax.dynamic_index_in_dim(a, source, 0, False)  42.8 us
  transfers between devices with their start and end apart: 8, of which 7 were waited for; matrix products, arithmetic and copies ran while one was open for 21% of the time, Pallas kernels for 0%

commit v1 on v0

v1 whole, which is shorter than its diff:
```python
from functools import partial

import jax
import jax.numpy as jnp
from jax import lax
from jax.experimental import pallas as pl
from jax.experimental.pallas import tpu as pltpu
from jax.sharding import PartitionSpec as P

epsilon = 1e-05
bfloat = jnp.bfloat16
single = jnp.float32
MESH = pl.DeviceIdType.MESH
VMEM_LIMIT = 56 * 1024 * 1024


def matmul(a, b, contract):
    return lax.dot_general(
        a, b, (((contract[0],), (contract[1],)), ((), ())), preferred_element_type=single
    )


def norm_forward(values, gain_vector, shift_vector):
    centered = values - jnp.mean(values, axis=-1, keepdims=True)
    inverse = lax.rsqrt(jnp.mean(centered * centered, axis=-1, keepdims=True) + epsilon)
    unit_rows = centered * inverse
    return (unit_rows * gain_vector + shift_vector, unit_rows, inverse)


def norm_backward(gradient, unit_rows, inverse, gain_vector):
    inner = gradient * gain_vector
    result = inverse * (
        inner
        - jnp.mean(inner, axis=-1, keepdims=True)
        - unit_rows * jnp.mean(inner * unit_rows, axis=-1, keepdims=True)
    )
    return (result, jnp.sum(gradient * unit_rows, axis=0), jnp.sum(gradient, axis=0))


def doc_number(positions, first_bound, second_bound):
    return (positions >= first_bound).astype(jnp.int32) + (positions >= second_bound).astype(
        jnp.int32
    )


def two_softmaxes(mapped):
    up = jnp.exp(mapped - jnp.max(mapped, axis=0, keepdims=True))
    down = jnp.exp(jnp.min(mapped, axis=0, keepdims=True) - mapped)
    return (
        up / jnp.sum(up, axis=0, keepdims=True),
        down / jnp.sum(down, axis=0, keepdims=True),
    )


def with_ones(rows):
    return jnp.concatenate([rows, jnp.ones((16, rows.shape[1]), rows.dtype)], axis=0)


def state_rows(state, micro, head_width):
    low = state[micro * head_width : (micro + 1) * head_width, :]
    count = state.shape[0] // (head_width + 2)
    total = state[count * head_width + micro : count * head_width + micro + 1, :]
    return jnp.concatenate([low, jnp.broadcast_to(total, (16, low.shape[1]))], axis=0)


def feature_kernel(micro_count, q_ref, k_ref, v_ref, qm_ref, km_ref, last_ref, fq_ref, fk_ref, state_ref):
    head_width = q_ref.shape[0]
    rows = q_ref.shape[1] // micro_count
    for source, weights, target in ((q_ref, qm_ref, fq_ref), (k_ref, km_ref, fk_ref)):
        mapped = matmul(weights[0], source[...], (0, 0))
        up, down = two_softmaxes(mapped)
        target[...] = jnp.concatenate([up, down], axis=0).astype(bfloat)
    wide = with_ones(v_ref[...]) * last_ref[...]
    sums = []
    for m in range(micro_count):
        part = slice(m * rows, (m + 1) * rows)
        local = matmul(wide[:, part], fk_ref[:, part], (1, 1))
        state_ref[0, m * head_width : (m + 1) * head_width, :] = local[:head_width]
        sums.append(local[head_width : head_width + 1])
    sums = jnp.concatenate(sums + sums, axis=0)
    state_ref[0, micro_count * head_width :, :] = sums


def attend_kernel(micro_count, fq_ref, fk_ref, v_ref, state_ref, mask_ref, use_ref, att_ref, low_ref, den_ref):
    head_width = v_ref.shape[0]
    rows = v_ref.shape[1] // micro_count
    wide = with_ones(v_ref[...])
    used = fq_ref[...] * use_ref[...]
    for m in range(micro_count):
        part = slice(m * rows, (m + 1) * rows)
        scores = matmul(fk_ref[:, part], fq_ref[:, part], (0, 0)) * mask_ref[m]
        state = state_rows(state_ref[0], m, head_width).astype(bfloat)
        numer = matmul(wide[:, part], scores.astype(bfloat), (1, 0)) + matmul(
            state, used[:, part], (1, 0)
        )
        denom = numer[head_width : head_width + 1]
        attended = numer[:head_width] / denom
        att_ref[:, part] = attended
        low_ref[:, part] = attended.astype(bfloat)
        den_ref[0, :, part] = denom


def score_grads(grad, attended, denom):
    inverse = 1.0 / denom
    numer_grad = grad * inverse
    denom_grad = -jnp.sum(grad * attended, axis=0, keepdims=True) * inverse
    pad = jnp.zeros((15, grad.shape[1]), single)
    return jnp.concatenate([numer_grad, denom_grad, pad], axis=0)


def state_grad_kernel(micro_count, grad_ref, att_ref, den_ref, fq_ref, use_ref, state_ref):
    head_width = grad_ref.shape[0]
    rows = grad_ref.shape[1] // micro_count
    wide = (score_grads(grad_ref[...], att_ref[...], den_ref[0]) * use_ref[...]).astype(bfloat)
    sums = []
    for m in range(micro_count):
        part = slice(m * rows, (m + 1) * rows)
        local = matmul(wide[:, part], fq_ref[:, part], (1, 1))
        state_ref[0, m * head_width : (m + 1) * head_width, :] = local[:head_width]
        sums.append(local[head_width : head_width + 1])
    sums = jnp.concatenate(sums + sums, axis=0)
    state_ref[0, micro_count * head_width :, :] = sums


def feature_backward(feat_grad, source, weights):
    head_width = source.shape[0]
    up, down = two_softmaxes(matmul(weights, source, (0, 0)))
    grad_up, grad_down = (feat_grad[:head_width], feat_grad[head_width:])
    mapped = up * (grad_up - jnp.sum(up * grad_up, axis=0, keepdims=True)) - down * (
        grad_down - jnp.sum(down * grad_down, axis=0, keepdims=True)
    )
    low = mapped.astype(bfloat)
    return (matmul(weights, low, (1, 0)), matmul(source, low, (1, 1)))


def backward_kernel(
    micro_count, q_ref, k_ref, v_ref, qm_ref, km_ref, fq_ref, fk_ref, grad_ref, att_ref, den_ref,
    state_ref, out_grad_ref, mask_ref, use_ref, last_ref, proj_ref, qmg_ref, kmg_ref, fqg, fkg,
):
    head_width = q_ref.shape[0]
    rows = q_ref.shape[1] // micro_count
    grads = score_grads(grad_ref[...], att_ref[...], den_ref[0])
    low_grads = grads.astype(bfloat)
    used_grads = (grads * use_ref[...]).astype(bfloat)
    wide = with_ones(v_ref[...])
    wide_last = wide * last_ref[...]
    for m in range(micro_count):
        part = slice(m * rows, (m + 1) * rows)
        fq, fk = (fq_ref[:, part], fk_ref[:, part])
        mask = mask_ref[m]
        scores = (matmul(fk, fq, (0, 0)) * mask).astype(bfloat)
        grad_scores = (matmul(wide[:, part], low_grads[:, part], (0, 0)) * mask).astype(bfloat)
        state = state_rows(state_ref[0], m, head_width).astype(bfloat)
        out_grad = state_rows(out_grad_ref[0], m, head_width)
        row = lax.broadcasted_iota(jnp.int32, out_grad.shape, 0)
        out_grad = jnp.where(row <= head_width, out_grad, 0.0).astype(bfloat)
        fqg[:, part] = matmul(fk, grad_scores, (1, 0)) + matmul(state, used_grads[:, part], (0, 0))
        fkg[:, part] = matmul(fq, grad_scores, (1, 1)) + matmul(out_grad, wide_last[:, part], (0, 0))
        value_grad = matmul(low_grads[:head_width, part], scores, (1, 1)) + matmul(
            out_grad[:head_width], fk * last_ref[:, part], (1, 0)
        )
        proj_ref[2, :, part] = value_grad.astype(bfloat)
    q_grad, qmg = feature_backward(fqg[...], q_ref[...], qm_ref[0])
    proj_ref[0] = q_grad.astype(bfloat)
    qmg_ref[0] = qmg
    k_grad, kmg = feature_backward(fkg[...], k_ref[...], km_ref[0])
    proj_ref[1] = k_grad.astype(bfloat)
    kmg_ref[0] = kmg


def scan_kernel(
    reverse, count, local_ref, mask_ref, out_ref, carry, onward, aside, beside,
    carry_send, carry_recv, side_send, side_recv,
):
    place, column = (lax.axis_index("seq"), lax.axis_index("batch"))
    high, low = (place // 2, lax.rem(place, 2))
    length = count // 2
    if reverse:
        lap = length - 1 - high
        ahead, behind = (place - 2, place + 2)
    else:
        lap = high
        ahead, behind = (place + 2, place - 2)
    partner = place + 1 - 2 * low
    first = lap == 0
    final = lap == length - 1
    chunks = local_ref.shape[0]
    barrier = pltpu.get_barrier_semaphore()

    @pl.when(jnp.logical_not(final))
    def _():
        pl.semaphore_signal(barrier, inc=1, device_id=(ahead, column), device_id_type=MESH)

    @pl.when(jnp.logical_not(first))
    def _():
        pl.semaphore_signal(barrier, inc=1, device_id=(behind, column), device_id_type=MESH)

    pl.semaphore_signal(barrier, inc=1, device_id=(partner, column), device_id_type=MESH)
    pl.semaphore_wait(
        barrier, 1 + jnp.where(first, 0, 1) + jnp.where(final, 0, 1)
    )

    def along(i):
        return pltpu.make_async_remote_copy(
            src_ref=onward.at[i], dst_ref=carry.at[i], send_sem=carry_send.at[i],
            recv_sem=carry_recv.at[i], device_id=(ahead, column), device_id_type=MESH,
        )

    def across(i):
        return pltpu.make_async_remote_copy(
            src_ref=aside.at[i], dst_ref=beside.at[i], send_sem=side_send.at[i],
            recv_sem=side_recv.at[i], device_id=(partner, column), device_id_type=MESH,
        )

    @pl.when(first)
    def _():
        carry[...] = jnp.zeros_like(carry)

    def one(i, _):
        @pl.when(jnp.logical_not(first))
        def _():
            along(i).wait_recv()

        state, local = (carry[i], local_ref[i])
        aside[i] = mask_ref[2] * state + mask_ref[3] * local
        across(i).start()

        @pl.when(jnp.logical_not(final))
        def _():
            onward[i] = mask_ref[0] * state + mask_ref[1] * local
            along(i).start()

        return 0

    lax.fori_loop(0, chunks, one, 0)

    def two(i, _):
        across(i).wait_recv()
        out_ref[i] = mask_ref[4] * carry[i] + beside[i]
        return 0

    lax.fori_loop(0, chunks, two, 0)

    def three(i, _):
        across(i).wait_send()

        @pl.when(jnp.logical_not(final))
        def _():
            along(i).wait_send()

        return 0

    lax.fori_loop(0, chunks, three, 0)


def scan_states(local, masks, count, reverse, identity):
    chunks = local.shape[0]
    whole = pl.BlockSpec(memory_space=pltpu.VMEM)
    return pl.pallas_call(
        partial(scan_kernel, reverse, count),
        out_shape=jax.ShapeDtypeStruct(local.shape, single),
        in_specs=[whole, whole],
        out_specs=whole,
        scratch_shapes=[pltpu.VMEM(local.shape, single)] * 4
        + [pltpu.SemaphoreType.DMA((chunks,))] * 4,
        compiler_params=pltpu.CompilerParams(
            collective_id=identity, has_side_effects=True, vmem_limit_bytes=VMEM_LIMIT
        ),
    )(local, masks)


def scan_masks(bounds, first_row, row_count, place, micro_count, head_width, reverse):
    def doc(position):
        return doc_number(position, bounds[:, 0], bounds[:, 1])

    low = lax.rem(place, 2)
    base = first_row - low * row_count
    step = 2 * row_count
    if reverse:
        low = 1 - low
        own_edge = doc(first_row)
        pair = doc(base + step - 1)
        ahead = doc(base - 1)
        inner = doc(base + row_count - 1)
    else:
        own_edge = doc(first_row + row_count - 1)
        pair = doc(base - 1)
        ahead = doc(base + step - 1)
        inner = doc(base + row_count - 1)
    if reverse:
        own_edge = doc(first_row - 1)
    one = jnp.ones((micro_count,), single)
    keep = (pair == inner).astype(single)
    masks = jnp.stack(
        [
            (pair == ahead).astype(single),
            (own_edge == ahead).astype(single),
            jnp.where(low == 0, keep, one),
            jnp.where(low == 0, one, 0 * one),
            jnp.where(low == 0, one, keep),
        ]
    )
    wide = jnp.concatenate([jnp.repeat(masks, head_width, axis=1), masks, masks], axis=1)
    return jnp.broadcast_to(wide[:, :, None], wide.shape + (2 * head_width,))


def per_device(
    inputs, gain_one, bias_one, project_weight, project_bias, query_map, key_map, output_weight,
    output_bias, gain_two, bias_two, expand_weight, expand_bias, contract_weight, contract_bias,
    bounds, cotangent,
):
    micro_count, row_count, model_width = inputs.shape
    head_count, head_width = (query_map.shape[0], query_map.shape[1])
    feat_width = 2 * head_width
    total_rows = micro_count * row_count
    count = lax.axis_size("seq")
    place = lax.axis_index("seq")
    first_row = place * row_count
    positions = first_row + jnp.arange(row_count, dtype=jnp.int32)
    first_bound, second_bound = (bounds[:, 0:1], bounds[:, 1:2])
    doc_ids = doc_number(positions[None, :], first_bound, second_bound)
    doc_prev = doc_number(first_row - 1, first_bound, second_bound)
    doc_last = doc_number(first_row + row_count - 1, first_bound, second_bound)
    use_in = (doc_ids == doc_prev).astype(single).reshape(1, total_rows)
    in_last = (doc_ids == doc_last).astype(single).reshape(1, total_rows)
    use_low, last_low = (use_in.astype(bfloat), in_last.astype(bfloat))
    causal = positions[:, None] <= positions[None, :]
    mask = (causal[None] & (doc_ids[:, :, None] == doc_ids[:, None, :])).astype(single)
    masks_forward = scan_masks(bounds, first_row, row_count, place, micro_count, head_width, False)
    masks_reverse = scan_masks(bounds, first_row, row_count, place, micro_count, head_width, True)

    flat_input = inputs.reshape(total_rows, model_width).astype(single)
    normed, unit_one, inverse_one = norm_forward(
        flat_input, gain_one.astype(single), bias_one.astype(single)
    )
    normed_low = normed.astype(bfloat)
    projected = (
        jnp.einsum("dc,rd->cr", project_weight, normed_low, preferred_element_type=single)
        + project_bias.astype(single)[:, None]
    ).astype(bfloat)

    head_rows = lambda offset: pl.BlockSpec((head_width, total_rows), lambda h: (h + offset, 0))
    map_spec = pl.BlockSpec((1, head_width, head_width), lambda h: (h, 0, 0))
    feat_spec = pl.BlockSpec((feat_width, total_rows), lambda h: (h, 0))
    line_spec = pl.BlockSpec((1, total_rows), lambda h: (0, 0))
    den_spec = pl.BlockSpec((1, 1, total_rows), lambda h: (h, 0, 0))
    state_height = micro_count * (head_width + 2)
    state_spec = pl.BlockSpec((1, state_height, feat_width), lambda h: (h, 0, 0))
    mask_spec = pl.BlockSpec((micro_count, row_count, row_count), lambda h: (0, 0, 0))
    q_spec, k_spec, v_spec = (head_rows(0), head_rows(head_count), head_rows(2 * head_count))
    feat_shape = jax.ShapeDtypeStruct((head_count * feat_width, total_rows), bfloat)
    state_shape = jax.ShapeDtypeStruct((head_count, state_height, feat_width), single)
    params = pltpu.CompilerParams(vmem_limit_bytes=VMEM_LIMIT)

    feat_query, feat_key, local_state = pl.pallas_call(
        partial(feature_kernel, micro_count),
        grid=(head_count,),
        in_specs=[q_spec, k_spec, v_spec, map_spec, map_spec, line_spec],
        out_specs=[feat_spec, feat_spec, state_spec],
        out_shape=[feat_shape, feat_shape, state_shape],
        compiler_params=params,
    )(projected, projected, projected, query_map, key_map, last_low)
    state_in = scan_states(local_state, masks_forward, count, False, 1)
    attended, attended_low, denominator = pl.pallas_call(
        partial(attend_kernel, micro_count),
        grid=(head_count,),
        in_specs=[feat_spec, feat_spec, v_spec, state_spec, mask_spec, line_spec],
        out_specs=[head_rows(0), head_rows(0), den_spec],
        out_shape=[
            jax.ShapeDtypeStruct((model_width, total_rows), single),
            jax.ShapeDtypeStruct((model_width, total_rows), bfloat),
            jax.ShapeDtypeStruct((head_count, 1, total_rows), single),
        ],
        compiler_params=params,
    )(feat_query, feat_key, projected, state_in, mask, use_low)

    branch = jnp.einsum(
        "er,ed->rd", attended_low, output_weight, preferred_element_type=single
    ) + output_bias.astype(single)
    middle = flat_input + branch
    normed_two, unit_two, inverse_two = norm_forward(
        middle, gain_two.astype(single), bias_two.astype(single)
    )
    normed_two_low = normed_two.astype(bfloat)
    expanded = jnp.dot(
        normed_two_low, expand_weight, preferred_element_type=single
    ) + expand_bias.astype(single)
    gelu_value, gelu_pull = jax.vjp(partial(jax.nn.gelu, approximate=True), expanded)
    hidden_low = gelu_value.astype(bfloat)
    result = (
        middle
        + jnp.dot(hidden_low, contract_weight, preferred_element_type=single)
        + contract_bias.astype(single)
    )
    block_output = result.astype(bfloat).reshape(micro_count, row_count, model_width)
    grad_contract = cotangent.reshape(total_rows, model_width)
    grad_wide = grad_contract.astype(single)
    hidden_grad = jnp.einsum(
        "rd,fd->rf", grad_contract, contract_weight, preferred_element_type=single
    )
    expanded_grad = gelu_pull(hidden_grad)[0].astype(bfloat)
    normed_two_grad = jnp.einsum(
        "rf,df->rd", expanded_grad, expand_weight, preferred_element_type=single
    )
    middle_norm_grad, gain_two_grad, bias_two_grad = norm_backward(
        normed_two_grad, unit_two, inverse_two, gain_two.astype(single)
    )
    middle_grad = grad_wide + middle_norm_grad
    branch_low = middle_grad.astype(bfloat)
    attended_grad = jnp.einsum(
        "rd,ed->er", branch_low, output_weight, preferred_element_type=single
    )
    local_grad = pl.pallas_call(
        partial(state_grad_kernel, micro_count),
        grid=(head_count,),
        in_specs=[head_rows(0), head_rows(0), den_spec, feat_spec, line_spec],
        out_specs=state_spec,
        out_shape=state_shape,
        compiler_params=params,
    )(attended_grad, attended, denominator, feat_query, use_in)
    out_grad = scan_states(local_grad, masks_reverse, count, True, 2)
    proj_spec = pl.BlockSpec((3, head_width, total_rows), lambda h: (0, h, 0))
    projected_grad, query_map_grad, key_map_grad = pl.pallas_call(
        partial(backward_kernel, micro_count),
        grid=(head_count,),
        in_specs=[
            q_spec, k_spec, v_spec, map_spec, map_spec, feat_spec, feat_spec, head_rows(0),
            head_rows(0), den_spec, state_spec, state_spec, mask_spec, line_spec, line_spec,
        ],
        out_specs=[proj_spec, map_spec, map_spec],
        out_shape=[
            jax.ShapeDtypeStruct((3, model_width, total_rows), bfloat),
            jax.ShapeDtypeStruct(query_map.shape, single),
            jax.ShapeDtypeStruct(key_map.shape, single),
        ],
        scratch_shapes=[pltpu.VMEM((feat_width, total_rows), single)] * 2,
        compiler_params=params,
    )(
        projected, projected, projected, query_map, key_map, feat_query, feat_key, attended_grad,
        attended, denominator, state_in, out_grad, mask, use_in, last_low,
    )
    projected_grad = projected_grad.reshape(3 * model_width, total_rows)
    normed_grad = jnp.einsum(
        "cr,dc->rd", projected_grad, project_weight, preferred_element_type=single
    )
    input_norm_grad, gain_one_grad, bias_one_grad = norm_backward(
        normed_grad, unit_one, inverse_one, gain_one.astype(single)
    )
    input_grad = (
        (middle_grad + input_norm_grad).astype(bfloat).reshape(micro_count, row_count, model_width)
    )

    def scatter(value):
        return lax.psum_scatter(value, "seq", scatter_dimension=0, tiled=True)

    shares = (
        scatter(jnp.einsum("rd,cr->dc", normed_low, projected_grad, preferred_element_type=single)),
        scatter(jnp.einsum("er,rd->ed", attended_low, branch_low, preferred_element_type=single)),
        scatter(
            jnp.einsum("rd,rf->df", normed_two_low, expanded_grad, preferred_element_type=single)
        ),
        scatter(jnp.einsum("rf,rd->fd", hidden_low, grad_contract, preferred_element_type=single)),
    )
    totals = lax.psum(shares, "batch")
    project_bias_grad = jnp.sum(projected_grad.astype(single), axis=1)
    output_bias_grad = jnp.sum(branch_low.astype(single), axis=0)
    expand_bias_grad = jnp.sum(expanded_grad.astype(single), axis=0)
    contract_bias_grad = jnp.sum(grad_wide, axis=0)
    small_sums = lax.psum(
        (
            gain_one_grad, bias_one_grad, project_bias_grad, query_map_grad, key_map_grad,
            output_bias_grad, gain_two_grad, bias_two_grad, expand_bias_grad, contract_bias_grad,
        ),
        ("seq", "batch"),
    )
    return (
        block_output, input_grad, small_sums[0], small_sums[1], totals[0], small_sums[2],
        small_sums[3], small_sums[4], totals[1], small_sums[5], small_sums[6], small_sums[7],
        totals[2], small_sums[8], totals[3], small_sums[9],
    )


def solution(mesh):
    rows = P("batch", "seq", None)
    placed = (rows,) + (P(),) * 14 + (P("batch", None), rows)
    shard = P("seq", None)
    return jax.shard_map(
        per_device,
        mesh=mesh,
        in_specs=placed,
        out_specs=(
            rows, rows, P(), P(), shard, P(), P(), P(), shard, P(), P(), P(), shard, P(), shard, P(),
        ),
        check_vma=False,
    )
```

time: 1320 us -> 815 us (0.62)
  waiting for transfers between devices: 693 us -> 452 us
  Pallas kernels: 0 us -> 185 us
  blocking collectives: 224 us -> 41.8 us
  local copies, waits for them, and re-layouts: 129 us -> 21 us
  matrix products: 166 us -> 69.1 us
  other arithmetic: 81.8 us -> 28.5 us
    pallas_call x0 -> x6, Pallas kernels: none -> 185 us  [the longest x2 131 us: scan_states(): pl.pallas_call(partial(scan_kernel, reverse, count), out_shape=jax.ShapeD...]
    all_gather x2 -> x0, waiting for transfers between devices: 160 us -> none  [entering(): gathered = jax.tree.map(lambda a: lax.all_gather(a, axis), part)]
    all_gather x2 -> x0, blocking collectives: 159 us -> none  [entering(): gathered = jax.tree.map(lambda a: lax.all_gather(a, axis), part)]
    dot_general x25 -> x7, matrix products: 117 us -> 34.8 us  [the longest x1 10.5 us: per_device(): jnp.einsum('rf,rd->fd', hidden_low, grad_contract, preferred_element_type...]
    psum x1, waiting for transfers between devices: 73.4 us -> 0.01 us  [per_device(): lax.psum((gain_one_grad, bias_one_grad, project_bias_grad, query_map_grad...]
    psum x1, waiting for transfers between devices: 77 us -> 16.6 us  [per_device(): totals = lax.psum(shares, 'batch')]
    reduce_scatter x4, waiting for transfers between devices: 382 us -> 434 us  [scatter(): return lax.psum_scatter(value, 'seq', scatter_dimension=0, tiled=True)]
    add x15 -> x0, other arithmetic: 48.5 us -> none  [the longest x7 38.3 us: carry_combine(): later_part[0] + factor[:, None, None, None] * earlier_part[0]]
  transfers between devices with their start and end apart: 8 -> 6, of which waited for: 7 -> 4; matrix products, arithmetic and copies ran while one was open for 21% -> 7% of each run, Pallas kernels for 0% -> 15%
where the time goes in v1:
time: 815 us; the launch traced here: 813 us
  waiting for transfers between devices  452 us (55%)
  Pallas kernels  185 us (23%)
  matrix products  69.1 us (8%)
  blocking collectives  41.8 us (5%)
  other arithmetic  28.5 us (3%)
  local copies, waits for them, and re-layouts  21 us (3%)
  between operations  15.7 us (2%)
    reduce_scatter x4, waiting for transfers between devices, scatter(): return lax.psum_scatter(value, 'seq', scatter_dimension=0, tiled=True)  434 us
    pallas_call x2, Pallas kernels, scan_states(): pl.pallas_call(partial(scan_kernel, reverse, count), out_shape=jax.ShapeD...  131 us
    psum x1, blocking collectives, per_device(): lax.psum((gain_one_grad, bias_one_grad, project_bias_grad, query_map_grad...  41.8 us
    pallas_call x1, Pallas kernels, per_device(): pl.pallas_call(partial(backward_kernel, micro_count), grid=(head_count,),...  21.8 us
    psum x1, waiting for transfers between devices, per_device(): totals = lax.psum(shares, 'batch')  16.6 us
  transfers between devices with their start and end apart: 6, of which 4 were waited for; matrix products, arithmetic and copies ran while one was open for 7% of the time, Pallas kernels for 15%

profile of v1, /device:TPU:0, one launch (start us, length us, event | category | flops | bytes accessed | tf_op | source)
XLA Modules:
  0.0 812.9 jit_solution(8452827588430721775)
XLA Ops:
  8.6 1.0 slice_bitcast_fusion.1
  9.6 0.8 broadcast_compare_fusion
  10.4 1.3 convert_add_fusion
  11.7 1.3 fusion.32
  13.0 1.3 fusion.41
  14.3 1.3 compare_convert_fusion.3
  16.2 1.3 convert_reduce_fusion.2
  18.6 1.5 fusion.11
  24.1 1.3 stack.9
  25.4 1.4 broadcast_in_dim.8
  26.7 1.4 reshape.740
  28.1 0.8 pad_maximum_fusion
  29.0 1.3 convert_element_type.481.use_ref
  30.9 1.5 fusion.21
  32.4 3.6 fusion.8.q_ref.k_ref.v_ref
  36.0 10.6 %shard_map.288 = (bf16[1536,512]{1,0:T(8,128)(2,1)}, bf16[1536,512]{1,0:T(8,128)(2,1)}, f32[12,264,128]{2,1,0:T(8,128)}) custom-call(bf16[2304,512]{1,0:T(8,128)(2,1)} %fusion.8.q_ref.k_ref.v_ref, bf16[2304,512]{1,0:T(8,128)(2,1)} %fusion.8.q_ref.k_ref.v_ref, bf16[2304,512]{1,0:T(8,128)(2,1)} %fusion.8.q_ref.k_ref.v_ref, bf16[12,64,64]{2,1,0:T(8,128)(2,1)} %qm_ref.3, ...), custom_call_target="tpu_custom_call" | custom-call | tf_op jit(solution)/shard_map/pallas_call | solution.py:355
  46.6 1.1 broadcast_in_dim.9.mask_ref
  47.7 43.3 %shard_map.289.state_ref = f32[12,264,128]{2,1,0:T(8,128)} custom-call(f32[12,264,128]{2,1,0:T(8,128)} %get-tuple-element.27.local_ref, f32[5,264,128]{2,1,0:T(8,128)} %broadcast_in_dim.9.mask_ref), custom_call_target="tpu_custom_call" | custom-call | tf_op jit(solution)/shard_map/pallas_call | solution.py:259
  91.0 0.8 and_convert_fusion.mask_ref
  91.8 11.7 %shard_map.290 = (f32[768,512]{1,0:T(8,128)}, bf16[768,512]{1,0:T(8,128)(2,1)}, f32[12,1,512]{2,1,0:T(1,128)}) custom-call(bf16[1536,512]{1,0:T(8,128)(2,1)} %get-tuple-element.25.fq_ref, bf16[1536,512]{1,0:T(8,128)(2,1)} %get-tuple-element.26.fk_ref, bf16[2304,512]{1,0:T(8,128)(2,1)} %fusion.8.q_ref.k_ref.v_ref, f32[12,264,128]{2,1,0:T(8,128)} %shard_map.289.state_ref, ...), custom_call_target="tpu_custom_call" | custom-call | tf_op jit(solution)/shard_map/pallas_call | solution.py:364
  103.6 2.1 fusion.56
  106.5 5.5 fusion.48
  112.2 7.2 convert_reduce_fusion
  119.4 3.6 multiply_reduce_fusion
  123.0 1.2 convert_reduce_fusion.4
  124.2 1.1 copy-done.1
  125.4 2.2 fusion.42
  129.7 3.7 convolution_bitcast_fusion.grad_ref
  133.4 9.2 %shard_map.291.local_ref = f32[12,264,128]{2,1,0:T(8,128)} custom-call(f32[768,512]{1,0:T(8,128)} %convolution_bitcast_fusion.grad_ref, f32[768,512]{1,0:T(8,128)} %get-tuple-element.29.att_ref, f32[12,1,512]{2,1,0:T(1,128)} %get-tuple-element.30.den_ref, bf16[1536,512]{1,0:T(8,128)(2,1)} %get-tuple-element.25.fq_ref, f32[1,512]{1,0:T(1,128)} %bitcast.98), custom_call_target="tpu_custom_call" | custom-call | tf_op jit(solution)/shard_map/pallas_call | solution.py:413
  142.7 1.1 broadcast_in_dim.11.mask_ref
  143.7 88.1 %shard_map.292.out_grad_ref = f32[12,264,128]{2,1,0:T(8,128)} custom-call(f32[12,264,128]{2,1,0:T(8,128)} %shard_map.291.local_ref, f32[5,264,128]{2,1,0:T(8,128)} %broadcast_in_dim.11.mask_ref), custom_call_target="tpu_custom_call" | custom-call | tf_op jit(solution)/shard_map/pallas_call | solution.py:259
  231.9 21.8 %shard_map.293 = (bf16[3,768,512]{2,1,0:T(8,128)(2,1)}, f32[12,64,64]{2,1,0:T(8,128)}, f32[12,64,64]{2,1,0:T(8,128)}) custom-call(bf16[2304,512]{1,0:T(8,128)(2,1)} %fusion.8.q_ref.k_ref.v_ref, bf16[2304,512]{1,0:T(8,128)(2,1)} %fusion.8.q_ref.k_ref.v_ref, bf16[2304,512]{1,0:T(8,128)(2,1)} %fusion.8.q_ref.k_ref.v_ref, bf16[12,64,64]{2,1,0:T(8,128)(2,1)} %qm_ref.3, ...), custom_call_target="tpu_custom_call" | custom-call | tf_op jit(solution)/shard_map/pallas_call | solution.py:423
  254.1 6.6 fusion.57
  261.4 8.9 %fusion.47 = f32[768,3072]{1,0:T(8,128)} fusion(bf16[512,3072]{1,0:T(8,128)(2,1)} %copy-done.45, f32[512,768]{1,0:T(8,128)} %copy-done.5, f32[768]{0:T(1024)} %copy-done.36, f32[768]{0:T(1024)S(1)} %copy-done.26, f32[512]{0:T(512)S(1)} %copy-done.33, f32[512]{0:T(512)S(1)} %copy-done.24), kind=kOutput, calls=%fused_computation.108 | convolution fusion | flops 2417885184 | bytes 14166016 | tf_op jit(solution)/shard_map/rd,rf->df/dot_general | solution.py:460
  271.1 10.5 %fusion.49 = f32[3072,768]{1,0:T(8,128)} fusion(bf16[512,768]{1,0:T(8,128)(2,1)} %bitcast.94, f32[512,3072]{1,0:T(8,128)} %copy-done.44, f32[3072]{0:T(1024)S(1)} %copy-done.28), kind=kOutput, calls=%fused_computation.110 | convolution fusion | flops 2431647744 | bytes 16527360 | tf_op jit(solution)/shard_map/rf,rd->fd/dot_general | solution.py:462
  282.5 6.2 fusion.27
  289.6 99.7 %reduce-scatter.5.cloned.1.call-done = f32[96,2304]{1,0:T(8,128)} async-done(((f32[768,2304]{1,0:T(8,128)}), f32[96,2304]{1,0:T(8,128)}) %reduce-scatter.5.cloned.1.call-update) | async-done | bytes 884752 | tf_op jit(solution)/shard_map/reduce_scatter | solution.py:454
  389.3 168.6 %reduce-scatter.9.cloned.1.call-done = f32[96,3072]{1,0:T(8,128)} async-done(((f32[768,3072]{1,0:T(8,128)}), f32[96,3072]{1,0:T(8,128)}) %reduce-scatter.9.cloned.1.call-update) | async-done | bytes 1179664 | tf_op jit(solution)/shard_map/reduce_scatter | solution.py:454
  558.0 166.1 %reduce-scatter.11.cloned.1.call-done = f32[384,768]{1,0:T(8,128)} async-done(((f32[3072,768]{1,0:T(8,128)}), f32[384,768]{1,0:T(8,128)}) %reduce-scatter.11.cloned.1.call-update) | async-done | bytes 1179664 | tf_op jit(solution)/shard_map/reduce_scatter | solution.py:454
  724.1 1.9 convert_reduce_fusion.3
  727.2 41.8 %all-reduce = (f32[768]{0:T(1024)}, f32[768]{0:T(1024)}, f32[2304]{0:T(1024)}, f32[768]{0:T(1024)}, f32[768]{0:T(1024)}, /*index=5*/f32[768]{0:T(1024)}, f32[3072]{0:T(1024)}, f32[768]{0:T(1024)}) all-reduce(f32[768]{0:T(1024)} %get-tuple-element.36, f32[768]{0:T(1024)} %get-tuple-element.41, ...), channel_id=1, replica_groups=mesh['seq'=8,'batch'=4] {'seq','batch'}, use_global_device_ids=true, to_apply=%region_9.10 | all-reduce | flops 9984 | bytes 79872 | tf_op jit(solution)/shard_map/psum | solution.py:469
  769.8 3.8 fusion.26
  773.6 9.1 %add_convert_fusion = bf16[512,768]{1,0:T(8,128)(2,1)} fusion(f32[512,768]{1,0:T(8,128)S(1)} %copy-done.6, bf16[3072,768]{1,0:T(8,128)(2,1)} %param.30, f32[768]{0:T(1024)S(1)} %convert_element_type.488, f32[512,3072]{1,0:T(8,128)} %copy-done.44, f32[3072]{0:T(1024)S(1)} %copy-done.29), kind=kOutput, calls=%fused_computation.43 | convolution fusion | flops 2432827392 | bytes 13384704 | tf_op jit(solution)/shard_map/dot_general | solution.py:392
  782.7 16.6 %all-reduce.8.cloned.1.call-done = (f32[96,2304]{1,0:T(8,128)}, f32[96,768]{1,0:T(8,128)}, f32[96,3072]{1,0:T(8,128)}, f32[384,768]{1,0:T(8,128)}) async-done(((f32[96,2304]{1,0:T(8,128)}, f32[96,768]{1,0:T(8,128)}, f32[96,3072]{1,0:T(8,128)}, f32[384,768]{1,0:T(8,128)}), (f32[96,2304]{1,0:T(8,128)}, f32[96,768]{1,0:T(8,128)}, f32[96,3072]{1,0:T(8,128)}, f32[384,768]{1,0:T(8,128)})) %all-reduce.8.cloned.1.call-update) | async-done | bytes 3538960 | tf_op jit(solution)/shard_map/psum | solution.py:464
  799.3 2.3 copy.46
  802.3 0.7 copy.48
  803.8 1.0 copy.50
  804.8 1.0 copy.51
  (146 shorter events, 17.0 us)
Async XLA Ops:
  8.0 24.4 %copy-start = (bf16[768,2304]{1,0:T(8,128)(2,1)S(1)}, bf16[768,2304]{1,0:T(8,128)(2,1)}, u32[]{:S(2)}) copy-start(bf16[768,2304]{1,0:T(8,128)(2,1)} %param.20) | copy-start | bytes 10616836
  8.0 281.6 %reduce-scatter.7.cloned.1.call-start = ((), (), s32[]{:S(2)}) async-start(), calls=%async_computation.5 | async-start | bytes 2654208 | tf_op jit(solution)/shard_map/reduce_scatter | solution.py:454
  8.6 12.1 %copy-start.37 = (bf16[768]{0:T(1024)(128)(2,1)S(1)}, bf16[768]{0:T(1024)(128)(2,1)}, u32[]{:S(2)}) copy-start(bf16[768]{0:T(1024)(128)(2,1)} %param.18) | copy-start | bytes 4612
  8.6 12.7 %copy-start.38 = (bf16[768]{0:T(1024)(128)(2,1)S(1)}, bf16[768]{0:T(1024)(128)(2,1)}, u32[]{:S(2)}) copy-start(bf16[768]{0:T(1024)(128)(2,1)} %param.19) | copy-start | bytes 4612
  8.6 13.3 %copy-start.34 = (bf16[2304]{0:T(1024)(128)(2,1)S(1)}, bf16[2304]{0:T(1024)(128)(2,1)}, u32[]{:S(2)}) copy-start(bf16[2304]{0:T(1024)(128)(2,1)} %param.21) | copy-start | bytes 13828
  28.1 4.3 copy-start.30
  47.7 43.3 %copy-start.22 = (s32[4,128]{1,0:T(4,128)S(1)}, s32[4,128]{1,0:T(4,128)}, u32[]{:S(2)}) copy-start(s32[4,128]{1,0:T(4,128)} %convert_add_fusion) | copy-start | bytes 6148
  91.8 11.8 %copy-start.2 = (bf16[4,128,768]{2,1,0:T(8,128)(2,1)S(1)}, bf16[4,128,768]{2,1,0:T(8,128)(2,1)}, u32[]{:S(2)}) copy-start(bf16[4,128,768]{2,1,0:T(8,128)(2,1)} %param.17) | copy-start | bytes 2359300
  91.8 11.8 %copy-start.10 = (bf16[768,768]{1,0:T(8,128)(2,1)S(1)}, bf16[768,768]{1,0:T(8,128)(2,1)}, u32[]{:S(2)}) copy-start(bf16[768,768]{1,0:T(8,128)(2,1)} %param.24) | copy-start | bytes 3538948
  105.7 17.3 %copy-start.5 = (f32[512,768]{1,0:T(8,128)}, f32[512,768]{1,0:T(8,128)S(1)}, u32[]{:S(2)}) copy-start(f32[512,768]{1,0:T(8,128)S(1)} %get-tuple-element.84) | copy-start | bytes 4718596
  105.7 0.7 copy-start.40
  105.7 0.8 copy-start.35
  105.7 17.2 %copy-start.23 = (f32[512]{0:T(512)}, f32[512]{0:T(512)S(1)}, u32[]{:S(2)}) copy-start(f32[512]{0:T(512)S(1)} %broadcast_multiply_fusion.4) | copy-start | bytes 6148
  105.7 6.4 slice-start.2
  106.4 16.6 %copy-start.32 = (f32[512]{0:T(512)}, f32[512]{0:T(512)S(1)}, u32[]{:S(2)}) copy-start(f32[512]{0:T(512)S(1)} %add_rsqrt_fusion) | copy-start | bytes 6148
  106.4 16.5 %copy-start.25 = (f32[768]{0:T(1024)}, f32[768]{0:T(1024)S(1)}, u32[]{:S(2)}) copy-start(f32[768]{0:T(1024)S(1)} %convert_element_type.483) | copy-start | bytes 9220
  106.5 5.6 copy-start.36
  106.5 5.6 copy-start.27
  106.5 5.6 copy-start.7
  106.5 5.6 slice-start.3
  106.5 12.8 %slice-start = ((s8[4718592]{0:T(1024)(128)(4,1)}), s8[4194304]{0:T(1024)(128)(4,1)S(1)}, s32[]{:S(2)}) async-start(s8[4718592]{0:T(1024)(128)(4,1)} %bitcast.104), calls=%async_computation.10 | async-start | bytes 8388608
  112.1 7.3 copy-start.44
  112.1 7.2 slice-start.1
  119.4 3.6 copy-start.45
  123.0 2.4 copy-start.11
  124.2 1.2 copy-start.1
  127.6 261.8 %reduce-scatter.5.cloned.1.call-start = ((), (), s32[]{:S(2)}) async-start(), calls=%async_computation.4 | async-start | bytes 7962624 | tf_op jit(solution)/shard_map/reduce_scatter | solution.py:454
  133.4 9.2 %copy-start.17 = (f32[5,256]{1,0:T(8,128)S(1)}, f32[5,256]{1,0:T(8,128)}, u32[]{:S(2)}) copy-start(f32[5,256]{1,0:T(8,128)} %reshape.743) | copy-start | bytes 15364
  231.9 21.8 %copy-start.3 = (bf16[4,128,768]{2,1,0:T(8,128)(2,1)S(1)}, bf16[4,128,768]{2,1,0:T(8,128)(2,1)}, u32[]{:S(2)}) copy-start(bf16[4,128,768]{2,1,0:T(8,128)(2,1)} %param.17) | copy-start | bytes 2359300
  231.9 21.8 %copy-start.15 = (f32[768]{0:T(1024)S(1)}, f32[768]{0:T(1024)}, u32[]{:S(2)}) copy-start(f32[768]{0:T(1024)} %convert_element_type.456) | copy-start | bytes 9220
  231.9 21.8 %copy-start.16 = (f32[768]{0:T(1024)S(1)}, f32[768]{0:T(1024)}, u32[]{:S(2)}) copy-start(f32[768]{0:T(1024)} %convert_element_type.457) | copy-start | bytes 9220
  231.9 21.8 %copy-start.21 = (f32[4,128]{1,0:T(4,128)S(1)}, f32[4,128]{1,0:T(4,128)}, u32[]{:S(2)}) copy-start(f32[4,128]{1,0:T(4,128)} %copy-done.20) | copy-start | bytes 6148
  231.9 21.8 %copy-start.31 = (f32[4,128]{1,0:T(4,128)S(1)}, f32[4,128]{1,0:T(4,128)}, u32[]{:S(2)}) copy-start(f32[4,128]{1,0:T(4,128)} %get-tuple-element.68) | copy-start | bytes 6148
  260.8 297.2 %reduce-scatter.9.cloned.1.call-start = ((), (), s32[]{:S(2)}) async-start(), calls=%async_computation.6 | async-start | bytes 10616832 | tf_op jit(solution)/shard_map/reduce_scatter | solution.py:454
  270.4 0.7 copy-start.28
  270.4 453.7 %reduce-scatter.11.cloned.1.call-start = ((), (), s32[]{:S(2)}) async-start(), calls=%async_computation.7 | async-start | bytes 10616832 | tf_op jit(solution)/shard_map/reduce_scatter | solution.py:454
  281.6 0.9 copy-start.18
  281.6 0.9 copy-start.19
  281.6 501.1 %all-reduce.6.cloned.1.call-start = ((), (), s32[]{:S(2)}) async-start(), calls=%async_computation.8 | async-start | bytes 1572864 | tf_op jit(solution)/shard_map/psum | solution.py:469
  282.2 517.1 %all-reduce.8.cloned.1.call-start = ((), (), s32[]{:S(2)}) async-start(), calls=%async_computation.9 | async-start | bytes 7077888 | tf_op jit(solution)/shard_map/psum | solution.py:464
  282.5 6.2 copy-start.4
  769.7 3.8 copy-start.6
  769.7 3.8 copy-start.29
  799.2 2.3 copy-start.13
  799.2 3.0 copy-start.12
  799.3 3.8 copy-start.14
  799.3 4.5 copy-start.9
  803.0 1.7 copy-start.8
  (8 other events, 5.2 us)
Sparse Core Ops, SparseCore 0:
  127.7 96.1 reduce-scatter.6
  260.9 128.3 reduce-scatter.4
  392.9 165.0 reduce-scatter.8
  561.4 162.5 reduce-scatter.10
Sparse Core Ops, SparseCore 1:
  288.0 223.2 all-reduce.5
  724.2 75.0 all-reduce.7

commit v2 on v1

--- a/solution.py
+++ b/solution.py
@@ -12,6 +12,7 @@
 single = jnp.float32
 MESH = pl.DeviceIdType.MESH
 VMEM_LIMIT = 56 * 1024 * 1024
+REDUCE_LIMIT = 60 * 1024 * 1024
 
 
 def matmul(a, b, contract):
@@ -269,6 +270,333 @@
     )(local, masks)
 
 
+def reduce_kernel(count, lines, plans, sources, *refs):
+    direct, halved = plans
+    total = direct + halved
+    arrays = len({s[0] for s in sources})
+    inputs, outputs = (refs[:arrays], refs[arrays : 2 * arrays])
+    refs = refs[2 * arrays :]
+    out, own, got, y_got, zr_got, zl_got, x_got = refs[:7]
+    hx_got, hy_got, hzr_got, hzl_got = refs[7:11]
+    sems = refs[11:]
+    own_sem, core_send, core_recv, y_send, y_recv, zr_send, zr_recv, zl_send, zl_recv = sems[:9]
+    x_send, x_recv, hx_send, hx_recv, back_send, back_recv = sems[9:]
+    length = count // 2
+    rows, wide = out.shape[1:]
+    half = wide // 2
+    part = rows // lines
+    place, column = (lax.axis_index("seq"), lax.axis_index("batch"))
+    high, low = (place // 2, lax.rem(place, 2))
+    across, core = (column // 2, lax.rem(column, 2))
+    mine = pl.ds(pl.multiple_of(core * half, 128), half)
+    strip = pl.ds(pl.multiple_of(across * part, 8), part)
+    at_core = (place, column + 1 - 2 * core)
+    at_y = (place + 1 - 2 * low, column)
+    at_right, at_left = ((place + 2, column), (place - 2, column))
+    not_first, not_last = (high > 0, high < length - 1)
+
+    def line(d):
+        other = lax.rem(across + d, lines)
+        return other, (place, other * 2 + core)
+
+    def remote(src, dst, send, recv, device):
+        return pltpu.make_async_remote_copy(
+            src_ref=src, dst_ref=dst, send_sem=send, recv_sem=recv, device_id=device, device_id_type=MESH
+        )
+
+    barrier = pltpu.get_barrier_semaphore()
+    for device in [at_core, at_y] + [line(d)[1] for d in range(1, lines)]:
+        pl.semaphore_signal(barrier, inc=1, device_id=device, device_id_type=MESH)
+
+    @pl.when(not_last)
+    def _():
+        pl.semaphore_signal(barrier, inc=1, device_id=at_right, device_id_type=MESH)
+
+    @pl.when(not_first)
+    def _():
+        pl.semaphore_signal(barrier, inc=1, device_id=at_left, device_id_type=MESH)
+
+    pl.semaphore_wait(barrier, 1 + lines + jnp.where(not_first, 1, 0) + jnp.where(not_last, 1, 0))
+
+    def source(u, column_half):
+        array, lead, row, col = sources[u]
+        window = (pl.ds(row, rows), pl.ds(pl.multiple_of(col + column_half * half, 128), half))
+        if lead is None:
+            return inputs[array].at[(slice(None), slice(None)) + window]
+        return inputs[array].at[(slice(None), slice(None), lead) + window]
+
+    def load(u):
+        return pltpu.make_async_copy(source(u, core), own.at[u], own_sem.at[u])
+
+    def give(u):
+        return remote(source(u, 1 - core), got.at[u], core_send.at[u], core_recv.at[u], at_core)
+
+    for u in range(total):
+        give(u).start()
+        load(u).start()
+
+    def settle(u):
+        pltpu.make_async_copy(own.at[u], own.at[u], own_sem.at[u]).wait()
+        remote(own.at[u], got.at[u], core_send.at[u], core_recv.at[u], at_core).wait_recv()
+        own[u] = own[u] + got[u]
+
+    def give_back(u):
+        block = out.at[u, :, mine]
+        return remote(block, block, back_send.at[u], back_recv.at[u], at_core)
+
+    class Grid:
+        def __init__(self, base, window, y, zr, zl):
+            self.base, self.window, self.y, self.zr, self.zl = base, window, y, zr, zl
+
+        def block(self, i, h, l):
+            return own.at[(self.base + i, h, l) + self.window]
+
+        def y_copy(self, i):
+            return remote(
+                own.at[(self.base + i, slice(None), 1 - low) + self.window], self.y.at[i],
+                y_send.at[self.base + i], y_recv.at[self.base + i], at_y,
+            )
+
+        def right(self, i, k):
+            return remote(
+                self.block(i, k, low), self.zr.at[i, k], zr_send.at[self.base + i, k],
+                zr_recv.at[self.base + i, k], at_right,
+            )
+
+        def left(self, i, k):
+            return remote(
+                self.block(i, k, low), self.zl.at[i, k], zl_send.at[self.base + i, k],
+                zl_recv.at[self.base + i, k], at_left,
+            )
+
+        def from_y(self, i):
+            self.y_copy(i).wait_recv()
+            target = own.at[(self.base + i, slice(None), low) + self.window]
+            target[...] = target[...] + self.y[i]
+            self.z_step(i, 1)
+
+        def take_right(self, i, k):
+            self.right(i, k).wait_recv()
+            target = self.block(i, k, low)
+            target[...] = target[...] + self.zr[i, k]
+
+        def take_left(self, i, k):
+            self.left(i, k).wait_recv()
+            target = self.block(i, k, low)
+            target[...] = target[...] + self.zl[i, k]
+
+        def z_step(self, i, t):
+            k = high + length - t
+
+            @pl.when(high <= t - 1)
+            def _():
+                if t > 1:
+                    @pl.when(not_first)
+                    def _():
+                        self.take_right(i, k)
+
+                self.right(i, k).start()
+
+            j = high - length + t
+
+            @pl.when(high >= length - t)
+            def _():
+                if t > 1:
+                    @pl.when(not_last)
+                    def _():
+                        self.take_left(i, j)
+
+                self.left(i, j).start()
+
+        def z_end(self, i):
+            @pl.when(not_first)
+            def _():
+                self.take_right(i, high)
+
+            @pl.when(not_last)
+            def _():
+                self.take_left(i, high)
+
+        def drain(self, i):
+            self.y_copy(i).wait_send()
+
+            def right_one(k, _):
+                self.right(i, k).wait_send()
+                return 0
+
+            def left_one(k, _):
+                self.left(i, k).wait_send()
+                return 0
+
+            lax.fori_loop(high + 1, length, right_one, 0)
+            lax.fori_loop(0, high, left_one, 0)
+
+    full = Grid(0, (), y_got, zr_got, zl_got)
+    thin = Grid(direct, (strip,), hy_got, hzr_got, hzl_got)
+
+    def x_copy(i, d):
+        return remote(
+            full.block(i, high, low), x_got.at[i, d - 1], x_send.at[i, d - 1], x_recv.at[i, d - 1], line(d)[1]
+        )
+
+    def direct_first(i):
+        settle(i)
+        full.y_copy(i).start()
+
+    def direct_reduced(i):
+        full.z_end(i)
+        for d in range(1, lines):
+            x_copy(i, d).start()
+
+    def direct_done(i):
+        for d in range(1, lines):
+            x_copy(i, d).wait_recv()
+        value = full.block(i, high, low)[...]
+        if lines == 2:
+            value = value + x_got[i, 0]
+        else:
+            parts = []
+            for x in range(lines):
+                slot = lax.rem(across - x + lines - 1, lines)
+                parts.append(jnp.where(x == across, value, x_got[i, jnp.minimum(slot, lines - 2)]))
+            value = sum(parts[1:], parts[0])
+        out[i, :, mine] = value
+        give_back(i).start()
+
+    def strip_copy(i, d):
+        other, device = line(d)
+        theirs = pl.ds(pl.multiple_of(other * part, 8), part)
+        return remote(
+            own.at[direct + i, :, :, theirs], hx_got.at[i, d - 1], hx_send.at[i, 0, d - 1],
+            hx_recv.at[i, 0, d - 1], device,
+        )
+
+    def strip_back(i, d):
+        block = out.at[direct + i, strip, mine]
+        return remote(block, block, hx_send.at[i, 1, d - 1], hx_recv.at[i, 1, d - 1], line(d)[1])
+
+    def halved_first(i):
+        settle(direct + i)
+        for d in range(1, lines):
+            strip_copy(i, d).start()
+
+    def halved_next(i):
+        for d in range(1, lines):
+            strip_copy(i, d).wait_recv()
+            target = own.at[direct + i, :, :, strip]
+            target[...] = target[...] + hx_got[i, d - 1]
+        thin.y_copy(i).start()
+
+    def halved_reduced(i):
+        thin.z_end(i)
+        out[direct + i, strip, mine] = thin.block(i, high, low)[...]
+        for d in range(1, lines):
+            strip_back(i, d).start()
+
+    def halved_done(i):
+        for d in range(1, lines):
+            strip_back(i, d).wait_recv()
+        give_back(direct + i).start()
+
+    def z_steps(grid):
+        return [partial(grid.z_step, t=t) for t in range(2, length)]
+
+    stages = []
+    if direct:
+        steps = [direct_first, full.from_y] + z_steps(full) + [direct_reduced, direct_done]
+        stages += [(s, f, direct) for s, f in enumerate(steps)]
+    if halved:
+        steps = [halved_first, halved_next, thin.from_y] + z_steps(thin) + [halved_reduced, halved_done]
+        stages += [(s, f, halved) for s, f in enumerate(steps)]
+    stages.sort(key=lambda s: -s[0])
+    rounds = max(direct, halved) + stages[0][0]
+
+    def one_round(r, _):
+        for lag, step, size in stages:
+            @pl.when((r >= lag) & (r < lag + size))
+            def _(lag=lag, step=step):
+                step(r - lag)
+
+        return 0
+
+    lax.fori_loop(0, rounds, one_round, 0)
+
+    def finish(u, _):
+        remote(own.at[u], got.at[u], core_send.at[u], core_recv.at[u], at_core).wait_send()
+        give_back(u).wait()
+        return 0
+
+    lax.fori_loop(0, total, finish, 0)
+
+    def store(u):
+        array, lead, row, col = sources[u]
+        window = (pl.ds(row, rows), pl.ds(col, wide))
+        window = window if lead is None else (lead,) + window
+        return pltpu.make_async_copy(out.at[u], outputs[array].at[window], own_sem.at[u])
+
+    for u in range(total):
+        store(u).start()
+
+    def drain_direct(i, _):
+        full.drain(i)
+        for d in range(1, lines):
+            x_copy(i, d).wait_send()
+        return 0
+
+    def drain_halved(i, _):
+        thin.drain(i)
+        for d in range(1, lines):
+            strip_copy(i, d).wait_send()
+            strip_back(i, d).wait_send()
+        return 0
+
+    if direct:
+        lax.fori_loop(0, direct, drain_direct, 0)
+    if halved:
+        lax.fori_loop(0, halved, drain_halved, 0)
+    for u in range(total):
+        store(u).wait()
+
+
+def reduce_all(arrays, sources, plans, rows, count, lines, identity):
+    direct, halved = plans
+    total = direct + halved
+    length = count // 2
+    wide = 768
+    half = wide // 2
+    part = max(rows // lines, 8)
+    spare = max(halved, 1)
+    DMA = pltpu.SemaphoreType.DMA
+    others = max(lines - 1, 1)
+    return pl.pallas_call(
+        partial(reduce_kernel, count, lines, plans, sources),
+        out_shape=[jax.ShapeDtypeStruct(a.shape[2:], single) for a in arrays],
+        in_specs=[pl.BlockSpec(memory_space=pl.ANY)] * len(arrays),
+        out_specs=[pl.BlockSpec(memory_space=pl.ANY)] * len(arrays),
+        scratch_shapes=[
+            pltpu.VMEM((total, rows, wide), single),
+            pltpu.VMEM((total, length, 2, rows, half), single),
+            pltpu.VMEM((total, length, 2, rows, half), single),
+            pltpu.VMEM((max(direct, 1), length, rows, half), single),
+            pltpu.VMEM((max(direct, 1), length, rows, half), single),
+            pltpu.VMEM((max(direct, 1), length, rows, half), single),
+            pltpu.VMEM((max(direct, 1), others, rows, half), single),
+            pltpu.VMEM((spare, others, length, 2, part, half), single),
+            pltpu.VMEM((spare, length, part, half), single),
+            pltpu.VMEM((spare, length, part, half), single),
+            pltpu.VMEM((spare, length, part, half), single),
+            DMA((total,)), DMA((total,)), DMA((total,)), DMA((total,)), DMA((total,)),
+            DMA((total, length)), DMA((total, length)), DMA((total, length)), DMA((total, length)),
+            DMA((max(direct, 1), others)), DMA((max(direct, 1), others)),
+            DMA((spare, 2, others)), DMA((spare, 2, others)),
+            DMA((total,)), DMA((total,)),
+        ],
+        compiler_params=pltpu.CompilerParams(
+            collective_id=identity, has_side_effects=True, vmem_limit_bytes=REDUCE_LIMIT
+        ),
+    )(*arrays)
+
+
 def scan_masks(bounds, first_row, row_count, place, micro_count, head_width, reverse):
     def doc(position):
         return doc_number(position, bounds[:, 0], bounds[:, 1])
@@ -450,18 +778,31 @@
         (middle_grad + input_norm_grad).astype(bfloat).reshape(micro_count, row_count, model_width)
     )
 
-    def scatter(value):
-        return lax.psum_scatter(value, "seq", scatter_dimension=0, tiled=True)
-
-    shares = (
-        scatter(jnp.einsum("rd,cr->dc", normed_low, projected_grad, preferred_element_type=single)),
-        scatter(jnp.einsum("er,rd->ed", attended_low, branch_low, preferred_element_type=single)),
-        scatter(
-            jnp.einsum("rd,rf->df", normed_two_low, expanded_grad, preferred_element_type=single)
+    lines = lax.axis_size("batch") // 2
+    share = model_width // count
+    rows = share // 2 if share // 2 % (8 * lines) == 0 else share
+    tiles = (count // 2, 2)
+    arrays = [
+        jnp.einsum("rf,rd->fd", hidden_low, grad_contract, preferred_element_type=single).reshape(
+            tiles + (expand_weight.shape[1] // model_width, share, model_width)
         ),
-        scatter(jnp.einsum("rf,rd->fd", hidden_low, grad_contract, preferred_element_type=single)),
-    )
-    totals = lax.psum(shares, "batch")
+        jnp.einsum("rd,rf->df", normed_two_low, expanded_grad, preferred_element_type=single),
+        jnp.einsum("er,rd->ed", attended_low, branch_low, preferred_element_type=single),
+        jnp.einsum("rd,cr->dc", normed_low, projected_grad, preferred_element_type=single),
+    ]
+    arrays[1:] = [a.reshape(tiles + (share, a.shape[1])) for a in arrays[1:]]
+    units = [(0, u, 0) for u in range(arrays[0].shape[2])]
+    for a in (1, 2, 3):
+        units += [(a, None, c) for c in range(0, arrays[a].shape[3], model_width)]
+    chunks = [(a, lead, row, col) for a, lead, col in units for row in range(0, share, rows)]
+    if rows % (8 * lines) == 0:
+        direct, halved = (chunks[0::2], chunks[1::2])
+    else:
+        direct, halved = (chunks, [])
+    totals = reduce_all(
+        arrays, direct + halved, (len(direct), len(halved)), rows, count, lines, 3
+    )
+    totals = [totals[3], totals[2], totals[1], totals[0].reshape(-1, model_width)]
     project_bias_grad = jnp.sum(projected_grad.astype(single), axis=1)
     output_bias_grad = jnp.sum(branch_low.astype(single), axis=0)
     expand_bias_grad = jnp.sum(expanded_grad.astype(single), axis=0)

time: 815 us -> 504 us (0.62)
  waiting for transfers between devices: 452 us -> 0.02 us
  Pallas kernels: 185 us -> 326 us
    reduce_scatter x4 -> x0, waiting for transfers between devices: 434 us -> none  [scatter(): return lax.psum_scatter(value, 'seq', scatter_dimension=0, tiled=True)]
    pallas_call x0 -> x1, Pallas kernels: none -> 162 us  [reduce_all(): pl.pallas_call(partial(reduce_kernel, count, lines, plans, sources), out_...]
    pallas_call x2, Pallas kernels: 131 us -> 110 us  [scan_states(): pl.pallas_call(partial(scan_kernel, reverse, count), out_shape=jax.ShapeD...]
    psum x1 -> x0, waiting for transfers between devices: 16.6 us -> none  [per_device(): totals = lax.psum(shares, 'batch')]
  transfers between devices with their start and end apart: 6 -> 1, of which waited for: 4 -> 0; matrix products, arithmetic and copies ran while one was open for 7% -> 10% of each run, Pallas kernels for 15% -> 32%
where the time goes in v2:
time: 504 us; the launch traced here: 502 us
  Pallas kernels  326 us (65%)
  matrix products  62.8 us (12%)
  blocking collectives  41.7 us (8%)
  other arithmetic  29.8 us (6%)
  local copies, waits for them, and re-layouts  27.7 us (5%)
  between operations  14.4 us (3%)
    pallas_call x1, Pallas kernels, reduce_all(): pl.pallas_call(partial(reduce_kernel, count, lines, plans, sources), out_...  162 us
    pallas_call x2, Pallas kernels, scan_states(): pl.pallas_call(partial(scan_kernel, reverse, count), out_shape=jax.ShapeD...  110 us
    psum x1, blocking collectives, per_device(): lax.psum((gain_one_grad, bias_one_grad, project_bias_grad, query_map_grad...  41.7 us
    pallas_call x1, Pallas kernels, per_device(): pl.pallas_call(partial(backward_kernel, micro_count), grid=(head_count,),...  21.7 us
    pallas_call x1, Pallas kernels, per_device(): pl.pallas_call(partial(attend_kernel, micro_count), grid=(head_count,), i...  11.7 us
    pallas_call x1, Pallas kernels, per_device(): pl.pallas_call(partial(feature_kernel, micro_count), grid=(head_count,),...  10.6 us
  transfers between devices with their start and end apart: 1, of which 0 were waited for; matrix products, arithmetic and copies ran while one was open for 10% of the time, Pallas kernels for 32%

profile of v2, /device:TPU:0, one launch (start us, length us, event | category | flops | bytes accessed | tf_op | source)
XLA Modules:
  0.0 502.3 jit_solution(11487258089276568085)
XLA Ops:
  7.8 1.0 slice_bitcast_fusion.1
  8.8 1.3 fusion.37
  10.0 1.3 fusion.46
  12.3 0.8 broadcast_compare_fusion
  13.2 1.3 convert_add_fusion
  16.9 1.3 convert_reduce_fusion.2
  18.7 1.5 fusion.19
  24.3 1.3 stack.9
  25.6 1.4 broadcast_in_dim.8
  27.0 1.4 reshape.734
  28.4 1.4 pad_maximum_fusion
  30.3 1.3 stack.11
  31.6 1.4 broadcast_in_dim.10
  33.0 1.4 reshape.737
  34.4 0.8 pad_maximum_fusion.1
  36.6 1.6 and_convert_fusion.mask_ref
  38.2 1.5 fusion.26
  39.7 3.6 fusion.16.q_ref.k_ref.v_ref
  43.3 10.6 %shard_map.288 = (bf16[1536,512]{1,0:T(8,128)(2,1)}, bf16[1536,512]{1,0:T(8,128)(2,1)}, f32[12,264,128]{2,1,0:T(8,128)}) custom-call(bf16[2304,512]{1,0:T(8,128)(2,1)} %fusion.16.q_ref.k_ref.v_ref, bf16[2304,512]{1,0:T(8,128)(2,1)} %fusion.16.q_ref.k_ref.v_ref, bf16[2304,512]{1,0:T(8,128)(2,1)} %fusion.16.q_ref.k_ref.v_ref, bf16[12,64,64]{2,1,0:T(8,128)(2,1)} %qm_ref.3, ...), custom_call_target="tpu_custom_call" | custom-call | tf_op jit(solution)/shard_map/pallas_call | solution.py:683
  53.9 1.1 broadcast_in_dim.9.mask_ref
  55.0 43.3 %shard_map.289.state_ref = f32[12,264,128]{2,1,0:T(8,128)} custom-call(f32[12,264,128]{2,1,0:T(8,128)} %get-tuple-element.31.local_ref, f32[5,264,128]{2,1,0:T(8,128)} %broadcast_in_dim.9.mask_ref), custom_call_target="tpu_custom_call" | custom-call | tf_op jit(solution)/shard_map/pallas_call | solution.py:260
  98.4 11.7 %shard_map.290 = (f32[768,512]{1,0:T(8,128)}, bf16[768,512]{1,0:T(8,128)(2,1)}, f32[12,1,512]{2,1,0:T(1,128)}) custom-call(bf16[1536,512]{1,0:T(8,128)(2,1)} %get-tuple-element.29.fq_ref, bf16[1536,512]{1,0:T(8,128)(2,1)} %get-tuple-element.30.fk_ref, bf16[2304,512]{1,0:T(8,128)(2,1)} %fusion.16.q_ref.k_ref.v_ref, f32[12,264,128]{2,1,0:T(8,128)} %shard_map.289.state_ref, ...), custom_call_target="tpu_custom_call" | custom-call | tf_op jit(solution)/shard_map/pallas_call | solution.py:692
  110.2 2.1 fusion.63
  112.7 8.9 %fusion.14 = (bf16[3072,512]{0,1:T(8,128)(2,1)}, f32[512,3072]{1,0:T(8,128)S(1)}) fusion(f32[3072]{0:T(1024)S(1)} %convert_element_type.483, bf16[768,3072]{1,0:T(8,128)(2,1)} %param.28, f32[512,768]{1,0:T(8,128)S(1)} %get-tuple-element.86, f32[768]{0:T(1024)S(1)} %copy-done.25, f32[768]{0:T(1024)S(1)} %copy-done.22, f32[512]{0:T(512)S(1)} %add_rsqrt_fusion, ...), kind=kOutput, calls=%fused_computation.17 | convolution fusion | flops 2433613824 | bytes 15751168 | tf_op jit(solution)/shard_map/dot_general | solution.py:713
  121.6 7.2 %convert_reduce_fusion = (f32[3072]{0:T(1024)}, bf16[512,3072]{1,0:T(8,128)(2,1)S(1)}) fusion(f32[512,3072]{1,0:T(8,128)S(1)} %get-tuple-element.90, f32[3072]{0:T(1024)S(1)} %convert_element_type.483, bf16[512,768]{1,0:T(8,128)(2,1)S(1)} %bitcast.114, bf16[3072,768]{1,0:T(8,128)(2,1)S(1)} %bitcast.128), kind=kOutput, calls=%fused_computation.18 | convolution fusion | flops 2452091904 | bytes 14966784 | tf_op jit(solution)/shard_map/rd,fd->rf/dot_general | solution.py:726
  128.8 3.6 multiply_reduce_fusion
  132.4 1.2 convert_reduce_fusion.4
  133.6 2.0 convolution_bitcast_fusion.grad_ref
  135.6 9.2 %shard_map.291.local_ref = f32[12,264,128]{2,1,0:T(8,128)} custom-call(f32[768,512]{1,0:T(8,128)} %convolution_bitcast_fusion.grad_ref, f32[768,512]{1,0:T(8,128)} %get-tuple-element.33.att_ref, f32[12,1,512]{2,1,0:T(1,128)} %get-tuple-element.34.den_ref, bf16[1536,512]{1,0:T(8,128)(2,1)} %get-tuple-element.29.fq_ref, f32[1,512]{1,0:T(1,128)} %bitcast.119), custom_call_target="tpu_custom_call" | custom-call | tf_op jit(solution)/shard_map/pallas_call | solution.py:741
  144.8 1.1 broadcast_in_dim.11.mask_ref
  145.8 66.9 %shard_map.292.out_grad_ref = f32[12,264,128]{2,1,0:T(8,128)} custom-call(f32[12,264,128]{2,1,0:T(8,128)} %shard_map.291.local_ref, f32[5,264,128]{2,1,0:T(8,128)} %broadcast_in_dim.11.mask_ref), custom_call_target="tpu_custom_call" | custom-call | tf_op jit(solution)/shard_map/pallas_call | solution.py:260
  212.8 21.7 %shard_map.293 = (bf16[3,768,512]{2,1,0:T(8,128)(2,1)}, f32[12,64,64]{2,1,0:T(8,128)}, f32[12,64,64]{2,1,0:T(8,128)}) custom-call(bf16[2304,512]{1,0:T(8,128)(2,1)} %fusion.16.q_ref.k_ref.v_ref, bf16[2304,512]{1,0:T(8,128)(2,1)} %fusion.16.q_ref.k_ref.v_ref, bf16[2304,512]{1,0:T(8,128)(2,1)} %fusion.16.q_ref.k_ref.v_ref, bf16[12,64,64]{2,1,0:T(8,128)(2,1)} %qm_ref.3, ...), custom_call_target="tpu_custom_call" | custom-call | tf_op jit(solution)/shard_map/pallas_call | solution.py:751
  234.6 1.9 convert_reduce_fusion.3
  236.4 4.1 fusion.47
  240.5 5.6 %fusion.55 = f32[768,3072]{1,0:T(8,128)} fusion(bf16[512,3072]{1,0:T(8,128)(2,1)S(1)} %copy-done.34, f32[512,768]{1,0:T(8,128)S(1)} %copy-done.6, f32[768]{0:T(1024)S(1)} %copy-done.25, f32[768]{0:T(1024)S(1)} %copy-done.22, f32[512]{0:T(512)S(1)} %add_rsqrt_fusion, f32[512]{0:T(512)S(1)} %broadcast_multiply_fusion.4), kind=kOutput, calls=%fused_computation.117 | convolution fusion | flops 2417885184 | bytes 14166016 | tf_op jit(solution)/shard_map/rd,rf->df/dot_general | solution.py:789
  246.2 2.3 copy.40
  248.5 4.7 copy.39
  253.2 9.7 %add_convert_fusion = bf16[512,768]{1,0:T(8,128)(2,1)} fusion(f32[512,768]{1,0:T(8,128)} %copy-done.5, bf16[3072,768]{1,0:T(8,128)(2,1)} %param.30, f32[512,3072]{1,0:T(8,128)} %copy-done.35, f32[3072]{0:T(1024)S(1)} %copy-done.24, f32[768]{0:T(1024)S(1)} %convert_element_type.485), kind=kOutput, calls=%fused_computation.49 | convolution fusion | flops 2432827392 | bytes 13384704 | tf_op jit(solution)/shard_map/dot_general | solution.py:720
  263.8 6.2 %fusion.32 = (f32[768]{0:T(1024)}, f32[512]{0:T(512)S(1)}, f32[512]{0:T(512)S(1)}, f32[768]{0:T(1024)}, f32[512,768]{1,0:T(8,128)}) fusion(bf16[4,128,768]{2,1,0:T(8,128)(2,1)} %param.17, f32[512]{0:T(512)} %rsqrt_bitcast_fusion, f32[512]{0:T(512)} %get-tuple-element.72, f32[768]{0:T(1024)S(1)} %copy-done.20, bf16[2304,512]{1,0:T(8,128)(2,1)} %bitcast.109, ...), kind=kOutput, calls=%fused_computation.43 | convolution fusion | flops 1815868928 | bytes 8274944 | tf_op jit(solution)/shard_map/cr,dc->rd/dot_general | solution.py:771
  271.2 5.0 fusion.65.refs_3_
  276.2 5.0 fusion.64.refs_0_
  281.2 162.4 %shard_map.294 = (f32[4,96,768]{2,1,0:T(8,128)}, f32[96,3072]{1,0:T(8,128)}, f32[96,768]{1,0:T(8,128)}, f32[96,2304]{1,0:T(8,128)}) custom-call(f32[4,2,4,96,768]{4,3,2,1,0:T(8,128)} %fusion.64.refs_0_, f32[4,2,96,3072]{3,2,1,0:T(8,128)} %bitcast.108, f32[4,2,96,768]{3,2,1,0:T(8,128)} %bitcast.107, f32[4,2,96,2304]{3,2,1,0:T(8,128)} %fusion.65.refs_3_), custom_call_target="tpu_custom_call" | custom-call | tf_op jit(solution)/shard_map/pallas_call | solution.py:571
  443.6 41.7 %all-reduce = (f32[768]{0:T(1024)}, f32[768]{0:T(1024)}, f32[2304]{0:T(1024)}, f32[768]{0:T(1024)}, f32[768]{0:T(1024)}, /*index=5*/f32[768]{0:T(1024)}, f32[3072]{0:T(1024)}, f32[768]{0:T(1024)}) all-reduce(f32[768]{0:T(1024)} %get-tuple-element.44, f32[768]{0:T(1024)} %get-tuple-element.49, ...), channel_id=1, replica_groups=mesh['seq'=8,'batch'=4] {'seq','batch'}, use_global_device_ids=true, to_apply=%region_9.10 | all-reduce | flops 9984 | bytes 79872 | tf_op jit(solution)/shard_map/psum | solution.py:810
  485.3 3.6 fusion.31
  488.9 2.3 copy.54
  491.2 0.7 copy.55
  493.4 1.0 copy.58
  494.4 1.0 copy.59
  (113 shorter events, 14.7 us)
Async XLA Ops:
  7.2 32.5 %copy-start = (bf16[768,2304]{1,0:T(8,128)(2,1)S(1)}, bf16[768,2304]{1,0:T(8,128)(2,1)}, u32[]{:S(2)}) copy-start(bf16[768,2304]{1,0:T(8,128)(2,1)} %param.20) | copy-start | bytes 10616836
  7.2 481.7 %all-reduce.4.cloned.1.call-start = ((), (), s32[]{:S(2)}) async-start(), calls=%async_computation | async-start | bytes 1572864 | tf_op jit(solution)/shard_map/psum | solution.py:810
  7.8 13.0 %copy-start.27 = (bf16[768]{0:T(1024)(128)(2,1)S(1)}, bf16[768]{0:T(1024)(128)(2,1)}, u32[]{:S(2)}) copy-start(bf16[768]{0:T(1024)(128)(2,1)} %param.26) | copy-start | bytes 4612
  7.8 13.6 %copy-start.28 = (bf16[768]{0:T(1024)(128)(2,1)S(1)}, bf16[768]{0:T(1024)(128)(2,1)}, u32[]{:S(2)}) copy-start(bf16[768]{0:T(1024)(128)(2,1)} %param.18) | copy-start | bytes 4612
  7.8 14.2 %copy-start.29 = (bf16[768]{0:T(1024)(128)(2,1)S(1)}, bf16[768]{0:T(1024)(128)(2,1)}, u32[]{:S(2)}) copy-start(bf16[768]{0:T(1024)(128)(2,1)} %param.27) | copy-start | bytes 4612
  7.8 14.8 %copy-start.30 = (bf16[768]{0:T(1024)(128)(2,1)S(1)}, bf16[768]{0:T(1024)(128)(2,1)}, u32[]{:S(2)}) copy-start(bf16[768]{0:T(1024)(128)(2,1)} %param.19) | copy-start | bytes 4612
  7.8 15.4 %copy-start.31 = (bf16[768]{0:T(1024)(128)(2,1)S(1)}, bf16[768]{0:T(1024)(128)(2,1)}, u32[]{:S(2)}) copy-start(bf16[768]{0:T(1024)(128)(2,1)} %param.25) | copy-start | bytes 4612
  15.2 0.5 copy-start.21
  35.9 85.6 %copy-start.23 = (f32[3072]{0:T(1024)}, f32[3072]{0:T(1024)S(1)}, u32[]{:S(2)}) copy-start(f32[3072]{0:T(1024)S(1)} %convert_element_type.483) | copy-start | bytes 36868
  39.7 3.6 copy-start.9
  43.3 10.6 %copy-start.19 = (f32[5,264]{1,0:T(8,128)S(1)}, f32[5,264]{1,0:T(8,128)}, u32[]{:S(2)}) copy-start(f32[5,264]{1,0:T(8,128)} %pad_maximum_fusion) | copy-start | bytes 15844
  98.3 11.8 %copy-start.2 = (bf16[4,128,768]{2,1,0:T(8,128)(2,1)S(1)}, bf16[4,128,768]{2,1,0:T(8,128)(2,1)}, u32[]{:S(2)}) copy-start(bf16[4,128,768]{2,1,0:T(8,128)(2,1)} %param.17) | copy-start | bytes 2359300
  98.4 11.8 %copy-start.14 = (bf16[768,768]{1,0:T(8,128)(2,1)S(1)}, bf16[768,768]{1,0:T(8,128)(2,1)}, u32[]{:S(2)}) copy-start(bf16[768,768]{1,0:T(8,128)(2,1)} %param.24) | copy-start | bytes 3538948
  98.4 11.8 %copy-start.26 = (f32[768]{0:T(1024)S(1)}, f32[768]{0:T(1024)}, u32[]{:S(2)}) copy-start(f32[768]{0:T(1024)} %convert_element_type.479) | copy-start | bytes 9220
  110.2 2.4 copy-start.22
  110.2 2.4 copy-start.25
  112.3 20.1 %copy-start.5 = (f32[512,768]{1,0:T(8,128)}, f32[512,768]{1,0:T(8,128)S(1)}, u32[]{:S(2)}) copy-start(f32[512,768]{1,0:T(8,128)S(1)} %get-tuple-element.86) | copy-start | bytes 4718596
  112.3 9.3 %slice-start.2 = ((s8[4718592]{0:T(1024)(128)(4,1)}), s8[4194304]{0:T(1024)(128)(4,1)S(1)}, s32[]{:S(2)}) async-start(s8[4718592]{0:T(1024)(128)(4,1)} %bitcast.127), calls=%async_computation.3 | async-start | bytes 8388608
  112.6 8.9 %copy-start.10 = (bf16[4,128,768]{2,1,0:T(8,128)(2,1)S(1)}, bf16[4,128,768]{2,1,0:T(8,128)(2,1)}, u32[]{:S(2)}) copy-start(bf16[4,128,768]{2,1,0:T(8,128)(2,1)} %param.33) | copy-start | bytes 2359300
  112.6 8.9 %slice-start.3 = ((s8[4718592]{0:T(1024)(128)(4,1)}), s8[524288]{0:T(1024)(128)(4,1)S(1)}, s32[]{:S(2)}) async-start(s8[4718592]{0:T(1024)(128)(4,1)} %bitcast.127), calls=%async_computation.4 | async-start | bytes 1048576
  112.6 16.1 %slice-start = ((s8[4718592]{0:T(1024)(128)(4,1)}), s8[4194304]{0:T(1024)(128)(4,1)S(1)}, s32[]{:S(2)}) async-start(s8[4718592]{0:T(1024)(128)(4,1)} %bitcast.125), calls=%async_computation.1 | async-start | bytes 8388608
  121.5 7.3 %copy-start.35 = (f32[512,3072]{1,0:T(8,128)}, f32[512,3072]{1,0:T(8,128)S(1)}, u32[]{:S(2)}) copy-start(f32[512,3072]{1,0:T(8,128)S(1)} %get-tuple-element.90) | copy-start | bytes 18874372
  121.6 7.2 %slice-start.1 = ((s8[4718592]{0:T(1024)(128)(4,1)}), s8[524288]{0:T(1024)(128)(4,1)S(1)}, s32[]{:S(2)}) async-start(s8[4718592]{0:T(1024)(128)(4,1)} %bitcast.125), calls=%async_computation.2 | async-start | bytes 1048576
  128.8 3.6 copy-start.33
  133.6 2.0 copy-start.1
  236.4 4.1 copy-start.6
  236.4 4.1 copy-start.34
  240.5 5.6 %copy-start.32 = (bf16[768]{0:T(1024)(128)(2,1)S(1)}, bf16[768]{0:T(1024)(128)(2,1)}, u32[]{:S(2)}) copy-start(bf16[768]{0:T(1024)(128)(2,1)} %param.31) | copy-start | bytes 4612
  248.5 4.7 copy-start.24
  253.2 9.7 %copy-start.3 = (bf16[3,768,512]{2,1,0:T(8,128)(2,1)S(1)}, bf16[3,768,512]{2,1,0:T(8,128)(2,1)}, u32[]{:S(2)}) copy-start(bf16[3,768,512]{2,1,0:T(8,128)(2,1)} %get-tuple-element.35) | copy-start | bytes 7077892
  262.8 1.0 copy-start.20
  263.8 7.4 %copy-start.4 = (bf16[3,768,512]{2,1,0:T(8,128)(2,1)S(1)}, bf16[3,768,512]{2,1,0:T(8,128)(2,1)}, u32[]{:S(2)}) copy-start(bf16[3,768,512]{2,1,0:T(8,128)(2,1)} %get-tuple-element.35) | copy-start | bytes 7077892
  263.8 7.4 %copy-start.7 = (bf16[768,512]{1,0:T(8,128)(2,1)S(1)}, bf16[768,512]{1,0:T(8,128)(2,1)}, u32[]{:S(2)}) copy-start(bf16[768,512]{1,0:T(8,128)(2,1)} %copy.40) | copy-start | bytes 2359300
  271.2 5.0 copy-start.8
  271.2 5.0 copy-start.11
  281.2 162.4 %copy-start.18 = (f32[2304]{0:T(1024)S(1)}, f32[2304]{0:T(1024)}, u32[]{:S(2)}) copy-start(f32[2304]{0:T(1024)} %reduce_sum.157) | copy-start | bytes 27652
  488.9 2.3 copy-start.16
  488.9 3.1 copy-start.15
  488.9 3.8 copy-start.17
  488.9 4.5 copy-start.13
  492.7 1.7 copy-start.12
Sparse Core Ops, SparseCore 0:
  234.7 127.8 all-reduce.3

commit v3 on v2

--- a/solution.py
+++ b/solution.py
@@ -57,48 +57,11 @@
     return jnp.concatenate([rows, jnp.ones((16, rows.shape[1]), rows.dtype)], axis=0)
 
 
-def state_rows(state, micro, head_width):
+def state_rows(state, micro, micro_count, head_width):
     low = state[micro * head_width : (micro + 1) * head_width, :]
-    count = state.shape[0] // (head_width + 2)
-    total = state[count * head_width + micro : count * head_width + micro + 1, :]
+    row = micro_count * head_width + micro
+    total = state[row : row + 1, :]
     return jnp.concatenate([low, jnp.broadcast_to(total, (16, low.shape[1]))], axis=0)
-
-
-def feature_kernel(micro_count, q_ref, k_ref, v_ref, qm_ref, km_ref, last_ref, fq_ref, fk_ref, state_ref):
-    head_width = q_ref.shape[0]
-    rows = q_ref.shape[1] // micro_count
-    for source, weights, target in ((q_ref, qm_ref, fq_ref), (k_ref, km_ref, fk_ref)):
-        mapped = matmul(weights[0], source[...], (0, 0))
-        up, down = two_softmaxes(mapped)
-        target[...] = jnp.concatenate([up, down], axis=0).astype(bfloat)
-    wide = with_ones(v_ref[...]) * last_ref[...]
-    sums = []
-    for m in range(micro_count):
-        part = slice(m * rows, (m + 1) * rows)
-        local = matmul(wide[:, part], fk_ref[:, part], (1, 1))
-        state_ref[0, m * head_width : (m + 1) * head_width, :] = local[:head_width]
-        sums.append(local[head_width : head_width + 1])
-    sums = jnp.concatenate(sums + sums, axis=0)
-    state_ref[0, micro_count * head_width :, :] = sums
-
-
-def attend_kernel(micro_count, fq_ref, fk_ref, v_ref, state_ref, mask_ref, use_ref, att_ref, low_ref, den_ref):
-    head_width = v_ref.shape[0]
-    rows = v_ref.shape[1] // micro_count
-    wide = with_ones(v_ref[...])
-    used = fq_ref[...] * use_ref[...]
-    for m in range(micro_count):
-        part = slice(m * rows, (m + 1) * rows)
-        scores = matmul(fk_ref[:, part], fq_ref[:, part], (0, 0)) * mask_ref[m]
-        state = state_rows(state_ref[0], m, head_width).astype(bfloat)
-        numer = matmul(wide[:, part], scores.astype(bfloat), (1, 0)) + matmul(
-            state, used[:, part], (1, 0)
-        )
-        denom = numer[head_width : head_width + 1]
-        attended = numer[:head_width] / denom
-        att_ref[:, part] = attended
-        low_ref[:, part] = attended.astype(bfloat)
-        den_ref[0, :, part] = denom
 
 
 def score_grads(grad, attended, denom):
@@ -151,8 +114,8 @@
         mask = mask_ref[m]
         scores = (matmul(fk, fq, (0, 0)) * mask).astype(bfloat)
         grad_scores = (matmul(wide[:, part], low_grads[:, part], (0, 0)) * mask).astype(bfloat)
-        state = state_rows(state_ref[0], m, head_width).astype(bfloat)
-        out_grad = state_rows(out_grad_ref[0], m, head_width)
+        state = state_rows(state_ref.at[0], m, micro_count, head_width).astype(bfloat)
+        out_grad = state_rows(out_grad_ref.at[0], m, micro_count, head_width)
         row = lax.broadcasted_iota(jnp.int32, out_grad.shape, 0)
         out_grad = jnp.where(row <= head_width, out_grad, 0.0).astype(bfloat)
         fqg[:, part] = matmul(fk, grad_scores, (1, 0)) + matmul(state, used_grads[:, part], (0, 0))
@@ -270,7 +233,274 @@
     )(local, masks)
 
 
-def reduce_kernel(count, lines, plans, sources, *refs):
+def document(position, bounds_ref, m):
+    return jnp.where(position >= bounds_ref[m, 0], 1, 0) + jnp.where(
+        position >= bounds_ref[m, 1], 1, 0
+    )
+
+
+def token_masks(bounds_ref, first_row, rows, micro_count, mask_ref, use_ref, last_ref):
+    low_shape, line_shape = ((rows, rows), (1, rows))
+    source = first_row + lax.broadcasted_iota(jnp.int32, low_shape, 0)
+    target = first_row + lax.broadcasted_iota(jnp.int32, low_shape, 1)
+    line = first_row + lax.broadcasted_iota(jnp.int32, line_shape, 1)
+    for m in range(micro_count):
+        part = slice(m * rows, (m + 1) * rows)
+        same = document(source, bounds_ref, m) == document(target, bounds_ref, m)
+        mask_ref[m] = jnp.where((source <= target) & same, 1.0, 0.0)
+        own = document(line, bounds_ref, m)
+        use_ref[:, part] = jnp.where(own == document(first_row - 1, bounds_ref, m), 1.0, 0.0)
+        last_ref[:, part] = jnp.where(
+            own == document(first_row + rows - 1, bounds_ref, m), 1.0, 0.0
+        )
+
+
+def chain_masks(bounds_ref, first_row, low, rows, micro_count, head_width, reverse, mask_ref):
+    base = first_row - low * rows
+    step = 2 * rows
+    height, wide = mask_ref.shape[1:]
+    for m in range(micro_count):
+        def doc(position, m=m):
+            return document(position, bounds_ref, m)
+
+        inner = doc(base + rows - 1)
+        if reverse:
+            lead = 1 - low
+            own_edge, pair, ahead = (doc(first_row - 1), doc(base + step - 1), doc(base - 1))
+        else:
+            lead = low
+            own_edge, pair, ahead = (
+                doc(first_row + rows - 1), doc(base - 1), doc(base + step - 1),
+            )
+        keep = jnp.where(pair == inner, 1.0, 0.0)
+        values = [
+            jnp.where(pair == ahead, 1.0, 0.0),
+            jnp.where(own_edge == ahead, 1.0, 0.0),
+            jnp.where(lead == 0, keep, 1.0),
+            jnp.where(lead == 0, 1.0, 0.0),
+            jnp.where(lead == 0, 1.0, keep),
+        ]
+        for i, value in enumerate(values):
+            mask_ref[i, m * head_width : (m + 1) * head_width, :] = jnp.full(
+                (head_width, wide), value
+            )
+            tail = slice(micro_count * head_width, height)
+            row = lax.broadcasted_iota(jnp.int32, (height - tail.start, wide), 0)
+            before = jnp.zeros(row.shape, single) if m == 0 else mask_ref[i, tail, :]
+            mask_ref[i, tail, :] = jnp.where(lax.rem(row, micro_count) == m, value, before)
+
+
+class Chain:
+    def __init__(self, reverse, count, carry, onward, aside, beside, mask, sems):
+        self.carry, self.onward, self.aside, self.beside = carry, onward, aside, beside
+        self.mask, self.sems = mask, sems
+        place, self.column = (lax.axis_index("seq"), lax.axis_index("batch"))
+        high, low = (place // 2, lax.rem(place, 2))
+        length = count // 2
+        self.lap = length - 1 - high if reverse else high
+        self.ahead, self.behind = (place - 2, place + 2) if reverse else (place + 2, place - 2)
+        self.partner = place + 1 - 2 * low
+        self.first, self.final = (self.lap == 0, self.lap == length - 1)
+
+    def greet(self, barrier):
+        def signal(place):
+            pl.semaphore_signal(
+                barrier, inc=1, device_id=(place, self.column), device_id_type=MESH
+            )
+
+        signal(self.partner)
+
+        @pl.when(jnp.logical_not(self.final))
+        def _():
+            signal(self.ahead)
+
+        @pl.when(jnp.logical_not(self.first))
+        def _():
+            signal(self.behind)
+
+        return 1 + jnp.where(self.first, 0, 1) + jnp.where(self.final, 0, 1)
+
+    def along(self, i):
+        return pltpu.make_async_remote_copy(
+            src_ref=self.onward.at[i], dst_ref=self.carry.at[i], send_sem=self.sems[0].at[i],
+            recv_sem=self.sems[1].at[i], device_id=(self.ahead, self.column), device_id_type=MESH,
+        )
+
+    def across(self, i):
+        return pltpu.make_async_remote_copy(
+            src_ref=self.aside.at[i], dst_ref=self.beside.at[i], send_sem=self.sems[2].at[i],
+            recv_sem=self.sems[3].at[i], device_id=(self.partner, self.column),
+            device_id_type=MESH,
+        )
+
+    def start(self):
+        @pl.when(self.first)
+        def _():
+            self.carry[...] = jnp.zeros_like(self.carry)
+
+    def step(self, i, local):
+        @pl.when(jnp.logical_not(self.first))
+        def _():
+            self.along(i).wait_recv()
+
+        state = self.carry[i]
+
+        @pl.when(jnp.logical_not(self.final))
+        def _():
+            self.onward[i] = self.mask[0] * state + self.mask[1] * local
+            self.along(i).start()
+
+        self.aside[i] = self.mask[2] * state + self.mask[3] * local
+        self.across(i).start()
+
+    def result(self, i):
+        self.across(i).wait_recv()
+        return self.mask[4] * self.carry[i] + self.beside[i]
+
+    def drain(self, chunks):
+        def one(i, _):
+            self.across(i).wait_send()
+
+            @pl.when(jnp.logical_not(self.final))
+            def _():
+                self.along(i).wait_send()
+
+            return 0
+
+        lax.fori_loop(0, chunks, one, 0)
+
+
+def local_state(wide, other, micro_count, head_width, target):
+    rows = wide.shape[1] // micro_count
+    sums = []
+    for m in range(micro_count):
+        part = slice(m * rows, (m + 1) * rows)
+        local = matmul(wide[:, part], other[:, part], (1, 1))
+        target[m * head_width : (m + 1) * head_width, :] = local[:head_width]
+        sums.append(local[head_width : head_width + 1])
+    target[micro_count * head_width :, :] = jnp.concatenate(sums + sums, axis=0)
+
+
+def forward_kernel(
+    count, micro_count, x_ref, gain_ref, shift_ref, weight_ref, bias_ref, qm_ref, km_ref,
+    bounds_ref, proj_ref, fq_ref, fk_ref, state_ref, att_ref, low_ref, den_ref,
+    normed, mask, use, last, chain_mask, local, carry, onward, aside, beside, *sems,
+):
+    heads, head_width = qm_ref.shape[:2]
+    total_rows = x_ref.shape[0]
+    rows = total_rows // micro_count
+    model_width = x_ref.shape[1]
+    pair = 2 * head_width
+    place = lax.axis_index("seq")
+    first_row = place * rows
+    chain = Chain(False, count, carry, onward, aside, beside, chain_mask, sems)
+    barrier = pltpu.get_barrier_semaphore()
+    greeted = chain.greet(barrier)
+    token_masks(bounds_ref, first_row, rows, micro_count, mask, use, last)
+    chain_masks(
+        bounds_ref, first_row, lax.rem(place, 2), rows, micro_count, head_width, False, chain_mask
+    )
+    chain.start()
+    normed[...] = norm_forward(
+        x_ref[...].astype(single), gain_ref[...].astype(single), shift_ref[...].astype(single)
+    )[0].astype(bfloat)
+    pl.semaphore_wait(barrier, greeted)
+
+    def project(p):
+        for part in range(3):
+            columns = pl.ds(pl.multiple_of(part * model_width + p * pair, pair), pair)
+            value = matmul(normed[...], weight_ref[:, columns], (1, 0))
+            value = (value + bias_ref[:, columns].astype(single)).astype(bfloat).T
+            proj_ref[part * heads + 2 * p] = value[:head_width]
+            proj_ref[part * heads + 2 * p + 1] = value[head_width:]
+
+    def features(h):
+        for offset, weights, target in ((0, qm_ref, fq_ref), (heads, km_ref, fk_ref)):
+            mapped = matmul(weights[h], proj_ref[offset + h], (0, 0))
+            up, down = two_softmaxes(mapped)
+            target[h] = jnp.concatenate([up, down], axis=0).astype(bfloat)
+        wide = with_ones(proj_ref[2 * heads + h]) * last[...].astype(bfloat)
+        local_state(wide, fk_ref.at[h], micro_count, head_width, local.at[h])
+
+    def attend(h):
+        state_ref[h] = chain.result(h)
+        wide = with_ones(proj_ref[2 * heads + h])
+        used = fq_ref[h] * use[...].astype(bfloat)
+        for m in range(micro_count):
+            part = slice(m * rows, (m + 1) * rows)
+            scores = matmul(fk_ref[h, :, part], fq_ref[h, :, part], (0, 0)) * mask[m]
+            state = state_rows(state_ref.at[h], m, micro_count, head_width).astype(bfloat)
+            numer = matmul(wide[:, part], scores.astype(bfloat), (1, 0)) + matmul(
+                state, used[:, part], (1, 0)
+            )
+            denom = numer[head_width : head_width + 1]
+            attended = numer[:head_width] / denom
+            att_ref[h, :, part] = attended
+            low_ref[h, :, part] = attended.astype(bfloat)
+            den_ref[h, :, part] = denom
+
+    def one_round(r, _):
+        @pl.when((r < heads) & (lax.rem(r, 2) == 0))
+        def _():
+            project(r // 2)
+
+        @pl.when(r < heads)
+        def _():
+            features(r)
+
+        @pl.when((r >= chain.lap) & (r < heads + chain.lap))
+        def _():
+            chain.step(r - chain.lap, local[r - chain.lap])
+
+        @pl.when(r >= chain.lap + 1)
+        def _():
+            attend(r - chain.lap - 1)
+
+        return 0
+
+    lax.fori_loop(0, heads + chain.lap + 1, one_round, 0)
+    chain.drain(heads)
+
+
+def forward_attention(x, gain, shift, weight, bias, query_map, key_map, bounds, count):
+    total_rows, model_width = x.shape
+    heads, head_width = query_map.shape[:2]
+    micro_count = bounds.shape[0]
+    rows = total_rows // micro_count
+    height = micro_count * (head_width + 2)
+    chunk = (heads, height, 2 * head_width)
+    whole = pl.BlockSpec(memory_space=pltpu.VMEM)
+    head = (heads, head_width, total_rows)
+    feat = (heads, 2 * head_width, total_rows)
+    shape = jax.ShapeDtypeStruct
+    return pl.pallas_call(
+        partial(forward_kernel, count, micro_count),
+        out_shape=[
+            shape((3 * heads,) + head[1:], bfloat), shape(feat, bfloat), shape(feat, bfloat),
+            shape(chunk, single), shape(head, single), shape(head, bfloat),
+            shape((heads, 1, total_rows), single),
+        ],
+        in_specs=[whole] * 7 + [pl.BlockSpec(memory_space=pltpu.SMEM)],
+        out_specs=[whole] * 7,
+        scratch_shapes=[
+            pltpu.VMEM((total_rows, model_width), bfloat),
+            pltpu.VMEM((micro_count, rows, rows), single),
+            pltpu.VMEM((1, total_rows), single),
+            pltpu.VMEM((1, total_rows), single),
+            pltpu.VMEM((5,) + chunk[1:], single),
+        ]
+        + [pltpu.VMEM(chunk, single)] * 5
+        + [pltpu.SemaphoreType.DMA((heads,))] * 4,
+        compiler_params=pltpu.CompilerParams(
+            collective_id=1, has_side_effects=True, vmem_limit_bytes=VMEM_LIMIT
+        ),
+    )(
+        x, gain.reshape(1, -1), shift.reshape(1, -1), weight, bias.reshape(1, -1), query_map,
+        key_map, bounds,
+    )
+
+
+def reduce_kernel(count, lines, plans, sources, *refs, ahead=2):
     direct, halved = plans
     total = direct + halved
     arrays = len({s[0] for s in sources})
@@ -331,9 +561,13 @@
     def give(u):
         return remote(source(u, 1 - core), got.at[u], core_send.at[u], core_recv.at[u], at_core)
 
-    for u in range(total):
-        give(u).start()
-        load(u).start()
+    def begin(r):
+        for u in ([r] if r < direct else []) + ([direct + r] if r < halved else []):
+            give(u).start()
+            load(u).start()
+
+    for r in range(ahead):
+        begin(r)
 
     def settle(u):
         pltpu.make_async_copy(own.at[u], own.at[u], own_sem.at[u]).wait()
@@ -508,10 +742,15 @@
     if halved:
         steps = [halved_first, halved_next, thin.from_y] + z_steps(thin) + [halved_reduced, halved_done]
         stages += [(s, f, halved) for s, f in enumerate(steps)]
-    stages.sort(key=lambda s: -s[0])
-    rounds = max(direct, halved) + stages[0][0]
+    stages.sort(key=lambda s: s[0])
+    rounds = max(direct, halved) + stages[-1][0]
 
     def one_round(r, _):
+        for later in range(ahead, max(direct, halved)):
+            @pl.when(r == later - ahead)
+            def _(later=later):
+                begin(later)
+
         for lag, step, size in stages:
             @pl.when((r >= lag) & (r < lag + size))
             def _(lag=lag, step=step):
@@ -654,7 +893,6 @@
     use_low, last_low = (use_in.astype(bfloat), in_last.astype(bfloat))
     causal = positions[:, None] <= positions[None, :]
     mask = (causal[None] & (doc_ids[:, :, None] == doc_ids[:, None, :])).astype(single)
-    masks_forward = scan_masks(bounds, first_row, row_count, place, micro_count, head_width, False)
     masks_reverse = scan_masks(bounds, first_row, row_count, place, micro_count, head_width, True)
 
     flat_input = inputs.reshape(total_rows, model_width).astype(single)
@@ -662,11 +900,6 @@
         flat_input, gain_one.astype(single), bias_one.astype(single)
     )
     normed_low = normed.astype(bfloat)
-    projected = (
-        jnp.einsum("dc,rd->cr", project_weight, normed_low, preferred_element_type=single)
-        + project_bias.astype(single)[:, None]
-    ).astype(bfloat)
-
     head_rows = lambda offset: pl.BlockSpec((head_width, total_rows), lambda h: (h + offset, 0))
     map_spec = pl.BlockSpec((1, head_width, head_width), lambda h: (h, 0, 0))
     feat_spec = pl.BlockSpec((feat_width, total_rows), lambda h: (h, 0))
@@ -676,31 +909,18 @@
     state_spec = pl.BlockSpec((1, state_height, feat_width), lambda h: (h, 0, 0))
     mask_spec = pl.BlockSpec((micro_count, row_count, row_count), lambda h: (0, 0, 0))
     q_spec, k_spec, v_spec = (head_rows(0), head_rows(head_count), head_rows(2 * head_count))
-    feat_shape = jax.ShapeDtypeStruct((head_count * feat_width, total_rows), bfloat)
     state_shape = jax.ShapeDtypeStruct((head_count, state_height, feat_width), single)
     params = pltpu.CompilerParams(vmem_limit_bytes=VMEM_LIMIT)
 
-    feat_query, feat_key, local_state = pl.pallas_call(
-        partial(feature_kernel, micro_count),
-        grid=(head_count,),
-        in_specs=[q_spec, k_spec, v_spec, map_spec, map_spec, line_spec],
-        out_specs=[feat_spec, feat_spec, state_spec],
-        out_shape=[feat_shape, feat_shape, state_shape],
-        compiler_params=params,
-    )(projected, projected, projected, query_map, key_map, last_low)
-    state_in = scan_states(local_state, masks_forward, count, False, 1)
-    attended, attended_low, denominator = pl.pallas_call(
-        partial(attend_kernel, micro_count),
-        grid=(head_count,),
-        in_specs=[feat_spec, feat_spec, v_spec, state_spec, mask_spec, line_spec],
-        out_specs=[head_rows(0), head_rows(0), den_spec],
-        out_shape=[
-            jax.ShapeDtypeStruct((model_width, total_rows), single),
-            jax.ShapeDtypeStruct((model_width, total_rows), bfloat),
-            jax.ShapeDtypeStruct((head_count, 1, total_rows), single),
-        ],
-        compiler_params=params,
-    )(feat_query, feat_key, projected, state_in, mask, use_low)
+    projected, feat_query, feat_key, state_in, attended, attended_low, denominator = forward_attention(
+        inputs.reshape(total_rows, model_width), gain_one, bias_one, project_weight, project_bias,
+        query_map, key_map, bounds, count,
+    )
+    projected = projected.reshape(3 * model_width, total_rows)
+    feat_query = feat_query.reshape(head_count * feat_width, total_rows)
+    feat_key = feat_key.reshape(head_count * feat_width, total_rows)
+    attended = attended.reshape(model_width, total_rows)
+    attended_low = attended_low.reshape(model_width, total_rows)
 
     branch = jnp.einsum(
         "er,ed->rd", attended_low, output_weight, preferred_element_type=single

time: 504 us -> 444 us (0.88)
  Pallas kernels: 326 us -> 296 us
  other arithmetic: 29.8 us -> 16 us
  local copies, waits for them, and re-layouts: 27.7 us -> 20 us
  matrix products: 62.8 us -> 56.4 us
    pallas_call x2 -> x1, Pallas kernels: 110 us -> 66.7 us  [scan_states(): pl.pallas_call(partial(scan_kernel, reverse, count), out_shape=jax.ShapeD...]
    pallas_call x2 -> x1, Pallas kernels: 22.3 us -> 50.5 us  [forward_attention(): pl.pallas_call(partial(forward_kernel, count, micro_count), out_shape=[sh...]
    pallas_call x1, Pallas kernels: 162 us -> 148 us  [reduce_all(): pl.pallas_call(partial(reduce_kernel, count, lines, plans, sources), out_...]
  transfers between devices with their start and end apart: 1 -> 1, of which waited for: 0 -> 0; matrix products, arithmetic and copies ran while one was open for 10% -> 11% of each run, Pallas kernels for 32% -> 33%
where the time goes in v3:
time: 444 us; the launch traced here: 443 us
  Pallas kernels  296 us (67%)
  matrix products  56.4 us (13%)
  blocking collectives  39.8 us (9%)
  local copies, waits for them, and re-layouts  20 us (5%)
  other arithmetic  16 us (4%)
  between operations  14.5 us (3%)
    pallas_call x1, Pallas kernels, reduce_all(): pl.pallas_call(partial(reduce_kernel, count, lines, plans, sources), out_...  148 us
    pallas_call x1, Pallas kernels, scan_states(): pl.pallas_call(partial(scan_kernel, reverse, count), out_shape=jax.ShapeD...  66.7 us
    pallas_call x1, Pallas kernels, forward_attention(): pl.pallas_call(partial(forward_kernel, count, micro_count), out_shape=[sh...  50.5 us
    psum x1, blocking collectives, per_device(): lax.psum((gain_one_grad, bias_one_grad, project_bias_grad, query_map_grad...  39.8 us
    pallas_call x1, Pallas kernels, per_device(): pl.pallas_call(partial(backward_kernel, micro_count), grid=(head_count,),...  21.7 us
    dot_general x1, matrix products, per_device(): jnp.dot(hidden_low, contract_weight, preferred_element_type=single)  9.57 us
    pallas_call x1, Pallas kernels, per_device(): pl.pallas_call(partial(state_grad_kernel, micro_count), grid=(head_count,...  9.12 us
  transfers between devices with their start and end apart: 1, of which 0 were waited for; matrix products, arithmetic and copies ran while one was open for 11% of the time, Pallas kernels for 33%

profile of v3, /device:TPU:0, one launch (start us, length us, event | category | flops | bytes accessed | tf_op | source)
XLA Modules:
  0.0 442.5 jit_solution(2725623594737255735)
XLA Ops:
  7.3 1.4 copy.37.bounds_ref
  8.7 0.8 fusion.41
  9.4 0.8 fusion.40
  10.2 0.8 fusion.36
  11.0 0.8 fusion.44
  11.8 0.7 convert_add_fusion.1
  12.5 0.7 fusion.34
  13.1 0.6 copy.47
  13.7 1.3 reshape.614.gain_ref
  15.0 1.3 reshape.615.shift_ref
  16.2 0.7 convert_element_type.309
  16.9 0.7 convert_element_type.310
  17.6 0.7 convert_element_type.308
  18.3 1.3 reshape.616.bias_ref
  19.9 0.7 convert_element_type.312
  20.6 50.5 %shard_map.288 = (bf16[36,64,512]{2,1,0:T(8,128)(2,1)}, bf16[12,128,512]{2,1,0:T(8,128)(2,1)}, bf16[12,128,512]{2,1,0:T(8,128)(2,1)}, f32[12,264,128]{2,1,0:T(8,...) custom-call(bf16[512,768]{1,0:T(8,128)(2,1)} %bitcast.86, ...), custom_call_target="tpu_custom_call" | custom-call | tf_op jit(solution)/shard_map/pallas_call | solution.py:476
  71.1 2.2 fusion.57
  73.7 5.8 %fusion.14 = (bf16[3072,512]{0,1:T(8,128)(2,1)}, f32[512,3072]{1,0:T(8,128)S(1)}) fusion(f32[3072]{0:T(1024)S(1)} %convert_element_type.312, bf16[768,3072]{1,0:T(8,128)(2,1)S(1)} %copy-done.36, f32[512,768]{1,0:T(8,128)S(1)} %get-tuple-element.80, f32[768]{0:T(1024)S(1)} %convert_element_type.310, f32[768]{0:T(1024)S(1)} %convert_element_type.309, ...), kind=kOutput, calls=%fused_computation.17 | convolution fusion | flops 2433613824 | bytes 15751168 | tf_op jit(solution)/shard_map/dot_general | solution.py:933
  79.6 7.2 %convert_reduce_fusion = (f32[3072]{0:T(1024)}, bf16[512,3072]{1,0:T(8,128)(2,1)S(1)}) fusion(f32[512,3072]{1,0:T(8,128)S(1)} %get-tuple-element.83, f32[3072]{0:T(1024)S(1)} %convert_element_type.312, bf16[512,768]{1,0:T(8,128)(2,1)S(1)} %bitcast.97, bf16[3072,768]{1,0:T(8,128)(2,1)S(1)} %bitcast.109), kind=kOutput, calls=%fused_computation.18 | convolution fusion | flops 2452091904 | bytes 14966784 | tf_op jit(solution)/shard_map/rd,fd->rf/dot_general | solution.py:946
  86.8 3.6 multiply_reduce_fusion
  90.4 1.9 convert_reduce_fusion.4
  92.3 1.9 convolution_bitcast_fusion.grad_ref
  94.3 0.8 and_convert_fusion.mask_ref
  95.1 9.1 %shard_map.289.local_ref = f32[12,264,128]{2,1,0:T(8,128)} custom-call(f32[768,512]{1,0:T(8,128)} %convolution_bitcast_fusion.grad_ref, f32[768,512]{1,0:T(8,128)} %bitcast.93, f32[12,1,512]{2,1,0:T(1,128)} %get-tuple-element.35.den_ref, bf16[1536,512]{1,0:T(8,128)(2,1)} %bitcast.91, f32[1,512]{1,0:T(1,128)} %bitcast.104), custom_call_target="tpu_custom_call" | custom-call | tf_op jit(solution)/shard_map/pallas_call | solution.py:961
  104.2 1.1 broadcast_in_dim.5.mask_ref
  105.3 66.7 %shard_map.290.out_grad_ref = f32[12,264,128]{2,1,0:T(8,128)} custom-call(f32[12,264,128]{2,1,0:T(8,128)} %shard_map.289.local_ref, f32[5,264,128]{2,1,0:T(8,128)} %broadcast_in_dim.5.mask_ref), custom_call_target="tpu_custom_call" | custom-call | tf_op jit(solution)/shard_map/pallas_call | solution.py:223
  172.0 21.7 %shard_map.291 = (bf16[3,768,512]{2,1,0:T(8,128)(2,1)}, f32[12,64,64]{2,1,0:T(8,128)}, f32[12,64,64]{2,1,0:T(8,128)}) custom-call(bf16[2304,512]{1,0:T(8,128)(2,1)} %bitcast.83, bf16[2304,512]{1,0:T(8,128)(2,1)} %bitcast.84, bf16[2304,512]{1,0:T(8,128)(2,1)} %bitcast.85, bf16[12,64,64]{2,1,0:T(8,128)(2,1)} %qm_ref.3, bf16[12,64,64]{2,1,0:T(8,128)(2,1)} %km_ref.3, ...), custom_call_target="tpu_custom_call" | custom-call | tf_op jit(solution)/shard_map/pallas_call | solution.py:971
  194.5 0.5 copy-done.9
  195.1 0.4 copy-done.5
  195.6 7.2 %fusion.52 = f32[768,3072]{1,0:T(8,128)} fusion(bf16[512,3072]{1,0:T(8,128)(2,1)} %copy-done.37, f32[512,768]{1,0:T(8,128)S(1)} %copy-done.5, f32[768]{0:T(1024)S(1)} %copy-done.34, f32[768]{0:T(1024)S(1)} %copy-done.23, f32[512]{0:T(512)S(1)} %copy-done.28, f32[512]{0:T(512)S(1)} %copy-done.20), kind=kOutput, calls=%fused_computation.107 | convolution fusion | flops 2417885184 | bytes 14166016 | tf_op jit(solution)/shard_map/rd,rf->df/dot_general | solution.py:1009
  203.2 4.7 %copy.39 = bf16[3072,512]{1,0:T(8,128)(2,1)} copy(bf16[3072,512]{0,1:T(8,128)(2,1)} %get-tuple-element.82) | data formatting | bytes 6291456 | tf_op jit(solution)/shard_map/convert_element_type | solution.py:937
  207.9 9.6 %add_convert_fusion = bf16[512,768]{1,0:T(8,128)(2,1)} fusion(f32[512,768]{1,0:T(8,128)} %copy-done.4, bf16[3072,768]{1,0:T(8,128)(2,1)} %param.30, f32[512,3072]{1,0:T(8,128)} %copy-done.38, f32[3072]{0:T(1024)S(1)} %copy-done.25, f32[768]{0:T(1024)S(1)} %convert_element_type.314), kind=kOutput, calls=%fused_computation.46 | convolution fusion | flops 2432827392 | bytes 13384704 | tf_op jit(solution)/shard_map/dot_general | solution.py:940
  217.4 2.2 fusion.32.refs_2_
  219.6 0.4 convert_reduce_fusion.1
  220.0 4.8 %fusion.58 = f32[512,768]{1,0:T(8,128)S(1)} fusion(bf16[2304,512]{1,0:T(8,128)(2,1)} %bitcast.89, bf16[768,2304]{1,0:T(8,128)(2,1)} %weight_ref.1), kind=kOutput, calls=%fused_computation.110 | convolution fusion | flops 1811939328 | bytes 7471104 | tf_op jit(solution)/shard_map/cr,dc->rd/dot_general | solution.py:991
  224.8 1.6 fusion.26
  226.4 1.4 copy.40
  227.9 6.8 %fusion.60.refs_3_ = f32[4,2,96,2304]{3,2,1,0:T(8,128)} fusion(bf16[4,2,96,512]{3,2,1,0:T(8,128)(2,1)S(1)} %bitcast.95, bf16[2304,512,1,1]{1,0,3,2:T(8,128)(2,1)} %bitcast.90), kind=kOutput, calls=%fused_computation.112 | convolution fusion | flops 1811939328 | bytes 10223616 | tf_op jit(solution)/shard_map/rd,cr->dc/dot_general | solution.py:1011
  234.6 5.1 %fusion.59.refs_0_ = f32[4,2,4,96,768]{4,3,2,1,0:T(8,128)} fusion(bf16[4,2,4,96,512]{4,3,2,1,0:T(8,128)(2,1)S(1)} %bitcast.96, bf16[512,768,1,1,1]{1,0,4,3,2:T(8,128)(2,1)S(1)} %bitcast.98), kind=kOutput, calls=%fused_computation.111 | convolution fusion | flops 2415919104 | bytes 13369344 | tf_op jit(solution)/shard_map/rf,rd->fd/dot_general | solution.py:1006
  239.7 147.8 %shard_map.292 = (f32[4,96,768]{2,1,0:T(8,128)}, f32[96,3072]{1,0:T(8,128)}, f32[96,768]{1,0:T(8,128)}, f32[96,2304]{1,0:T(8,128)}) custom-call(f32[4,2,4,96,768]{4,3,2,1,0:T(8,128)} %fusion.59.refs_0_, f32[4,2,96,3072]{3,2,1,0:T(8,128)} %bitcast.88, f32[4,2,96,768]{3,2,1,0:T(8,128)} %fusion.32.refs_2_, f32[4,2,96,2304]{3,2,1,0:T(8,128)} %fusion.60.refs_3_), custom_call_target="tpu_custom_call" | custom-call | tf_op jit(solution)/shard_map/pallas_call | solution.py:810
  387.5 39.8 %all-reduce = (f32[768]{0:T(1024)}, f32[768]{0:T(1024)}, f32[2304]{0:T(1024)}, f32[768]{0:T(1024)}, f32[768]{0:T(1024)}, /*index=5*/f32[768]{0:T(1024)}, f32[3072]{0:T(1024)}, f32[768]{0:T(1024)}) all-reduce(f32[768]{0:T(1024)S(1)} %get-tuple-element.46, ...), channel_id=1, replica_groups=mesh['seq'=8,'batch'=4] {'seq','batch'}, use_global_device_ids=true, to_apply=%region_9.10 | all-reduce | flops 9984 | bytes 79872 | tf_op jit(solution)/shard_map/psum | solution.py:1030
  427.4 2.9 fusion.25
  430.3 0.9 copy.54
  431.4 0.7 copy.55
  432.2 0.7 copy.56
  432.9 0.7 copy.57
  433.7 1.0 copy.58
  434.7 1.0 copy.59
  (107 shorter events, 2.3 us)
Async XLA Ops:
  7.2 63.9 %copy-start = (bf16[768,768]{1,0:T(8,128)(2,1)S(1)}, bf16[768,768]{1,0:T(8,128)(2,1)}, u32[]{:S(2)}) copy-start(bf16[768,768]{1,0:T(8,128)(2,1)} %param.24) | copy-start | bytes 3538948
  7.2 423.1 %all-reduce.4.cloned.1.call-start = ((), (), s32[]{:S(2)}) async-start(), calls=%async_computation | async-start | bytes 1572864 | tf_op jit(solution)/shard_map/psum | solution.py:1030
  16.9 69.8 %copy-start.22 = (f32[768]{0:T(1024)}, f32[768]{0:T(1024)S(1)}, u32[]{:S(2)}) copy-start(f32[768]{0:T(1024)S(1)} %convert_element_type.309) | copy-start | bytes 9220
  17.6 56.0 %copy-start.33 = (f32[768]{0:T(1024)}, f32[768]{0:T(1024)S(1)}, u32[]{:S(2)}) copy-start(f32[768]{0:T(1024)S(1)} %convert_element_type.310) | copy-start | bytes 9220
  20.6 59.0 %copy-start.24 = (f32[3072]{0:T(1024)}, f32[3072]{0:T(1024)S(1)}, u32[]{:S(2)}) copy-start(f32[3072]{0:T(1024)S(1)} %convert_element_type.312) | copy-start | bytes 36868
  20.6 50.5 %copy-start.2 = (bf16[4,128,768]{2,1,0:T(8,128)(2,1)S(1)}, bf16[4,128,768]{2,1,0:T(8,128)(2,1)}, u32[]{:S(2)}) copy-start(bf16[4,128,768]{2,1,0:T(8,128)(2,1)} %param.17) | copy-start | bytes 2359300
  71.0 2.6 copy-start.36
  73.3 17.1 %copy-start.4 = (f32[512,768]{1,0:T(8,128)}, f32[512,768]{1,0:T(8,128)S(1)}, u32[]{:S(2)}) copy-start(f32[512,768]{1,0:T(8,128)S(1)} %get-tuple-element.80) | copy-start | bytes 4718596
  73.3 17.1 %copy-start.19 = (f32[512]{0:T(512)}, f32[512]{0:T(512)S(1)}, u32[]{:S(2)}) copy-start(f32[512]{0:T(512)S(1)} %broadcast_multiply_fusion.5) | copy-start | bytes 6148
  73.3 6.2 %slice-start = ((s8[4718592]{0:T(1024)(128)(4,1)}), s8[4194304]{0:T(1024)(128)(4,1)S(1)}, s32[]{:S(2)}) async-start(s8[4718592]{0:T(1024)(128)(4,1)} %bitcast.108), calls=%async_computation.1 | async-start | bytes 8388608
  73.7 16.7 %copy-start.27 = (f32[512]{0:T(512)}, f32[512]{0:T(512)S(1)}, u32[]{:S(2)}) copy-start(f32[512]{0:T(512)S(1)} %add_rsqrt_fusion) | copy-start | bytes 6148
  73.7 5.9 %copy-start.8 = (bf16[4,128,768]{2,1,0:T(8,128)(2,1)S(1)}, bf16[4,128,768]{2,1,0:T(8,128)(2,1)}, u32[]{:S(2)}) copy-start(bf16[4,128,768]{2,1,0:T(8,128)(2,1)} %param.33) | copy-start | bytes 2359300
  73.7 5.8 %slice-start.1 = ((s8[4718592]{0:T(1024)(128)(4,1)}), s8[524288]{0:T(1024)(128)(4,1)S(1)}, s32[]{:S(2)}) async-start(s8[4718592]{0:T(1024)(128)(4,1)} %bitcast.108), calls=%async_computation.2 | async-start | bytes 1048576
  79.5 7.2 %copy-start.38 = (f32[512,3072]{1,0:T(8,128)}, f32[512,3072]{1,0:T(8,128)S(1)}, u32[]{:S(2)}) copy-start(f32[512,3072]{1,0:T(8,128)S(1)} %get-tuple-element.83) | copy-start | bytes 18874372
  86.7 3.6 copy-start.37
  92.3 2.0 copy-start.18
  193.8 0.7 copy-start.29
  193.8 0.7 copy-start.30
  193.8 1.1 copy-start.9
  193.8 1.3 copy-start.20
  193.8 1.3 copy-start.23
  193.8 1.3 copy-start.28
  193.9 1.3 copy-start.34
  193.9 1.7 copy-start.5
  195.6 7.6 %copy-start.35 = (bf16[768]{0:T(1024)(128)(2,1)S(1)}, bf16[768]{0:T(1024)(128)(2,1)}, u32[]{:S(2)}) copy-start(bf16[768]{0:T(1024)(128)(2,1)} %param.31) | copy-start | bytes 4612
  203.2 4.7 %copy-start.25 = (f32[3072]{0:T(1024)S(1)}, f32[3072]{0:T(1024)}, u32[]{:S(2)}) copy-start(f32[3072]{0:T(1024)} %copy-done.24) | copy-start | bytes 36868
  207.9 9.6 %copy-start.14 = (bf16[12,64,512]{2,1,0:T(8,128)(2,1)S(1)}, bf16[12,64,512]{2,1,0:T(8,128)(2,1)}, u32[]{:S(2)}) copy-start(bf16[12,64,512]{2,1,0:T(8,128)(2,1)} %get-tuple-element.30) | copy-start | bytes 2359300
  217.4 2.2 copy-start.3
  224.8 1.6 copy-start.6
  227.8 6.8 %copy-start.7 = (bf16[3072,512]{1,0:T(8,128)(2,1)S(1)}, bf16[3072,512]{1,0:T(8,128)(2,1)}, u32[]{:S(2)}) copy-start(bf16[3072,512]{1,0:T(8,128)(2,1)} %copy.39) | copy-start | bytes 9437188
  227.8 6.8 %copy-start.10 = (bf16[4,128,768]{2,1,0:T(8,128)(2,1)S(1)}, bf16[4,128,768]{2,1,0:T(8,128)(2,1)}, u32[]{:S(2)}) copy-start(bf16[4,128,768]{2,1,0:T(8,128)(2,1)} %param.33) | copy-start | bytes 2359300
  239.7 147.8 %copy-start.21 = (f32[768]{0:T(1024)S(1)}, f32[768]{0:T(1024)}, u32[]{:S(2)}) copy-start(f32[768]{0:T(1024)} %get-tuple-element.64) | copy-start | bytes 9220
  239.7 147.8 %copy-start.26 = (f32[3072]{0:T(1024)S(1)}, f32[3072]{0:T(1024)}, u32[]{:S(2)}) copy-start(f32[3072]{0:T(1024)} %get-tuple-element.62) | copy-start | bytes 36868
  239.7 147.8 %copy-start.31 = (f32[768]{0:T(1024)S(1)}, f32[768]{0:T(1024)}, u32[]{:S(2)}) copy-start(f32[768]{0:T(1024)} %get-tuple-element.44) | copy-start | bytes 9220
  239.7 147.8 %copy-start.32 = (f32[768]{0:T(1024)S(1)}, f32[768]{0:T(1024)}, u32[]{:S(2)}) copy-start(f32[768]{0:T(1024)} %get-tuple-element.50) | copy-start | bytes 9220
  427.4 2.9 copy-start.13
  430.3 1.2 copy-start.16
  430.3 1.9 copy-start.15
  430.3 2.6 copy-start.17
  430.3 3.4 copy-start.12
  432.9 1.7 copy-start.11
  433.7 2.0 copy-start.1
Sparse Core Ops, SparseCore 0:
  194.0 129.3 all-reduce.3

commit v4 on v1

v4 whole, which is shorter than its diff:
```python
from functools import partial

import jax
import jax.numpy as jnp
from jax import lax
from jax.experimental import pallas as pl
from jax.experimental.pallas import tpu as pltpu
from jax.sharding import PartitionSpec as P

epsilon = 1e-05
bfloat = jnp.bfloat16
single = jnp.float32
MESH = pl.DeviceIdType.MESH
VMEM_LIMIT = 56 * 1024 * 1024
BACKWARD_LIMIT = 63 * 1024 * 1024


def matmul(a, b, contract):
    return lax.dot_general(
        a, b, (((contract[0],), (contract[1],)), ((), ())), preferred_element_type=single
    )


def norm_forward(values, gain_vector, shift_vector):
    centered = values - jnp.mean(values, axis=-1, keepdims=True)
    inverse = lax.rsqrt(jnp.mean(centered * centered, axis=-1, keepdims=True) + epsilon)
    unit_rows = centered * inverse
    return (unit_rows * gain_vector + shift_vector, unit_rows, inverse)


def norm_backward(gradient, unit_rows, inverse, gain_vector):
    inner = gradient * gain_vector
    result = inverse * (
        inner
        - jnp.mean(inner, axis=-1, keepdims=True)
        - unit_rows * jnp.mean(inner * unit_rows, axis=-1, keepdims=True)
    )
    return (result, jnp.sum(gradient * unit_rows, axis=0), jnp.sum(gradient, axis=0))


def two_softmaxes(mapped):
    up = jnp.exp(mapped - jnp.max(mapped, axis=0, keepdims=True))
    down = jnp.exp(jnp.min(mapped, axis=0, keepdims=True) - mapped)
    return (
        up / jnp.sum(up, axis=0, keepdims=True),
        down / jnp.sum(down, axis=0, keepdims=True),
    )


def flat(vector):
    return vector.astype(single).reshape(1, -1)


def with_ones(rows):
    return jnp.concatenate([rows, jnp.ones((16, rows.shape[1]), rows.dtype)], axis=0)


def state_rows(state, micro, micro_count, head_width):
    low = state[micro * head_width : (micro + 1) * head_width, :]
    row = micro_count * head_width + micro
    total = state[row : row + 1, :]
    return jnp.concatenate([low, jnp.broadcast_to(total, (16, low.shape[1]))], axis=0)


def score_grads(grad, attended, denom):
    inverse = 1.0 / denom
    numer_grad = grad * inverse
    denom_grad = -jnp.sum(grad * attended, axis=0, keepdims=True) * inverse
    pad = jnp.zeros((15, grad.shape[1]), single)
    return jnp.concatenate([numer_grad, denom_grad, pad], axis=0)


def feature_backward(feat_grad, source, weights):
    head_width = source.shape[0]
    up, down = two_softmaxes(matmul(weights, source, (0, 0)))
    grad_up, grad_down = (feat_grad[:head_width], feat_grad[head_width:])
    mapped = up * (grad_up - jnp.sum(up * grad_up, axis=0, keepdims=True)) - down * (
        grad_down - jnp.sum(down * grad_down, axis=0, keepdims=True)
    )
    low = mapped.astype(bfloat)
    return (matmul(weights, low, (1, 0)), matmul(source, low, (1, 1)))


def document(position, bounds_ref, m):
    return jnp.where(position >= bounds_ref[0, m], 1, 0) + jnp.where(
        position >= bounds_ref[1, m], 1, 0
    )


def token_masks(bounds_ref, first_row, rows, micro_count, mask_ref, use_ref, last_ref):
    low_shape, line_shape = ((rows, rows), (1, rows))
    source = first_row + lax.broadcasted_iota(jnp.int32, low_shape, 0)
    target = first_row + lax.broadcasted_iota(jnp.int32, low_shape, 1)
    line = first_row + lax.broadcasted_iota(jnp.int32, line_shape, 1)
    for m in range(micro_count):
        part = slice(m * rows, (m + 1) * rows)
        same = document(source, bounds_ref, m) == document(target, bounds_ref, m)
        mask_ref[m] = jnp.where((source <= target) & same, 1.0, 0.0)
        own = document(line, bounds_ref, m)
        use_ref[:, part] = jnp.where(own == document(first_row - 1, bounds_ref, m), 1.0, 0.0)
        last_ref[:, part] = jnp.where(
            own == document(first_row + rows - 1, bounds_ref, m), 1.0, 0.0
        )


def chain_masks(bounds_ref, first_row, low, rows, micro_count, head_width, reverse, mask_ref):
    base = first_row - low * rows
    step = 2 * rows
    height, wide = mask_ref.shape[1:]
    for m in range(micro_count):
        def doc(position, m=m):
            return document(position, bounds_ref, m)

        inner = doc(base + rows - 1)
        if reverse:
            lead = 1 - low
            own_edge, pair, ahead = (doc(first_row - 1), doc(base + step - 1), doc(base - 1))
        else:
            lead = low
            own_edge, pair, ahead = (
                doc(first_row + rows - 1), doc(base - 1), doc(base + step - 1),
            )
        keep = jnp.where(pair == inner, 1.0, 0.0)
        values = [
            jnp.where(pair == ahead, 1.0, 0.0),
            jnp.where(own_edge == ahead, 1.0, 0.0),
            jnp.where(lead == 0, keep, 1.0),
            jnp.where(lead == 0, 1.0, 0.0),
            jnp.where(lead == 0, 1.0, keep),
        ]
        for i, value in enumerate(values):
            mask_ref[i, m * head_width : (m + 1) * head_width, :] = jnp.full(
                (head_width, wide), value
            )
            tail = slice(micro_count * head_width, height)
            row = lax.broadcasted_iota(jnp.int32, (height - tail.start, wide), 0)
            before = jnp.zeros(row.shape, single) if m == 0 else mask_ref[i, tail, :]
            mask_ref[i, tail, :] = jnp.where(lax.rem(row, micro_count) == m, value, before)


CHAIN_RING = 4


class Chain:
    def __init__(self, reverse, count, carry, onward, aside, beside, mask, sems):
        self.carry, self.onward, self.aside, self.beside = carry, onward, aside, beside
        self.mask, self.sems = mask, sems
        place, self.column = (lax.axis_index("seq"), lax.axis_index("batch"))
        high, low = (place // 2, lax.rem(place, 2))
        length = count // 2
        self.lap = length - 1 - high if reverse else high
        self.ahead, self.behind = (place - 2, place + 2) if reverse else (place + 2, place - 2)
        self.partner = place + 1 - 2 * low
        self.first, self.final = (self.lap == 0, self.lap == length - 1)

    def greet(self, barrier):
        def signal(place):
            pl.semaphore_signal(
                barrier, inc=1, device_id=(place, self.column), device_id_type=MESH
            )

        signal(self.partner)

        @pl.when(jnp.logical_not(self.final))
        def _():
            signal(self.ahead)

        @pl.when(jnp.logical_not(self.first))
        def _():
            signal(self.behind)

        return 1 + jnp.where(self.first, 0, 1) + jnp.where(self.final, 0, 1)

    def along(self, i):
        return pltpu.make_async_remote_copy(
            src_ref=self.onward.at[lax.rem(i, CHAIN_RING)], dst_ref=self.carry.at[i], send_sem=self.sems[0].at[i],
            recv_sem=self.sems[1].at[i], device_id=(self.ahead, self.column), device_id_type=MESH,
        )

    def across(self, i):
        return pltpu.make_async_remote_copy(
            src_ref=self.aside.at[lax.rem(i, CHAIN_RING)], dst_ref=self.beside.at[i], send_sem=self.sems[2].at[i],
            recv_sem=self.sems[3].at[i], device_id=(self.partner, self.column),
            device_id_type=MESH,
        )

    def start(self):
        @pl.when(self.first)
        def _():
            self.carry[...] = jnp.zeros_like(self.carry)

    def step(self, i, local):
        @pl.when(jnp.logical_not(self.first))
        def _():
            self.along(i).wait_recv()

        @pl.when(i >= CHAIN_RING)
        def _():
            self.sent(i - CHAIN_RING)

        state, slot = (self.carry[i], lax.rem(i, CHAIN_RING))

        @pl.when(jnp.logical_not(self.final))
        def _():
            self.onward[slot] = self.mask[0] * state + self.mask[1] * local
            self.along(i).start()

        self.aside[slot] = self.mask[2] * state + self.mask[3] * local
        self.across(i).start()

    def sent(self, i):
        self.across(i).wait_send()

        @pl.when(jnp.logical_not(self.final))
        def _():
            self.along(i).wait_send()

    def result(self, i):
        self.across(i).wait_recv()
        return self.mask[4] * self.carry[i] + self.beside[i]

    def drain(self, chunks):
        def one(i, _):
            self.sent(i)
            return 0

        lax.fori_loop(max(chunks - CHAIN_RING, 0), chunks, one, 0)


def local_state(wide, other, micro_count, head_width, target):
    rows = wide.shape[1] // micro_count
    sums = []
    for m in range(micro_count):
        part = slice(m * rows, (m + 1) * rows)
        local = matmul(wide[:, part], other[:, part], (1, 1))
        target[m * head_width : (m + 1) * head_width, :] = local[:head_width]
        sums.append(local[head_width : head_width + 1])
    target[micro_count * head_width :, :] = jnp.concatenate(sums + sums, axis=0)


def forward_kernel(
    count, micro_count, x_ref, gain_ref, shift_ref, weight_ref, bias_ref, qm_ref, km_ref,
    bounds_ref, proj_ref, fq_ref, fk_ref, state_ref, att_ref, low_ref, den_ref, norm_ref, turned_ref,
    normed, bias_row, mask, use, last, chain_mask, local, carry, onward, aside, beside, *sems,
):
    heads, head_width = qm_ref.shape[:2]
    total_rows = x_ref.shape[0]
    rows = total_rows // micro_count
    model_width = x_ref.shape[1]
    pair = 2 * head_width
    place = lax.axis_index("seq")
    first_row = place * rows
    chain = Chain(False, count, carry, onward, aside, beside, chain_mask, sems)
    barrier = pltpu.get_barrier_semaphore()
    greeted = chain.greet(barrier)
    token_masks(bounds_ref, first_row, rows, micro_count, mask, use, last)
    chain_masks(
        bounds_ref, first_row, lax.rem(place, 2), rows, micro_count, head_width, False, chain_mask
    )
    chain.start()
    bias_row[...] = flat(bias_ref[...])
    normed[...] = norm_forward(
        x_ref[...].astype(single), flat(gain_ref[...]), flat(shift_ref[...])
    )[0].astype(bfloat)
    pl.semaphore_wait(barrier, greeted)
    norm_ref[...] = normed[...].T
    turned_ref[...] = x_ref[...].T

    def project(p):
        for part in range(3):
            columns = pl.ds(pl.multiple_of(part * model_width + p * pair, pair), pair)
            value = matmul(normed[...], weight_ref[:, columns], (1, 0))
            value = (value + bias_row[:, columns]).astype(bfloat).T
            proj_ref[part * heads + 2 * p] = value[:head_width]
            proj_ref[part * heads + 2 * p + 1] = value[head_width:]

    def features(h):
        for offset, weights, target in ((0, qm_ref, fq_ref), (heads, km_ref, fk_ref)):
            mapped = matmul(weights[h], proj_ref[offset + h], (0, 0))
            up, down = two_softmaxes(mapped)
            target[h] = jnp.concatenate([up, down], axis=0).astype(bfloat)
        wide = with_ones(proj_ref[2 * heads + h]) * last[...].astype(bfloat)
        local_state(wide, fk_ref.at[h], micro_count, head_width, local.at[h])

    def attend(h):
        state_ref[h] = chain.result(h)
        wide = with_ones(proj_ref[2 * heads + h])
        used = fq_ref[h] * use[...].astype(bfloat)
        for m in range(micro_count):
            part = slice(m * rows, (m + 1) * rows)
            scores = matmul(fk_ref[h, :, part], fq_ref[h, :, part], (0, 0)) * mask[m]
            state = state_rows(state_ref.at[h], m, micro_count, head_width).astype(bfloat)
            numer = matmul(wide[:, part], scores.astype(bfloat), (1, 0)) + matmul(
                state, used[:, part], (1, 0)
            )
            denom = numer[head_width : head_width + 1]
            attended = numer[:head_width] / denom
            att_ref[h, :, part] = attended
            low_ref[h, :, part] = attended.astype(bfloat)
            den_ref[h, :, part] = denom

    def one_round(r, _):
        @pl.when((r < heads) & (lax.rem(r, 2) == 0))
        def _():
            project(r // 2)

        @pl.when(r < heads)
        def _():
            features(r)

        @pl.when((r >= chain.lap) & (r < heads + chain.lap))
        def _():
            chain.step(r - chain.lap, local[r - chain.lap])

        @pl.when(r >= chain.lap + 1)
        def _():
            attend(r - chain.lap - 1)

        return 0

    lax.fori_loop(0, heads + chain.lap + 1, one_round, 0)
    chain.drain(heads)


def forward_attention(x, gain, shift, weight, bias, query_map, key_map, bounds, count):
    total_rows, model_width = x.shape
    heads, head_width = query_map.shape[:2]
    micro_count = bounds.shape[0]
    rows = total_rows // micro_count
    height = micro_count * (head_width + 2)
    chunk = (heads, height, 2 * head_width)
    whole = pl.BlockSpec(memory_space=pltpu.VMEM)
    head = (heads, head_width, total_rows)
    feat = (heads, 2 * head_width, total_rows)
    shape = jax.ShapeDtypeStruct
    return pl.pallas_call(
        partial(forward_kernel, count, micro_count),
        out_shape=[
            shape((3 * heads,) + head[1:], bfloat), shape(feat, bfloat), shape(feat, bfloat),
            shape(chunk, single), shape(head, single), shape(head, bfloat),
            shape((heads, 1, total_rows), single), shape((model_width, total_rows), bfloat),
            shape((model_width, total_rows), bfloat),
        ],
        in_specs=[whole] * 7 + [pl.BlockSpec(memory_space=pltpu.SMEM)],
        out_specs=[whole] * 9,
        scratch_shapes=[
            pltpu.VMEM((total_rows, model_width), bfloat),
            pltpu.VMEM((1, 3 * model_width), single),
            pltpu.VMEM((micro_count, rows, rows), single),
            pltpu.VMEM((1, total_rows), single),
            pltpu.VMEM((1, total_rows), single),
            pltpu.VMEM((5,) + chunk[1:], single),
        ]
        + [pltpu.VMEM(chunk, single)] * 2
        + [pltpu.VMEM((CHAIN_RING,) + chunk[1:], single)] * 2
        + [pltpu.VMEM(chunk, single)]
        + [pltpu.SemaphoreType.DMA((heads,))] * 4,
        compiler_params=pltpu.CompilerParams(
            collective_id=1, has_side_effects=True, vmem_limit_bytes=VMEM_LIMIT
        ),
    )(
        x, gain, shift, weight, bias, query_map, key_map, bounds.T,
    )


def remote(src, dst, send, recv, device):
    return pltpu.make_async_remote_copy(
        src_ref=src, dst_ref=dst, send_sem=send, recv_sem=recv, device_id=device,
        device_id_type=MESH,
    )


FIRST, FIRST_ROWS, SECOND_ROWS = (8, 32, 32)


class Spot:
    def __init__(self, count, lines):
        self.place, self.column = (lax.axis_index("seq"), lax.axis_index("batch"))
        self.high, self.low = (self.place // 2, lax.rem(self.place, 2))
        self.across, self.core = (self.column // 2, lax.rem(self.column, 2))
        self.length, self.lines = (count // 2, lines)
        self.at_core = (self.place, self.column + 1 - 2 * self.core)
        self.at_y = (self.place + 1 - 2 * self.low, self.column)
        self.at_right, self.at_left = ((self.place + 2, self.column), (self.place - 2, self.column))
        self.not_first, self.not_last = (self.high > 0, self.high < self.length - 1)

    def line(self, d):
        other = lax.rem(self.across + d, self.lines)
        return other, (self.place, other * 2 + self.core)

    def along(self, d):
        count = 2 * self.length
        other = lax.rem(self.place + d, count)
        return other, (other, self.column)

    def greet(self, barrier):
        devices = [self.at_core]
        devices += [self.line(d)[1] for d in range(1, self.lines)]
        devices += [self.along(d)[1] for d in range(1, 2 * self.length)]
        other = self.at_core[1]
        devices += [(self.along(d)[0], other) for d in range(1, 2 * self.length)]
        for device in devices:
            pl.semaphore_signal(barrier, inc=1, device_id=device, device_id_type=MESH)
        return len(devices)


class Track:
    def __init__(
        self, spot, base, halved, rows, offset, ring, out, own, got, y_got, z_got, x_got, sems
    ):
        self.base = base
        self.spot, self.halved, self.rows, self.offset, self.ring = spot, halved, rows, offset, ring
        self.out, self.own, self.got, self.y_got, self.z_got, self.x_got = (
            out, own, got, y_got, z_got, x_got,
        )
        (
            self.load_sem, self.core_send, self.core_recv, self.y_send, self.y_recv, self.zr_send,
            self.zr_recv, self.zl_send, self.zl_recv, self.x_send, self.x_recv, self.back_send,
            self.back_recv,
        ) = sems
        half = own.shape[-1]
        self.mine = pl.ds(pl.multiple_of(spot.core * half, 128), half)
        self.theirs = pl.ds(pl.multiple_of((1 - spot.core) * half, 128), half)
        self.part = rows // spot.lines if halved else rows
        self.strip = self.window(spot.across) if halved else slice(None)

    def window(self, line, base=0):
        return pl.ds(pl.multiple_of(base + line * self.part, 8), self.part)

    def source(self, ref, col, columns):
        half = self.own.shape[-1]
        cols = pl.ds(pl.multiple_of(col + columns * half, 128), half)
        return ref.at[:, :, pl.ds(self.offset, self.rows), cols]

    def give(self, u, source):
        return remote(
            source, self.got.at[lax.rem(u, self.ring)], self.core_send.at[u],
            self.core_recv.at[u], self.spot.at_core,
        )

    def begin(self, u, ref, col):
        self.give(u, self.source(ref, col, 1 - self.spot.core)).start()
        pltpu.make_async_copy(
            self.source(ref, col, self.spot.core), self.own.at[u], self.load_sem.at[u]
        ).start()

    def settle(self, u):
        pltpu.make_async_copy(self.own.at[u], self.own.at[u], self.load_sem.at[u]).wait()
        self.give(u, self.own.at[u]).wait_recv()
        self.own[u] = self.own[u] + self.got[lax.rem(u, self.ring)]

    def given(self, u):
        self.give(u, self.own.at[u]).wait_send()

    def cut(self, u, d):
        other, device = self.spot.line(d)
        return remote(
            self.own.at[u, :, :, self.window(other)], self.x_got.at[u, d - 1],
            self.x_send.at[u, 0, d - 1], self.x_recv.at[u, 0, d - 1], device,
        )

    def first(self, u):
        self.settle(u)
        if self.halved:
            for d in range(1, self.spot.lines):
                self.cut(u, d).start()
        else:
            self.y_copy(u).start()

    def cut_taken(self, u):
        for d in range(1, self.spot.lines):
            self.cut(u, d).wait_recv()
            target = self.own.at[u, :, :, self.strip]
            target[...] = target[...] + self.x_got[u, d - 1]
        self.y_copy(u).start()

    def y_copy(self, u):
        return remote(
            self.own.at[u, :, 1 - self.spot.low, self.strip], self.y_got.at[u],
            self.y_send.at[u], self.y_recv.at[u], self.spot.at_y,
        )

    def y_taken(self, u):
        self.y_copy(u).wait_recv()
        target = self.own.at[u, :, self.spot.low, self.strip]
        target[...] = target[...] + self.y_got[u]
        self.z_step(u, 1)

    def block(self, u, h):
        return self.own.at[u, h, self.spot.low, self.strip]

    def right(self, u, k):
        return remote(
            self.block(u, k), self.z_got.at[u, k], self.zr_send.at[u, k], self.zr_recv.at[u, k],
            self.spot.at_right,
        )

    def left(self, u, k, taker):
        slot = jnp.where(k == taker, self.spot.length, k)
        return remote(
            self.block(u, k), self.z_got.at[u, slot], self.zl_send.at[u, k], self.zl_recv.at[u, k],
            self.spot.at_left,
        )

    def take_right(self, u, k):
        self.right(u, k).wait_recv()
        target = self.block(u, k)
        target[...] = target[...] + self.z_got[u, k]

    def take_left(self, u, k):
        high = self.spot.high
        self.left(u, k, high).wait_recv()
        target = self.block(u, k)
        target[...] = target[...] + self.z_got[u, jnp.where(k == high, self.spot.length, k)]

    def z_step(self, u, t):
        spot = self.spot
        k = spot.high + spot.length - t

        @pl.when(spot.high <= t - 1)
        def _():
            if t > 1:
                @pl.when(spot.not_first)
                def _():
                    self.take_right(u, k)

            self.right(u, k).start()

        j = spot.high - spot.length + t

        @pl.when(spot.high >= spot.length - t)
        def _():
            if t > 1:
                @pl.when(spot.not_last)
                def _():
                    self.take_left(u, j)

            self.left(u, j, spot.high - 1).start()

    def z_end(self, u):
        @pl.when(self.spot.not_first)
        def _():
            self.take_right(u, self.spot.high)

        @pl.when(self.spot.not_last)
        def _():
            self.take_left(u, self.spot.high)

    def x_copy(self, u, d):
        return remote(
            self.block(u, self.spot.high), self.x_got.at[u, d - 1], self.x_send.at[u, 0, d - 1],
            self.x_recv.at[u, 0, d - 1], self.spot.line(d)[1],
        )

    def x_back(self, u, d):
        rows = self.window(self.spot.across, self.offset)
        return remote(
            self.block(u, self.spot.high), self.out.at[self.base + u, rows, self.mine],
            self.x_send.at[u, 1, d - 1], self.x_recv.at[u, 1, d - 1], self.spot.line(d)[1],
        )

    def keep(self, u):
        rows = (
            self.window(self.spot.across, self.offset)
            if self.halved
            else pl.ds(self.offset, self.rows)
        )
        return pltpu.make_async_copy(
            self.block(u, self.spot.high), self.out.at[self.base + u, rows, self.mine], self.load_sem.at[u]
        )

    def reduced(self, u):
        self.z_end(u)
        if self.halved:
            self.keep(u).start()
        for d in range(1, self.spot.lines):
            (self.x_back if self.halved else self.x_copy)(u, d).start()

    def back(self, u):
        block = self.out.at[self.base + u, pl.ds(self.offset, self.rows), self.mine]
        source = block if self.halved else self.block(u, self.spot.high)
        return remote(source, block, self.back_send.at[u], self.back_recv.at[u], self.spot.at_core)

    def total(self, u):
        spot = self.spot
        for d in range(1, spot.lines):
            self.x_copy(u, d).wait()
        value = self.block(u, spot.high)[...]
        if spot.lines == 2:
            value = value + self.x_got[u, 0]
        else:
            parts = []
            for x in range(spot.lines):
                slot = lax.rem(spot.across - x + spot.lines - 1, spot.lines)
                slot = jnp.minimum(slot, spot.lines - 2)
                parts.append(jnp.where(x == spot.across, value, self.x_got[u, slot]))
            value = sum(parts[1:], parts[0])
        self.block(u, spot.high)[...] = value

    def done(self, u):
        if self.halved:
            for d in range(1, self.spot.lines):
                self.x_back(u, d).wait_recv()
            self.keep(u).wait()
        else:
            self.total(u)
            self.keep(u).start()
        self.back(u).start()

    def finish(self, u):
        self.back(u).wait()
        if not self.halved:
            self.keep(u).wait()

    def steps(self):
        z_steps = [partial(self.z_step, t=t) for t in range(2, self.spot.length)]
        cut = [self.cut_taken] if self.halved else []
        return [self.first] + cut + [self.y_taken] + z_steps + [self.reduced, self.done]

    def drain(self, u):
        self.y_copy(u).wait_send()
        for d in range(1, self.spot.lines):
            if self.halved:
                self.cut(u, d).wait_send()
                self.x_back(u, d).wait_send()

        def right_one(k, _):
            self.right(u, k).wait_send()
            return 0

        def left_one(k, _):
            self.left(u, k, self.spot.high - 1).wait_send()
            return 0

        lax.fori_loop(self.spot.high + 1, self.spot.length, right_one, 0)
        lax.fori_loop(0, self.spot.high, left_one, 0)


def bands(units, share, lines):
    groups = []
    for low, high, direct in ((0, FIRST, FIRST_ROWS), (FIRST, units, SECOND_ROWS)):
        direct = direct * share // 96
        if direct % 8 or (share - direct) % (8 * lines):
            return [(0, units, share, 0)]
        groups.append((low, high, direct, share - direct))
    return groups


def track_scratch(units, length, lines, rows, halved, ring, half):
    part = rows // lines if halved else rows
    DMA = pltpu.SemaphoreType.DMA
    others = lines - 1
    buffers = [
        pltpu.VMEM((units, length, 2, rows, half), single),
        pltpu.VMEM((ring, length, 2, rows, half), single),
        pltpu.VMEM((units, length, part, half), single),
        pltpu.VMEM((units, length + 1, part, half), single),
        pltpu.VMEM((units, others) + ((length, 2) if halved else ()) + (part, half), single),
    ]
    line = DMA((units, length))
    ends = DMA((units, 2, others))
    one = DMA((units,))
    return buffers + [one] * 5 + [line] * 4 + [ends] * 2 + [one] * 2


BEAT = 2


def unit_order(early, late, gap, length):
    order, starts, left = ([], [], list(range(early)))
    ready = {length + 2 + gap * g: early + g for g in range(late)}
    t = 0
    while len(order) < early + late:
        if t in ready or left:
            order.append(ready[t] if t in ready else left.pop(0))
            starts.append(t)
        t += 1
    return order, starts


def backward_kernel(
    count, lines, micro_count, early, proj_hbm, fq_hbm, fk_hbm, state_hbm, att_hbm, den_hbm,
    grad_hbm, qm_ref, km_ref, norm_ref, weight_ref, x_ref, mid_ref, gain_ref, vector_ref,
    bounds_ref, contract_ref, expand_ref, output_ref, out, in_grad_ref, qm_out, km_out, rows_out, bias_out, expand_bias_out,
    proj, fq_buf, fk_buf, state_buf, att_buf, den_buf, grad_buf, load_sem, pg_ref,
    mask, use, last, chain_mask, local, carry, onward, aside, beside, fqg, fkg, product, small,
    small_sum, small_out, gather_send, gather_recv, gather_keep, credit, *rest,
):
    heads, head_width = qm_ref.shape[:2]
    total_rows = pg_ref.shape[-1]
    rows = total_rows // micro_count
    model_width = heads * head_width
    sources = (contract_ref, expand_ref, output_ref)
    share, wide = out.shape[1:]
    group = wide // (3 * head_width)
    late = heads // group
    units = len(early) + late
    spot = Spot(count, lines)
    length = spot.length
    order, starts = unit_order(len(early), late, group // BEAT, length)
    chain_sems, rest = (rest[:4], rest[4:])
    chain = Chain(True, count, carry, onward, aside, beside, chain_mask, chain_sems)
    ring, half = (2, wide // 2)
    little = Track(spot, 0, False, small.shape[2], 0, 1, small_sum, *rest[:5], rest[5:18])
    rest = rest[18:]
    groups = []
    for low, high, direct, halved in bands(units, share, lines):
        group_tracks = []
        for kind, band, offset in ((False, direct, 0), (True, halved, direct)):
            if band:
                group_tracks.append(
                    Track(spot, low, kind, band, offset, ring, out, *rest[:5], rest[5:18])
                )
                rest = rest[18:]
        groups.append((low, high, group_tracks))
    slots = proj.shape[0]

    def loads(h):
        slot = lax.rem(h, slots)
        pairs = [(proj_hbm.at[:, h], proj.at[slot])]
        for source, target in (
            (fq_hbm, fq_buf), (fk_hbm, fk_buf), (state_hbm, state_buf), (att_hbm, att_buf),
            (den_hbm, den_buf), (grad_hbm, grad_buf),
        ):
            pairs.append((source.at[h], target.at[slot]))
        return [
            pltpu.make_async_copy(source, target, load_sem.at[slot, i])
            for i, (source, target) in enumerate(pairs)
        ]

    for h in range(BEAT):
        for copy in loads(h):
            copy.start()
    barrier = pltpu.get_barrier_semaphore()
    greeted = spot.greet(barrier)
    pl.semaphore_wait(barrier, greeted)

    def tracks_of(u):
        return [t for low, high, tracks in groups for t in tracks if low <= u < high]

    def begin(u):
        if u >= ring:
            pl.semaphore_wait(credit, 1)
        if order[u] < len(early):
            array, lead, col = early[order[u]]
            ref = sources[array]
            ref = ref if lead is None else ref.at[:, :, lead]
        else:
            ref, col = (product, 0)
        for track in tracks_of(u):
            track.begin(u - track.base, ref, col)

    def settled(u):
        @pl.when(u + ring < units)
        def _():
            pl.semaphore_signal(credit, inc=1, device_id=spot.at_core, device_id_type=MESH)

    def state_grad(h):
        for copy in loads(h):
            copy.wait()
        slot = lax.rem(h, slots)
        wide_grad = score_grads(grad_buf[slot], att_buf[slot], den_buf[slot]) * use[...]
        local_state(wide_grad.astype(bfloat), fq_buf.at[slot], micro_count, head_width, local)

    def attend_back(h):
        slot = lax.rem(h, slots)
        beside[h] = chain.result(h)
        grads = score_grads(grad_buf[slot], att_buf[slot], den_buf[slot])
        low_grads = grads.astype(bfloat)
        used_grads = (grads * use[...]).astype(bfloat)
        last_low = last[...].astype(bfloat)
        wide_value = with_ones(proj[slot, 2])
        wide_last = wide_value * last_low
        for m in range(micro_count):
            part = slice(m * rows, (m + 1) * rows)
            fq, fk = (fq_buf[slot, :, part], fk_buf[slot, :, part])
            scores = (matmul(fk, fq, (0, 0)) * mask[m]).astype(bfloat)
            grad_scores = (
                matmul(wide_value[:, part], low_grads[:, part], (0, 0)) * mask[m]
            ).astype(bfloat)
            state = state_rows(state_buf.at[slot], m, micro_count, head_width).astype(bfloat)
            out_grad = state_rows(beside.at[h], m, micro_count, head_width)
            row = lax.broadcasted_iota(jnp.int32, out_grad.shape, 0)
            out_grad = jnp.where(row <= head_width, out_grad, 0.0).astype(bfloat)
            fqg[:, part] = matmul(fk, grad_scores, (1, 0)) + matmul(
                state, used_grads[:, part], (0, 0)
            )
            fkg[:, part] = matmul(fq, grad_scores, (1, 1)) + matmul(
                out_grad, wide_last[:, part], (0, 0)
            )
            value_grad = matmul(low_grads[:head_width, part], scores, (1, 1)) + matmul(
                out_grad[:head_width], fk * last_low[:, part], (1, 0)
            )
            pg_ref[2, h, :, part] = value_grad.astype(bfloat)
        q_grad, qmg = feature_backward(fqg[...], proj[slot, 0], qm_ref[h])
        pg_ref[0, h] = q_grad.astype(bfloat)
        qm_out[h] = qmg
        k_grad, kmg = feature_backward(fkg[...], proj[slot, 1], km_ref[h])
        pg_ref[1, h] = k_grad.astype(bfloat)
        km_out[h] = kmg

    def late_begin(g):
        if g > 0:
            u = order.index(len(early) + g - 1)
            for track in tracks_of(u):
                track.given(u - track.base)
        columns = group * head_width
        for p in range(3):
            low = pg_ref[p, g * group : (g + 1) * group].reshape(columns, -1)
            value = matmul(norm_ref[...], low, (1, 1))
            product[:, :, :, p * columns : (p + 1) * columns] = value.reshape(
                product.shape[:3] + (columns,)
            )
        begin(order.index(len(early) + g))

    def input_back():
        gain_sum, bias_sum = (0.0, 0.0)
        gain = jnp.broadcast_to(flat(gain_ref[...]), (128, model_width)).T[:, :1]
        step = 2 * rows
        for start in range(0, total_rows, step):
            part = slice(start, start + step)
            grad = sum(
                matmul(
                    weight_ref[:, p * model_width : (p + 1) * model_width],
                    pg_ref[p, :, :, part].reshape(model_width, step), (1, 0),
                )
                for p in range(3)
            )
            value = x_ref[:, part].astype(single)
            value = value - jnp.mean(value, axis=0, keepdims=True)
            inverse = lax.rsqrt(jnp.mean(value * value, axis=0, keepdims=True) + epsilon)
            value = value * inverse
            inner = grad * gain
            result = mid_ref[:, part] + inverse * (
                inner
                - jnp.mean(inner, axis=0, keepdims=True)
                - value * jnp.mean(inner * value, axis=0, keepdims=True)
            )
            in_grad_ref[part, :] = result.T.astype(bfloat)
            gain_sum += jnp.sum((grad * value).T, axis=0, keepdims=True)
            bias_sum += jnp.sum(grad.T, axis=0, keepdims=True)
        ones = jnp.ones((16, total_rows), bfloat)
        sums = [
            matmul(ones, pg_ref[p].reshape(model_width, total_rows), (1, 1))[:1] for p in range(3)
        ]
        blank = jnp.zeros((4, model_width), single)
        vectors = vector_ref[...] + jnp.concatenate(
            [gain_sum, bias_sum, blank] + sums + [blank, blank[:3]], axis=0
        )
        maps = [
            jnp.concatenate([ref[h] for h in range(heads)], axis=1) for ref in (qm_out, km_out)
        ]
        size = small.shape[0] * small.shape[1] * small.shape[2]
        used = 2 * head_width + vectors.shape[0]
        pad = [jnp.zeros((size - used, model_width), single)] if size > used else []
        small[...] = jnp.concatenate(maps + [vectors] + pad, axis=0).reshape(small.shape)
        little.begin(0, small, 0)

    others = [(d, 0) for d in range(1, count)] + [(d, 1) for d in range(count)]

    def spread(k, incoming):
        d, other_core = others[k]
        here, there = (spot.place, lax.rem(spot.place + d, count))
        core = lax.rem(spot.core + other_core, 2)
        device = (there, 2 * spot.across + core)
        side = pl.ds(pl.multiple_of((core if incoming else spot.core) * half, 128), half)
        place, its_core = (there, core) if incoming else (here, spot.core)
        return remote(
            little.block(0, spot.high), small_out.at[place, :, side], gather_send.at[k],
            gather_recv.at[place, its_core], device,
        )

    def spread_keep():
        return pltpu.make_async_copy(
            little.block(0, spot.high), small_out.at[spot.place, :, little.mine],
            gather_keep.at[0],
        )

    def little_done(u):
        little.total(u)
        spread_keep().start()
        for k in range(len(others)):
            spread(k, False).start()

    little_steps = little.steps()[:-1] + [little_done]
    stages = [
        (s, f, low, high)
        for low, high, tracks in groups
        for track in tracks
        for s, f in enumerate(track.steps())
    ]
    stages.sort(key=lambda s: (s[0], s[2]))
    ahead = 1
    for u in range(ahead):
        begin(u)
    first_row = spot.place * rows
    token_masks(bounds_ref, first_row, rows, micro_count, mask, use, last)
    chain_masks(
        bounds_ref, first_row, spot.low, rows, micro_count, head_width, True, chain_mask
    )
    chain.start()

    def unit_at(t):
        if starts == list(range(units)):
            return t, (t >= 0) & (t < units)
        u, valid = (0, False)
        for start in starts:
            u = u + jnp.where(t > start, 1, 0)
            valid = valid | (t == start)
        return u, valid

    beats = heads // BEAT

    def one_round(r, _):
        c = r - chain.lap

        @pl.when((c >= 0) & (c < beats))
        def _():
            for i in range(BEAT):
                h = c * BEAT + i
                state_grad(h)
                chain.step(h, local[...])

        for u in range(ahead, units):
            if order[u] < len(early):
                @pl.when(r == starts[u] - ahead)
                def _(u=u):
                    begin(u)

        for lag, step, low, high in stages:
            u, valid = unit_at(r - lag)

            @pl.when(valid & (u >= low) & (u < high))
            def _(u=u, step=step, low=low):
                step(u - low)

        u, valid = unit_at(r)

        @pl.when(valid)
        def _():
            settled(u)

        for s, step in enumerate(little_steps):
            @pl.when(r == beats + length + 1 + s)
            def _(step=step):
                step(0)

        @pl.when((c >= 1) & (c <= beats))
        def _():
            for i in range(BEAT):
                attend_back((c - 1) * BEAT + i)

        @pl.when((c >= 0) & (c + 1 < beats))
        def _():
            for i in range(BEAT):
                for copy in loads((c + 1) * BEAT + i):
                    copy.start()

        for g in range(late):
            u = order.index(len(early) + g)

            @pl.when(r == starts[u] - 1)
            def _(g=g):
                late_begin(g)

        @pl.when(r == beats + length)
        def _():
            input_back()

        return 0

    rounds = max(starts[-1] + stages[-1][0] + 1, beats + length + 1 + len(little_steps))
    lax.fori_loop(0, rounds, one_round, 0)

    for u in range(units):
        for track in tracks_of(u):
            track.finish(u - track.base)
    chain.drain(heads)
    little.drain(0)
    little.given(0)
    spread_keep().wait()
    for k in range(len(others)):
        spread(k, False).wait_send()
        spread(k, True).wait_recv()

    sums = small_out[...].reshape(-1, model_width)
    for h in range(heads):
        part = slice(h * head_width, (h + 1) * head_width)
        qm_out[h] = sums[:head_width, part]
        km_out[h] = sums[head_width : 2 * head_width, part]
    row = 2 * head_width
    rows_out[...] = sums[row : row + 8]
    row += 6
    for target in (bias_out, expand_bias_out):
        for start in range(0, target.shape[0], model_width):
            target[start : start + model_width] = sums[row]
            row += 1

    for low, high, tracks in groups:
        def drain(v, _, tracks=tracks):
            for track in tracks:
                track.drain(v)
            return 0

        lax.fori_loop(0, high - low, drain, 0)
    for u in range(units):
        if order[u] < len(early) or order[u] == units - 1:
            for track in tracks_of(u):
                track.given(u - track.base)


def backward_attention(
    projected, feat_query, feat_key, state_in, attended, denominator, attended_grad, query_map,
    key_map, normed_rows, weight, input_rows, middle_grad_rows, gain, vectors, bounds,
    contract_grad, expand_grad, output_grad, count, lines,
):
    heads, head_width = query_map.shape[:2]
    model_width, total_rows = normed_rows.shape
    micro_count = bounds.shape[0]
    rows = total_rows // micro_count
    length = count // 2
    share = model_width // count
    chunk = state_in.shape
    early = [(0, u, 0) for u in range(contract_grad.shape[2])]
    early += [(1, None, c) for c in range(0, expand_grad.shape[3], model_width)]
    early += [(2, None, 0)]
    units = len(early) + 3
    shape = jax.ShapeDtypeStruct
    whole = pl.BlockSpec(memory_space=pltpu.VMEM)
    anywhere = pl.BlockSpec(memory_space=pl.ANY)
    DMA = pltpu.SemaphoreType.DMA
    half = model_width // 2
    used = 2 * head_width + vectors.shape[0]
    little = -(-used // (8 * count)) * 8
    tracks = track_scratch(1, length, lines, little, False, 1, half)
    for low, high, direct, halved in bands(units, share, lines):
        for kind, band in ((False, direct), (True, halved)):
            if band:
                tracks += track_scratch(high - low, length, lines, band, kind, 2, half)
    slots = 2 * BEAT
    head, feat = ((slots, head_width, total_rows), (slots, 2 * head_width, total_rows))
    return pl.pallas_call(
        partial(backward_kernel, count, lines, micro_count, early),
        out_shape=[
            shape((units, share, model_width), single), shape((total_rows, model_width), bfloat),
            shape(query_map.shape, single), shape(key_map.shape, single),
        ]
        + [shape((8, model_width), single)]
        + [shape((3 * model_width,), single), shape((expand_grad.shape[3],), single)],
        in_specs=[anywhere] * 7
        + [whole] * 8
        + [pl.BlockSpec(memory_space=pltpu.SMEM)]
        + [anywhere] * 3,
        out_specs=[anywhere] + [whole] * 6,
        scratch_shapes=[
            pltpu.VMEM((slots, 3) + head[1:], bfloat),
            pltpu.VMEM(feat, bfloat),
            pltpu.VMEM(feat, bfloat),
            pltpu.VMEM((slots,) + chunk[1:], single),
            pltpu.VMEM(head, single),
            pltpu.VMEM((slots, 1, total_rows), single),
            pltpu.VMEM(head, single),
            DMA((slots, 7)),
            pltpu.VMEM((3, heads, head_width, total_rows), bfloat),
            pltpu.VMEM((micro_count, rows, rows), single),
            pltpu.VMEM((1, total_rows), single),
            pltpu.VMEM((1, total_rows), single),
            pltpu.VMEM((5,) + chunk[1:], single),
            pltpu.VMEM(chunk[1:], single),
        ]
        + [pltpu.VMEM(chunk, single)]
        + [pltpu.VMEM((CHAIN_RING,) + chunk[1:], single)] * 2
        + [pltpu.VMEM(chunk, single)]
        + [pltpu.VMEM(feat[1:], single)] * 2
        + [
            pltpu.VMEM((length, 2, share, model_width), single),
            pltpu.VMEM((length, 2, little, model_width), single),
            pltpu.VMEM((1, little, model_width), single),
            pltpu.VMEM((count, little, model_width), single),
            DMA((2 * count - 1,)),
            DMA((count, 2)),
            DMA((1,)),
            pltpu.SemaphoreType.REGULAR,
        ]
        + [DMA((heads,))] * 4
        + tracks,
        compiler_params=pltpu.CompilerParams(
            collective_id=2, has_side_effects=True, vmem_limit_bytes=BACKWARD_LIMIT
        ),
    )(
        projected, feat_query, feat_key, state_in, attended, denominator, attended_grad, query_map,
        key_map, normed_rows, weight, input_rows, middle_grad_rows,
        gain, vectors, bounds.T, contract_grad, expand_grad,
        output_grad,
    )


def feed_kernel(
    att_ref, x_ref, grad_ref, out_weight_ref, out_bias_ref, gain_ref, shift_ref, contract_bias_ref,
    expand_ref, expand_bias_ref, contract_ref,
    result_ref, contract_grad_ref, expand_grad_ref, output_grad_ref, att_grad_ref, mid_grad_ref,
    vector_ref, unit, inverse, low, turned, total, back,
):
    step, steps = (pl.program_id(0), pl.num_programs(0))
    out_bias, gain, shift, contract_bias = (
        flat(ref[...]) for ref in (out_bias_ref, gain_ref, shift_ref, contract_bias_ref)
    )
    wide = x_ref.shape[1]
    columns = pl.ds(pl.multiple_of(step * wide, wide), wide)

    @pl.when(step == 0)
    def _():
        branch = matmul(att_ref[...], out_weight_ref[...], (0, 0)) + out_bias
        middle = x_ref[...].astype(single) + branch
        normed, unit_rows, factor = norm_forward(middle, gain, shift)
        unit[...] = unit_rows
        inverse[...] = factor
        low[...] = normed.astype(bfloat)
        turned[...] = normed.astype(bfloat).T
        total[...] = middle + contract_bias
        back[...] = jnp.zeros_like(back)
        vector_ref[...] = jnp.zeros_like(vector_ref)

    expanded = matmul(low[...], expand_ref[...], (1, 0)) + flat(expand_bias_ref[columns])
    slope = 0.7978845608028654
    square = expanded * expanded
    bend = jnp.tanh(slope * expanded * (1.0 + 0.044715 * square))
    half = 0.5 * (1.0 + bend)
    hidden = (expanded * half).astype(bfloat)
    derivative = half + expanded * (0.5 * slope) * (1.0 - bend * bend) * (
        1.0 + 3.0 * 0.044715 * square
    )
    hidden_grad = matmul(grad_ref[...], contract_ref[...], (1, 1)) * derivative
    low_grad = hidden_grad.astype(bfloat)
    total[...] += matmul(hidden, contract_ref[...], (1, 0))
    back[...] += matmul(low_grad, expand_ref[...], (1, 1))
    expand_grad_ref[...] = matmul(turned[...], low_grad, (1, 0))
    contract_grad_ref[...] = matmul(hidden, grad_ref[...], (0, 0))
    bias_sum = jnp.sum(low_grad.astype(single), axis=0, keepdims=True)
    row = lax.broadcasted_iota(jnp.int32, vector_ref.shape, 0)
    vector_ref[...] = jnp.where(row == 9 + step, bias_sum, vector_ref[...])

    @pl.when(step == steps - 1)
    def _():
        result_ref[...] = total[...].astype(bfloat)
        wide_grad = grad_ref[...].astype(single)
        mid, gain_sum, shift_sum = norm_backward(back[...], unit[...], inverse[...], gain)
        mid = wide_grad + mid
        branch = mid.astype(bfloat)
        mid_grad_ref[...] = mid.T
        att_grad_ref[...] = matmul(out_weight_ref[...], branch, (1, 1))
        output_grad_ref[...] = matmul(att_ref[...], branch, (1, 0))
        sums = [
            gain_sum[None],
            shift_sum[None],
            jnp.sum(branch.astype(single), axis=0, keepdims=True),
            jnp.sum(wide_grad, axis=0, keepdims=True),
        ]
        height, wide = vector_ref.shape
        vector_ref[...] += jnp.concatenate(
            [jnp.zeros((2, wide), single)] + sums + [jnp.zeros((height - 6, wide), single)], axis=0
        )


def feed_forward(
    att, x, grad, output_weight, output_bias, gain, shift, expand_weight, expand_bias,
    contract_weight, contract_bias,
):
    total_rows, wide = x.shape
    steps = expand_weight.shape[1] // wide
    shape = jax.ShapeDtypeStruct
    whole = pl.BlockSpec(memory_space=pltpu.VMEM)
    square = (wide, wide)
    by_row, by_column = (lambda i: (i, 0), lambda i: (0, i))
    return pl.pallas_call(
        feed_kernel,
        grid=(steps,),
        out_shape=[
            shape((total_rows, wide), bfloat), shape((steps * wide, wide), single),
            shape((wide, steps * wide), single), shape(square, single),
            shape((wide, total_rows), single), shape((wide, total_rows), single),
            shape((16, wide), single),
        ],
        in_specs=[whole] * 8
        + [pl.BlockSpec(square, by_column), whole, pl.BlockSpec(square, by_row)],
        out_specs=[
            whole, pl.BlockSpec(square, by_row), pl.BlockSpec(square, by_column), whole, whole,
            whole, whole,
        ],
        scratch_shapes=[
            pltpu.VMEM((total_rows, wide), single),
            pltpu.VMEM((total_rows, 1), single),
            pltpu.VMEM((total_rows, wide), bfloat),
            pltpu.VMEM((wide, total_rows), bfloat),
            pltpu.VMEM((total_rows, wide), single),
            pltpu.VMEM((total_rows, wide), single),
        ],
        compiler_params=pltpu.CompilerParams(vmem_limit_bytes=VMEM_LIMIT),
    )(
        att, x, grad, output_weight, output_bias, gain, shift, contract_bias, expand_weight,
        expand_bias, contract_weight,
    )


def per_device(
    inputs, gain_one, bias_one, project_weight, project_bias, query_map, key_map, output_weight,
    output_bias, gain_two, bias_two, expand_weight, expand_bias, contract_weight, contract_bias,
    bounds, cotangent,
):
    micro_count, row_count, model_width = inputs.shape
    head_count, head_width = (query_map.shape[0], query_map.shape[1])
    total_rows = micro_count * row_count
    count = lax.axis_size("seq")
    flat_input = inputs.reshape(total_rows, model_width)
    (
        projected, feat_query, feat_key, state_in, attended, attended_low, denominator,
        normed_rows, input_rows,
    ) = forward_attention(
        flat_input, gain_one, bias_one, project_weight,
        project_bias, query_map, key_map, bounds, count,
    )
    attended_low = attended_low.reshape(model_width, total_rows)

    lines = lax.axis_size("batch") // 2
    share = model_width // count
    tiles = (count // 2, 2)
    (
        block_output, contract_grad, expand_grad, output_grad, attended_grad, middle_grad_rows,
        vectors,
    ) = feed_forward(
        attended_low, flat_input, cotangent.reshape(total_rows, model_width), output_weight,
        output_bias, gain_two, bias_two, expand_weight, expand_bias, contract_weight,
        contract_bias,
    )
    contract_grad = contract_grad.reshape(
        tiles + (expand_weight.shape[1] // model_width, share, model_width)
    )
    expand_grad = expand_grad.reshape(tiles + (share, -1))
    output_grad = output_grad.reshape(tiles + (share, model_width))
    (
        totals, input_grad, query_map_grad, key_map_grad, sums, project_bias_grad,
        expand_bias_grad,
    ) = backward_attention(
        projected.reshape(3, head_count, head_width, total_rows), feat_query, feat_key, state_in,
        attended, denominator, attended_grad.reshape(head_count, head_width, total_rows),
        query_map, key_map, normed_rows, project_weight, input_rows, middle_grad_rows, gain_one,
        vectors, bounds, contract_grad, expand_grad, output_grad, count, lines,
    )
    depth = contract_grad.shape[2]
    wide = expand_weight.shape[1] // model_width
    order, _ = unit_order(depth + wide + 1, 3, head_count // 3 // BEAT, count // 2)
    at = [order.index(i) for i in range(len(order))]
    contract_total = jnp.concatenate([totals[i] for i in at[:depth]])
    expand_total = jnp.concatenate([totals[i] for i in at[depth : depth + wide]], axis=1)
    output_total = totals[at[depth + wide]]
    late = [totals[i].reshape(share, 3, -1) for i in at[depth + wide + 1 :]]
    project_total = jnp.stack(late, axis=2).reshape(share, -1)
    return (
        block_output.reshape(inputs.shape), input_grad.reshape(inputs.shape), sums[0], sums[1],
        project_total, project_bias_grad, query_map_grad, key_map_grad, output_total, sums[4],
        sums[2], sums[3], expand_total, expand_bias_grad,
        contract_total, sums[5],
    )


def solution(mesh):
    rows = P("batch", "seq", None)
    placed = (rows,) + (P(),) * 14 + (P("batch", None), rows)
    shard = P("seq", None)
    return jax.shard_map(
        per_device,
        mesh=mesh,
        in_specs=placed,
        out_specs=(
            rows, rows, P(), P(), shard, P(), P(), P(), shard, P(), P(), P(), shard, P(), shard, P(),
        ),
        check_vma=False,
    )
```

time: 815 us -> 298 us (0.37)
  waiting for transfers between devices: 452 us -> 0 us
  Pallas kernels: 185 us -> 282 us
  matrix products: 69.1 us -> 0 us
  blocking collectives: 41.8 us -> 0 us
  other arithmetic: 28.5 us -> 2.48 us
  between operations: 15.7 us -> 0.71 us
  local copies, waits for them, and re-layouts: 21 us -> 11.1 us
    reduce_scatter x4 -> x0, waiting for transfers between devices: 434 us -> none  [scatter(): return lax.psum_scatter(value, 'seq', scatter_dimension=0, tiled=True)]
    pallas_call x6 -> x3, Pallas kernels: 185 us -> 282 us  [the longest x1 204 us: backward_attention(): pl.pallas_call(partial(backward_kernel, count, lines, micro_count, early)...]
    dot_general x12 -> x0, matrix products: 69.1 us -> none  [the longest x1 10.5 us: per_device(): jnp.einsum('rf,rd->fd', hidden_low, grad_contract, preferred_element_type...]
    psum x1 -> x0, blocking collectives: 41.8 us -> none  [per_device(): lax.psum((gain_one_grad, bias_one_grad, project_bias_grad, query_map_grad...]
    psum x2 -> x0, waiting for transfers between devices: 16.6 us -> none  [the longest x1 16.6 us: per_device(): totals = lax.psum(shares, 'batch')]
    convert_element_type x16 -> x0, other arithmetic: 14 us -> none  [the longest x1 3.8 us: per_device(): (middle_grad + input_norm_grad).astype(bfloat)]
  transfers between devices with their start and end apart: 6 -> 0, of which waited for: 4 -> 0; matrix products, arithmetic and copies ran while one was open for 7% -> 0% of each run, Pallas kernels for 15% -> 0%
where the time goes in v4:
time: 298 us; the launch traced here: 296 us
  Pallas kernels  282 us (95%)
  local copies, waits for them, and re-layouts  11.1 us (4%)
    pallas_call x1, Pallas kernels, backward_attention(): pl.pallas_call(partial(backward_kernel, count, lines, micro_count, early)...  204 us
    pallas_call x1, Pallas kernels, forward_attention(): pl.pallas_call(partial(forward_kernel, count, micro_count), out_shape=[sh...  51.1 us
    pallas_call x1, Pallas kernels, feed_forward(): pl.pallas_call(feed_kernel, grid=(steps,), out_shape=[shape((total_rows,...  27 us

profile of v4, /device:TPU:0, one launch (start us, length us, event | category | flops | bytes accessed | tf_op | source)
XLA Modules:
  0.0 296.4 jit_solution(12080989879228313263)
XLA Ops:
  0.6 51.1 %shard_map.288 = (bf16[36,64,512]{2,1,0:T(8,128)(2,1)}, bf16[12,128,512]{2,1,0:T(8,128)(2,1)}, bf16[12,128,512]{2,1,0:T(8,128)(2,1)}, f32[12,264,128]{2,1,0:T(8,...) custom-call(bf16[512,768]{1,0:T(8,128)(2,1)} %bitcast.31, ...), custom_call_target="tpu_custom_call" | custom-call | tf_op jit(solution)/shard_map/pallas_call | solution.py:336
  51.7 27.0 %shard_map.289 = (bf16[512,768]{1,0:T(8,128)(2,1)}, f32[3072,768]{1,0:T(8,128)}, f32[768,3072]{1,0:T(8,128)}, f32[768,768]{1,0:T(8,128)}, f32[768,512]{1,0:T(8,1...) custom-call(bf16[768,512]{1,0:T(8,128)(2,1)} %bitcast.37, bf16[512,768]{1,0:T(8,128)(2,1)} %bitcast.32, ...), custom_call_target="tpu_custom_call" | custom-call | tf_op jit(solution)/shard_map/pallas_call | solution.py:1175
  78.7 203.9 %shard_map.290 = (f32[12,96,768]{2,1,0:T(8,128)}, bf16[512,768]{1,0:T(8,128)(2,1)}, f32[12,64,64]{2,1,0:T(8,128)}, f32[12,64,64]{2,1,0:T(8,128)}, f32[8,768]{1,0:T(8,128)}, /*index=5*/f32[2304]{0:T(1024)}, f32[3072]{0:T(1024)}) custom-call(bf16[3,12,64,512]{3,2,1,0:T(8,128)(2,1)} %bitcast.33, bf16[12,128,512]{2,1,0:T(8,128)(2,1)} %get-tuple-element.42.fq_hbm, ...), custom_call_target="tpu_custom_call" | custom-call | tf_op jit(solution)/shard_map/pallas_call | solution.py:1042
  282.7 1.7 slice_reduce_fusion
  284.4 2.9 slice_bitcast_fusion.3
  287.3 1.1 pad_maximum_fusion.2
  288.4 0.2 stack_reshape_squeeze.11
  288.6 0.2 stack_reshape_squeeze.10
  288.8 0.2 stack_reshape_squeeze.9
  288.9 0.3 pad_maximum_fusion
  289.2 0.6 copy.34
  289.8 1.5 reshape.75
  291.3 0.0 copy-start
  291.3 1.1 pad_maximum_fusion.1
  292.5 0.3 copy-done
  292.8 0.0 copy-start.4
  292.8 0.0 copy-start.2
  292.8 0.0 copy-start.1
  292.8 0.9 copy.40
  293.6 0.0 copy-done.4
  293.6 0.0 copy-start.3
  293.6 0.6 copy.41
  294.3 0.0 copy-done.2
  294.3 0.7 copy.42
  295.0 0.0 copy-done.1
  295.0 0.7 copy.43
  295.7 0.0 copy-done.3
  295.8 0.6 copy.44
Async XLA Ops:
  291.3 1.4 copy-start
  292.8 0.9 copy-start.4
  292.8 1.5 copy-start.2
  292.8 2.2 copy-start.1
  293.6 2.1 copy-start.3

commit v5 on v4

--- a/solution.py
+++ b/solution.py
@@ -139,6 +139,7 @@
 
 
 CHAIN_RING = 4
+LATER = 2
 
 
 class Chain:
@@ -239,9 +240,10 @@
 
 
 def forward_kernel(
-    count, micro_count, x_ref, gain_ref, shift_ref, weight_ref, bias_ref, qm_ref, km_ref,
-    bounds_ref, proj_ref, fq_ref, fk_ref, state_ref, att_ref, low_ref, den_ref, norm_ref, turned_ref,
-    normed, bias_row, mask, use, last, chain_mask, local, carry, onward, aside, beside, *sems,
+    count, micro_count, x_ref, gain_ref, shift_ref, weight_hbm, bias_ref, qm_ref, km_ref,
+    bounds_ref, proj_out, fq_out, fk_out, state_out, att_out, low_out, den_out, norm_out,
+    turned_out, weight_ref, proj_ref, fq_ref, fk_ref, state_ref, att_ref, low_ref, den_ref,
+    norm_ref, turned_ref, out_sem, whole_sem, normed, bias_row, mask, use, last, chain_mask, local, carry, onward, aside, beside, *sems,
 ):
     heads, head_width = qm_ref.shape[:2]
     total_rows = x_ref.shape[0]
@@ -251,6 +253,25 @@
     place = lax.axis_index("seq")
     first_row = place * rows
     chain = Chain(False, count, carry, onward, aside, beside, chain_mask, sems)
+    weight_copy = pltpu.make_async_copy(weight_hbm, weight_ref, whole_sem.at[0])
+    weight_copy.start()
+    turned_copies = [
+        pltpu.make_async_copy(norm_ref, norm_out, whole_sem.at[1]),
+        pltpu.make_async_copy(turned_ref, turned_out, whole_sem.at[2]),
+    ]
+
+    def outward(h):
+        pairs = [(proj_ref.at[p * heads + h], proj_out.at[p * heads + h]) for p in range(3)]
+        for source, target in (
+            (fq_ref, fq_out), (fk_ref, fk_out), (state_ref, state_out), (att_ref, att_out),
+            (low_ref, low_out), (den_ref, den_out),
+        ):
+            pairs.append((source.at[h], target.at[h]))
+        return [
+            pltpu.make_async_copy(source, target, out_sem.at[h, i])
+            for i, (source, target) in enumerate(pairs)
+        ]
+
     barrier = pltpu.get_barrier_semaphore()
     greeted = chain.greet(barrier)
     token_masks(bounds_ref, first_row, rows, micro_count, mask, use, last)
@@ -265,6 +286,9 @@
     pl.semaphore_wait(barrier, greeted)
     norm_ref[...] = normed[...].T
     turned_ref[...] = x_ref[...].T
+    for copy in turned_copies:
+        copy.start()
+    weight_copy.wait()
 
     def project(p):
         for part in range(3):
@@ -315,11 +339,27 @@
         @pl.when(r >= chain.lap + 1)
         def _():
             attend(r - chain.lap - 1)
+            for copy in outward(r - chain.lap - 1):
+                copy.start()
+
+        @pl.when(r >= chain.lap + 1 + LATER)
+        def _():
+            for copy in outward(r - chain.lap - 1 - LATER):
+                copy.wait()
 
         return 0
 
     lax.fori_loop(0, heads + chain.lap + 1, one_round, 0)
     chain.drain(heads)
+
+    def arrived(h, _):
+        for copy in outward(h):
+            copy.wait()
+        return 0
+
+    lax.fori_loop(heads - LATER, heads, arrived, 0)
+    for copy in turned_copies:
+        copy.wait()
 
 
 def forward_attention(x, gain, shift, weight, bias, query_map, key_map, bounds, count):
@@ -333,17 +373,27 @@
     head = (heads, head_width, total_rows)
     feat = (heads, 2 * head_width, total_rows)
     shape = jax.ShapeDtypeStruct
+    results = [
+        shape((3 * heads,) + head[1:], bfloat), shape(feat, bfloat), shape(feat, bfloat),
+        shape(chunk, single), shape(head, single), shape(head, bfloat),
+        shape((heads, 1, total_rows), single), shape((model_width, total_rows), bfloat),
+        shape((model_width, total_rows), bfloat),
+    ]
+    anywhere = pl.BlockSpec(memory_space=pl.ANY)
+    DMA = pltpu.SemaphoreType.DMA
     return pl.pallas_call(
         partial(forward_kernel, count, micro_count),
-        out_shape=[
-            shape((3 * heads,) + head[1:], bfloat), shape(feat, bfloat), shape(feat, bfloat),
-            shape(chunk, single), shape(head, single), shape(head, bfloat),
-            shape((heads, 1, total_rows), single), shape((model_width, total_rows), bfloat),
-            shape((model_width, total_rows), bfloat),
-        ],
-        in_specs=[whole] * 7 + [pl.BlockSpec(memory_space=pltpu.SMEM)],
-        out_specs=[whole] * 9,
-        scratch_shapes=[
+        out_shape=results,
+        in_specs=[whole] * 3
+        + [anywhere]
+        + [whole] * 3
+        + [pl.BlockSpec(memory_space=pltpu.SMEM)],
+        out_specs=[anywhere] * 9,
+        scratch_shapes=[pltpu.VMEM(weight.shape, bfloat)]
+        + [pltpu.VMEM(result.shape, result.dtype) for result in results]
+        + [
+            DMA((heads, 9)),
+            DMA((3,)),
             pltpu.VMEM((total_rows, model_width), bfloat),
             pltpu.VMEM((1, 3 * model_width), single),
             pltpu.VMEM((micro_count, rows, rows), single),
@@ -354,7 +404,7 @@
         + [pltpu.VMEM(chunk, single)] * 2
         + [pltpu.VMEM((CHAIN_RING,) + chunk[1:], single)] * 2
         + [pltpu.VMEM(chunk, single)]
-        + [pltpu.SemaphoreType.DMA((heads,))] * 4,
+        + [DMA((heads,))] * 4,
         compiler_params=pltpu.CompilerParams(
             collective_id=1, has_side_effects=True, vmem_limit_bytes=VMEM_LIMIT
         ),
@@ -370,7 +420,7 @@
     )
 
 
-FIRST, FIRST_ROWS, SECOND_ROWS = (8, 32, 32)
+PIECES, PIECE_ROWS = (2, (1, 2))
 
 
 class Spot:
@@ -397,8 +447,6 @@
         devices = [self.at_core]
         devices += [self.line(d)[1] for d in range(1, self.lines)]
         devices += [self.along(d)[1] for d in range(1, 2 * self.length)]
-        other = self.at_core[1]
-        devices += [(self.along(d)[0], other) for d in range(1, 2 * self.length)]
         for device in devices:
             pl.semaphore_signal(barrier, inc=1, device_id=device, device_id_type=MESH)
         return len(devices)
@@ -406,9 +454,10 @@
 
 class Track:
     def __init__(
-        self, spot, base, halved, rows, offset, ring, out, own, got, y_got, z_got, x_got, sems
+        self, spot, base, halved, rows, offset, stride, ring, out, own, got, y_got, z_got, x_got,
+        sems,
     ):
-        self.base = base
+        self.base, self.stride = (base, stride)
         self.spot, self.halved, self.rows, self.offset, self.ring = spot, halved, rows, offset, ring
         self.out, self.own, self.got, self.y_got, self.z_got, self.x_got = (
             out, own, got, y_got, z_got, x_got,
@@ -424,13 +473,19 @@
         self.part = rows // spot.lines if halved else rows
         self.strip = self.window(spot.across) if halved else slice(None)
 
+    def row(self, u):
+        return pl.multiple_of(self.offset + u * self.stride, 8) if self.stride else self.offset
+
+    def seat(self, u):
+        return self.base if self.stride else self.base + u
+
     def window(self, line, base=0):
         return pl.ds(pl.multiple_of(base + line * self.part, 8), self.part)
 
-    def source(self, ref, col, columns):
+    def source(self, u, ref, col, columns):
         half = self.own.shape[-1]
         cols = pl.ds(pl.multiple_of(col + columns * half, 128), half)
-        return ref.at[:, :, pl.ds(self.offset, self.rows), cols]
+        return ref.at[:, :, pl.ds(self.row(u), self.rows), cols]
 
     def give(self, u, source):
         return remote(
@@ -439,9 +494,9 @@
         )
 
     def begin(self, u, ref, col):
-        self.give(u, self.source(ref, col, 1 - self.spot.core)).start()
+        self.give(u, self.source(u, ref, col, 1 - self.spot.core)).start()
         pltpu.make_async_copy(
-            self.source(ref, col, self.spot.core), self.own.at[u], self.load_sem.at[u]
+            self.source(u, ref, col, self.spot.core), self.own.at[u], self.load_sem.at[u]
         ).start()
 
     def settle(self, u):
@@ -553,20 +608,20 @@
         )
 
     def x_back(self, u, d):
-        rows = self.window(self.spot.across, self.offset)
+        rows = self.window(self.spot.across, self.row(u))
         return remote(
-            self.block(u, self.spot.high), self.out.at[self.base + u, rows, self.mine],
+            self.block(u, self.spot.high), self.out.at[self.seat(u), rows, self.mine],
             self.x_send.at[u, 1, d - 1], self.x_recv.at[u, 1, d - 1], self.spot.line(d)[1],
         )
 
     def keep(self, u):
         rows = (
-            self.window(self.spot.across, self.offset)
+            self.window(self.spot.across, self.row(u))
             if self.halved
-            else pl.ds(self.offset, self.rows)
+            else pl.ds(self.row(u), self.rows)
         )
         return pltpu.make_async_copy(
-            self.block(u, self.spot.high), self.out.at[self.base + u, rows, self.mine], self.load_sem.at[u]
+            self.block(u, self.spot.high), self.out.at[self.seat(u), rows, self.mine], self.load_sem.at[u]
         )
 
     def reduced(self, u):
@@ -577,7 +632,7 @@
             (self.x_back if self.halved else self.x_copy)(u, d).start()
 
     def back(self, u):
-        block = self.out.at[self.base + u, pl.ds(self.offset, self.rows), self.mine]
+        block = self.out.at[self.seat(u), pl.ds(self.row(u), self.rows), self.mine]
         source = block if self.halved else self.block(u, self.spot.high)
         return remote(source, block, self.back_send.at[u], self.back_recv.at[u], self.spot.at_core)
 
@@ -637,13 +692,16 @@
 
 
 def bands(units, share, lines):
-    groups = []
-    for low, high, direct in ((0, FIRST, FIRST_ROWS), (FIRST, units, SECOND_ROWS)):
-        direct = direct * share // 96
-        if direct % 8 or (share - direct) % (8 * lines):
-            return [(0, units, share, 0)]
-        groups.append((low, high, direct, share - direct))
-    return groups
+    third, rows = (share // 3, share // PIECES)
+    fits = [third % 8, 2 * third % (8 * lines), share % 3, share % PIECES]
+    direct = rows * PIECE_ROWS[0] // sum(PIECE_ROWS)
+    fits += [direct % 8, (rows - direct) % (8 * lines)]
+    if any(fits):
+        return [(0, units, share, 0, 0)]
+    return [
+        (0, units - 1, third, 2 * third, 0),
+        (units - 1, units - 1 + PIECES, direct, rows - direct, rows),
+    ]
 
 
 def track_scratch(units, length, lines, rows, halved, ring, half):
@@ -680,9 +738,9 @@
 
 def backward_kernel(
     count, lines, micro_count, early, proj_hbm, fq_hbm, fk_hbm, state_hbm, att_hbm, den_hbm,
-    grad_hbm, qm_ref, km_ref, norm_ref, weight_ref, x_ref, mid_ref, gain_ref, vector_ref,
+    grad_hbm, qm_ref, km_ref, norm_hbm, weight_hbm, x_hbm, mid_hbm, gain_ref, vector_ref,
     bounds_ref, contract_ref, expand_ref, output_ref, out, in_grad_ref, qm_out, km_out, rows_out, bias_out, expand_bias_out,
-    proj, fq_buf, fk_buf, state_buf, att_buf, den_buf, grad_buf, load_sem, pg_ref,
+    norm_ref, weight_ref, x_ref, mid_ref, whole_sem, proj, fq_buf, fk_buf, state_buf, att_buf, den_buf, grad_buf, load_sem, pg_ref,
     mask, use, last, chain_mask, local, carry, onward, aside, beside, fqg, fkg, product, small,
     small_sum, small_out, gather_send, gather_recv, gather_keep, credit, *rest,
 ):
@@ -698,18 +756,22 @@
     spot = Spot(count, lines)
     length = spot.length
     order, starts = unit_order(len(early), late, group // BEAT, length)
+    plan = bands(units, share, lines)
+    order = order + order[-1:] * (plan[-1][1] - units)
+    starts = starts + [starts[-1] + 1 + i for i in range(plan[-1][1] - units)]
+    units = len(order)
     chain_sems, rest = (rest[:4], rest[4:])
     chain = Chain(True, count, carry, onward, aside, beside, chain_mask, chain_sems)
     ring, half = (2, wide // 2)
-    little = Track(spot, 0, False, small.shape[2], 0, 1, small_sum, *rest[:5], rest[5:18])
+    little = Track(spot, 0, False, small.shape[2], 0, 0, 1, small_sum, *rest[:5], rest[5:18])
     rest = rest[18:]
     groups = []
-    for low, high, direct, halved in bands(units, share, lines):
+    for low, high, direct, halved, stride in plan:
         group_tracks = []
         for kind, band, offset in ((False, direct, 0), (True, halved, direct)):
             if band:
                 group_tracks.append(
-                    Track(spot, low, kind, band, offset, ring, out, *rest[:5], rest[5:18])
+                    Track(spot, low, kind, band, offset, stride, ring, out, *rest[:5], rest[5:18])
                 )
                 rest = rest[18:]
         groups.append((low, high, group_tracks))
@@ -731,6 +793,14 @@
     for h in range(BEAT):
         for copy in loads(h):
             copy.start()
+    whole_copies = [
+        pltpu.make_async_copy(source, target, whole_sem.at[i])
+        for i, (source, target) in enumerate(
+            ((norm_hbm, norm_ref), (weight_hbm, weight_ref), (x_hbm, x_ref), (mid_hbm, mid_ref))
+        )
+    ]
+    for copy in whole_copies:
+        copy.start()
     barrier = pltpu.get_barrier_semaphore()
     greeted = spot.greet(barrier)
     pl.semaphore_wait(barrier, greeted)
@@ -856,19 +926,17 @@
         small[...] = jnp.concatenate(maps + [vectors] + pad, axis=0).reshape(small.shape)
         little.begin(0, small, 0)
 
-    others = [(d, 0) for d in range(1, count)] + [(d, 1) for d in range(count)]
-
-    def spread(k, incoming):
-        d, other_core = others[k]
-        here, there = (spot.place, lax.rem(spot.place + d, count))
-        core = lax.rem(spot.core + other_core, 2)
-        device = (there, 2 * spot.across + core)
-        side = pl.ds(pl.multiple_of((core if incoming else spot.core) * half, 128), half)
-        place, its_core = (there, core) if incoming else (here, spot.core)
+    def spread(d, incoming):
+        there, device = spot.along(d)
+        place = there if incoming else spot.place
         return remote(
-            little.block(0, spot.high), small_out.at[place, :, side], gather_send.at[k],
-            gather_recv.at[place, its_core], device,
-        )
+            little.block(0, spot.high), small_out.at[place, :, little.mine],
+            gather_send.at[d - 1], gather_recv.at[place], device,
+        )
+
+    def spread_core():
+        block = small_out.at[:, :, little.mine]
+        return remote(block, block, gather_keep.at[1], gather_keep.at[2], spot.at_core)
 
     def spread_keep():
         return pltpu.make_async_copy(
@@ -879,15 +947,35 @@
     def little_done(u):
         little.total(u)
         spread_keep().start()
-        for k in range(len(others)):
-            spread(k, False).start()
-
-    little_steps = little.steps()[:-1] + [little_done]
+        for d in range(1, count):
+            spread(d, False).start()
+
+    def little_gather(u):
+        spread_keep().wait()
+        for d in range(1, count):
+            spread(d, True).wait_recv()
+        spread_core().start()
+
+    little_steps = little.steps()[:-1] + [little_done, little_gather]
+    lent = [order.index(len(early) + g) for g in range(late - 1)]
+
+    def settle_all(track, v):
+        track.finish(v)
+        track.drain(v)
+        u = v + track.base
+        waited = False
+        for k in lent:
+            waited = waited | (u == k)
+
+        @pl.when(jnp.logical_not(waited))
+        def _():
+            track.given(v)
+
     stages = [
         (s, f, low, high)
         for low, high, tracks in groups
         for track in tracks
-        for s, f in enumerate(track.steps())
+        for s, f in enumerate(track.steps() + [partial(settle_all, track)])
     ]
     stages.sort(key=lambda s: (s[0], s[2]))
     ahead = 1
@@ -911,6 +999,9 @@
 
     beats = heads // BEAT
 
+    for copy in whole_copies:
+        copy.wait()
+
     def one_round(r, _):
         c = r - chain.lap
 
@@ -972,16 +1063,12 @@
     rounds = max(starts[-1] + stages[-1][0] + 1, beats + length + 1 + len(little_steps))
     lax.fori_loop(0, rounds, one_round, 0)
 
-    for u in range(units):
-        for track in tracks_of(u):
-            track.finish(u - track.base)
     chain.drain(heads)
     little.drain(0)
     little.given(0)
-    spread_keep().wait()
-    for k in range(len(others)):
-        spread(k, False).wait_send()
-        spread(k, True).wait_recv()
+    for d in range(1, count):
+        spread(d, False).wait_send()
+    spread_core().wait()
 
     sums = small_out[...].reshape(-1, model_width)
     for h in range(heads):
@@ -995,18 +1082,6 @@
         for start in range(0, target.shape[0], model_width):
             target[start : start + model_width] = sums[row]
             row += 1
-
-    for low, high, tracks in groups:
-        def drain(v, _, tracks=tracks):
-            for track in tracks:
-                track.drain(v)
-            return 0
-
-        lax.fori_loop(0, high - low, drain, 0)
-    for u in range(units):
-        if order[u] < len(early) or order[u] == units - 1:
-            for track in tracks_of(u):
-                track.given(u - track.base)
 
 
 def backward_attention(
@@ -1033,7 +1108,7 @@
     used = 2 * head_width + vectors.shape[0]
     little = -(-used // (8 * count)) * 8
     tracks = track_scratch(1, length, lines, little, False, 1, half)
-    for low, high, direct, halved in bands(units, share, lines):
+    for low, high, direct, halved, _ in bands(units, share, lines):
         for kind, band in ((False, direct), (True, halved)):
             if band:
                 tracks += track_scratch(high - low, length, lines, band, kind, 2, half)
@@ -1048,11 +1123,18 @@
         + [shape((8, model_width), single)]
         + [shape((3 * model_width,), single), shape((expand_grad.shape[3],), single)],
         in_specs=[anywhere] * 7
-        + [whole] * 8
+        + [whole] * 2
+        + [anywhere] * 4
+        + [whole] * 2
         + [pl.BlockSpec(memory_space=pltpu.SMEM)]
         + [anywhere] * 3,
         out_specs=[anywhere] + [whole] * 6,
         scratch_shapes=[
+            pltpu.VMEM(normed_rows.shape, bfloat),
+            pltpu.VMEM(weight.shape, bfloat),
+            pltpu.VMEM(input_rows.shape, bfloat),
+            pltpu.VMEM(middle_grad_rows.shape, single),
+            DMA((4,)),
             pltpu.VMEM((slots, 3) + head[1:], bfloat),
             pltpu.VMEM(feat, bfloat),
             pltpu.VMEM(feat, bfloat),
@@ -1077,9 +1159,9 @@
             pltpu.VMEM((length, 2, little, model_width), single),
             pltpu.VMEM((1, little, model_width), single),
             pltpu.VMEM((count, little, model_width), single),
-            DMA((2 * count - 1,)),
-            DMA((count, 2)),
-            DMA((1,)),
+            DMA((count - 1,)),
+            DMA((count,)),
+            DMA((3,)),
             pltpu.SemaphoreType.REGULAR,
         ]
         + [DMA((heads,))] * 4

time: 298 us -> 285 us (0.956)
  Pallas kernels: 282 us -> 269 us
    pallas_call x1, Pallas kernels: 204 us -> 194 us  [backward_attention(): pl.pallas_call(partial(backward_kernel, count, lines, micro_count, early)...]
where the time goes in v5:
time: 285 us; the launch traced here: 284 us
  Pallas kernels  269 us (94%)
  local copies, waits for them, and re-layouts  11.1 us (4%)
    pallas_call x1, Pallas kernels, backward_attention(): pl.pallas_call(partial(backward_kernel, count, lines, micro_count, early)...  194 us
    pallas_call x1, Pallas kernels, forward_attention(): pl.pallas_call(partial(forward_kernel, count, micro_count), out_shape=res...  48.4 us
    pallas_call x1, Pallas kernels, feed_forward(): pl.pallas_call(feed_kernel, grid=(steps,), out_shape=[shape((total_rows,...  27 us

profile of v5, /device:TPU:0, one launch (start us, length us, event | category | flops | bytes accessed | tf_op | source)
XLA Modules:
  0.0 283.7 jit_solution(13031480432026606341)
XLA Ops:
  0.6 48.4 %shard_map.288 = (bf16[36,64,512]{2,1,0:T(8,128)(2,1)}, bf16[12,128,512]{2,1,0:T(8,128)(2,1)}, bf16[12,128,512]{2,1,0:T(8,128)(2,1)}, f32[12,264,128]{2,1,0:T(8,...) custom-call(bf16[512,768]{1,0:T(8,128)(2,1)} %bitcast.31, ...), custom_call_target="tpu_custom_call" | custom-call | tf_op jit(solution)/shard_map/pallas_call | solution.py:384
  49.0 27.0 %shard_map.289 = (bf16[512,768]{1,0:T(8,128)(2,1)}, f32[3072,768]{1,0:T(8,128)}, f32[768,3072]{1,0:T(8,128)}, f32[768,768]{1,0:T(8,128)}, f32[768,512]{1,0:T(8,1...) custom-call(bf16[768,512]{1,0:T(8,128)(2,1)} %bitcast.37, bf16[512,768]{1,0:T(8,128)(2,1)} %bitcast.32, ...), custom_call_target="tpu_custom_call" | custom-call | tf_op jit(solution)/shard_map/pallas_call | solution.py:1257
  76.0 194.0 %shard_map.290 = (f32[12,96,768]{2,1,0:T(8,128)}, bf16[512,768]{1,0:T(8,128)(2,1)}, f32[12,64,64]{2,1,0:T(8,128)}, f32[12,64,64]{2,1,0:T(8,128)}, f32[8,768]{1,0:T(8,128)}, /*index=5*/f32[2304]{0:T(1024)}, f32[3072]{0:T(1024)}) custom-call(bf16[3,12,64,512]{3,2,1,0:T(8,128)(2,1)} %bitcast.33, bf16[12,128,512]{2,1,0:T(8,128)(2,1)} %get-tuple-element.42.fq_hbm, ...), custom_call_target="tpu_custom_call" | custom-call | tf_op jit(solution)/shard_map/pallas_call | solution.py:1117
  270.1 1.7 slice_reduce_fusion
  271.8 2.9 %slice_bitcast_fusion.3 = (f32[96,768]{1,0:T(8,128)S(1)}, f32[96,768]{1,0:T(8,128)S(1)}, f32[96,768]{1,0:T(8,128)S(1)}, f32[96,768]{1,0:T(8,128)S(1)}, f32[96,76...) fusion(f32[12,96,768]{2,1,0:T(8,128)} %get-tuple-element.57), kind=kLoop, calls=%fused_computation.6 | loop fusion | bytes 7077888 | tf_op jit(solution)/shard_map/squeeze | solution.py:1335
  274.7 1.1 pad_maximum_fusion.2
  275.8 0.2 stack_reshape_squeeze.11
  276.0 0.2 stack_reshape_squeeze.10
  276.1 0.2 stack_reshape_squeeze.9
  276.3 0.3 pad_maximum_fusion
  276.6 0.6 copy.34
  277.2 1.5 reshape.75
  278.7 0.0 copy-start
  278.7 1.1 pad_maximum_fusion.1
  279.8 0.3 copy-done
  280.1 0.0 copy-start.4
  280.1 0.0 copy-start.2
  280.2 0.0 copy-start.1
  280.2 0.9 copy.40
  281.0 0.0 copy-done.4
  281.0 0.0 copy-start.3
  281.0 0.6 copy.41
  281.6 0.0 copy-done.2
  281.6 0.7 copy.42
  282.4 0.0 copy-done.1
  282.4 0.7 copy.43
  283.1 0.0 copy-done.3
  283.1 0.6 copy.44
Async XLA Ops:
  278.7 1.4 copy-start
  280.1 0.9 copy-start.4
  280.1 1.5 copy-start.2
  280.2 2.2 copy-start.1
  281.0 2.1 copy-start.3

commit v6 on v5

--- a/solution.py
+++ b/solution.py
@@ -324,6 +324,10 @@
             den_ref[h, :, part] = denom
 
     def one_round(r, _):
+        @pl.when((r >= chain.lap) & (r < heads + chain.lap) & jnp.logical_not(chain.first))
+        def _():
+            chain.step(r - chain.lap, local[r - chain.lap])
+
         @pl.when((r < heads) & (lax.rem(r, 2) == 0))
         def _():
             project(r // 2)
@@ -332,7 +336,7 @@
         def _():
             features(r)
 
-        @pl.when((r >= chain.lap) & (r < heads + chain.lap))
+        @pl.when((r >= chain.lap) & (r < heads + chain.lap) & chain.first)
         def _():
             chain.step(r - chain.lap, local[r - chain.lap])
 

time: 285 us -> 282 us (0.989)
  no operation moved by 1% of the time
where the time goes in v6:
time: 282 us; the launch traced here: 281 us
  Pallas kernels  267 us (95%)
  local copies, waits for them, and re-layouts  11.1 us (4%)
    pallas_call x1, Pallas kernels, backward_attention(): pl.pallas_call(partial(backward_kernel, count, lines, micro_count, early)...  191 us
    pallas_call x1, Pallas kernels, forward_attention(): pl.pallas_call(partial(forward_kernel, count, micro_count), out_shape=res...  48.4 us
    pallas_call x1, Pallas kernels, feed_forward(): pl.pallas_call(feed_kernel, grid=(steps,), out_shape=[shape((total_rows,...  27 us

profile of v6, /device:TPU:0, one launch (start us, length us, event | category | flops | bytes accessed | tf_op | source)
XLA Modules:
  0.0 281.2 jit_solution(7012356530587176947)
XLA Ops:
  0.6 48.4 %shard_map.288 = (bf16[36,64,512]{2,1,0:T(8,128)(2,1)}, bf16[12,128,512]{2,1,0:T(8,128)(2,1)}, bf16[12,128,512]{2,1,0:T(8,128)(2,1)}, f32[12,264,128]{2,1,0:T(8,...) custom-call(bf16[512,768]{1,0:T(8,128)(2,1)} %bitcast.31, ...), custom_call_target="tpu_custom_call" | custom-call | tf_op jit(solution)/shard_map/pallas_call | solution.py:388
  49.0 27.0 %shard_map.289 = (bf16[512,768]{1,0:T(8,128)(2,1)}, f32[3072,768]{1,0:T(8,128)}, f32[768,3072]{1,0:T(8,128)}, f32[768,768]{1,0:T(8,128)}, f32[768,512]{1,0:T(8,1...) custom-call(bf16[768,512]{1,0:T(8,128)(2,1)} %bitcast.37, bf16[512,768]{1,0:T(8,128)(2,1)} %bitcast.32, ...), custom_call_target="tpu_custom_call" | custom-call | tf_op jit(solution)/shard_map/pallas_call | solution.py:1261
  76.1 191.4 %shard_map.290 = (f32[12,96,768]{2,1,0:T(8,128)}, bf16[512,768]{1,0:T(8,128)(2,1)}, f32[12,64,64]{2,1,0:T(8,128)}, f32[12,64,64]{2,1,0:T(8,128)}, f32[8,768]{1,0:T(8,128)}, /*index=5*/f32[2304]{0:T(1024)}, f32[3072]{0:T(1024)}) custom-call(bf16[3,12,64,512]{3,2,1,0:T(8,128)(2,1)} %bitcast.33, bf16[12,128,512]{2,1,0:T(8,128)(2,1)} %get-tuple-element.42.fq_hbm, ...), custom_call_target="tpu_custom_call" | custom-call | tf_op jit(solution)/shard_map/pallas_call | solution.py:1121
  267.5 1.7 slice_reduce_fusion
  269.2 2.9 %slice_bitcast_fusion.3 = (f32[96,768]{1,0:T(8,128)S(1)}, f32[96,768]{1,0:T(8,128)S(1)}, f32[96,768]{1,0:T(8,128)S(1)}, f32[96,768]{1,0:T(8,128)S(1)}, f32[96,76...) fusion(f32[12,96,768]{2,1,0:T(8,128)} %get-tuple-element.57), kind=kLoop, calls=%fused_computation.6 | loop fusion | bytes 7077888 | tf_op jit(solution)/shard_map/squeeze | solution.py:1339
  272.2 1.1 pad_maximum_fusion.2
  273.2 0.2 stack_reshape_squeeze.11
  273.4 0.2 stack_reshape_squeeze.10
  273.6 0.2 stack_reshape_squeeze.9
  273.7 0.3 pad_maximum_fusion
  274.0 0.6 copy.34
  274.6 1.5 reshape.75
  276.2 0.0 copy-start
  276.2 1.1 pad_maximum_fusion.1
  277.3 0.3 copy-done
  277.6 0.0 copy-start.4
  277.6 0.0 copy-start.2
  277.6 0.0 copy-start.1
  277.6 0.9 copy.40
  278.5 0.0 copy-done.4
  278.5 0.0 copy-start.3
  278.5 0.6 copy.41
  279.1 0.0 copy-done.2
  279.1 0.7 copy.42
  279.8 0.0 copy-done.1
  279.8 0.7 copy.43
  280.6 0.0 copy-done.3
  280.6 0.6 copy.44
Async XLA Ops:
  276.2 1.4 copy-start
  277.6 0.9 copy-start.4
  277.6 1.5 copy-start.2
  277.6 2.2 copy-start.1
  278.5 2.1 copy-start.3
